TPU v7x, 128 devices: a whole 4x4x4 slice. The times are simulated.
128 devices in a mesh: seq: 16 (over z, y), col: 8 (over x, core).
Axes of the slice: x: 4, y: 4, z: 4, core: 2. Of those that a mesh axis runs over, the one named last changes fastest.
Arguments:
- item_table: bfloat16 [65536, 512], P('seq', 'col'), may hold values from -6 to 6
- hot_table: bfloat16 [256, 512], P(None, 'col'), may hold values from -6 to 6
- weight_in: bfloat16 [2, 512, 2048], replicated, may hold values from -0.25 to 0.25
- weight_out: bfloat16 [2, 512, 512], replicated, may hold values from -0.25 to 0.25
- row_owner: int32 [32768, 1], P('seq'), may hold values from 0 to 15; in each aligned block of 2048 rows (0 to 2047, 2048 to 4095, ...) at most 256 rows name the same one
- item_row: int32 [32768], P('seq'), may hold values from 0 to 4095
- hot_flag: int32 [32768], P('seq'), may hold values 0 or 1
- hot_row: int32 [32768], P('seq'), may hold values from 0 to 255
- segment: int32 [128, 256], P(('seq', 'col')), may hold values from 0 to 7, never falling along the last dimension, each value on 1 to 128 neighbouring positions
- cotangent: bfloat16 [32768, 512], P(('seq', 'col')), may hold values from -6 to 6
Outputs:
- encoded: bfloat16 [32768, 512], P(('seq', 'col'))
- table_grad: float32 [65536, 512], P('seq', 'col')
- hot_grad: float32 [256, 512], P(None, 'col')
- weight_in_grad: float32 [2, 512, 2048], replicated
- weight_out_grad: float32 [2, 512, 512], replicated
Inputs may be any that keep to these rules, and one draw needn't show every extreme that they name: `row_owner`: in each aligned block of 256 * 8 positions (the positions of one index of seq) no owner is named by more than 256 positions, a bound that some block reaches. `segment`: segment numbers never fall along a block; each history holds 1 to 128 positions.
All inputs are finite; a program needn't handle non-finite values. No bound on the sum of `hot_flag` on one device may be relied on, other than what follows from the above.
Results may differ from a plain program's by a relative error of at most 0.028.
Values may be sent and summed in bfloat16 or wider, within the bound.
No kernel may reach another device: no remote copies, remote signals or barrier semaphores. Data moves between devices by JAX's collectives and lax.ppermute only.
A program may use at most 128 MiB of HBM per device.

v0:
```python
import jax
import jax.numpy as jnp
from jax import lax
from jax.sharding import PartitionSpec as P

HEADS = 4
HEAD_DIM = 128
LAYERS = 2


def layer_norm(stream):
    center = stream - jnp.mean(stream, axis=-1, keepdims=True)
    variance = jnp.mean(center * center, axis=-1, keepdims=True)
    return center * lax.rsqrt(variance + 1e-05)


def causal_mask(segment_ids):
    position = jnp.arange(segment_ids.shape[0])
    return (segment_ids[:, None] == segment_ids[None, :]) & (position[None, :] <= position[:, None])


def hstu_layer(stream, proj_in, proj_out, allowed):
    count_rows, width = stream.shape
    normed = layer_norm(stream).astype(jnp.bfloat16)
    projected = jax.nn.silu(jnp.dot(normed, proj_in, preferred_element_type=jnp.float32)).astype(
        jnp.bfloat16
    )
    gates, values, queries, key_part = jnp.split(projected, 4, axis=1)
    queries = queries.reshape(count_rows, HEADS, HEAD_DIM)
    key_part = key_part.reshape(count_rows, HEADS, HEAD_DIM)
    values = values.reshape(count_rows, HEADS, HEAD_DIM)
    scores = jnp.einsum(
        "qhd,khd->hqk", queries, key_part, preferred_element_type=jnp.float32
    ) * HEAD_DIM ** (-0.5)
    attn = jnp.where(allowed[None], jax.nn.silu(scores), 0.0).astype(jnp.bfloat16)
    mixed = jnp.einsum("hqk,khd->qhd", attn, values, preferred_element_type=jnp.float32).reshape(
        count_rows, width
    )
    gated = (layer_norm(mixed) * gates.astype(jnp.float32)).astype(jnp.bfloat16)
    return stream + jnp.dot(gated, proj_out, preferred_element_type=jnp.float32)


def run_stack(embedded, weight_in, weight_out, allowed):
    stream = embedded.astype(jnp.float32)
    for layer_index in range(LAYERS):
        stream = hstu_layer(stream, weight_in[layer_index], weight_out[layer_index], allowed)
    return stream.astype(jnp.bfloat16)


def on_device(
    item_table,
    hot_table,
    weight_in,
    weight_out,
    row_owner,
    item_row,
    hot_flag,
    hot_row,
    segment,
    cotangent,
):
    seq_count = lax.axis_size("seq")
    seq_rows = row_owner.shape[0]
    capacity = 2 * seq_rows // seq_count
    hot_count = hot_table.shape[0]
    destination = row_owner[:, 0]
    regular = hot_flag == 0
    member = ((destination[:, None] == jnp.arange(seq_count)[None, :]) & regular[:, None]).astype(
        jnp.int32
    )
    slot_index = jnp.sum((jnp.cumsum(member, axis=0) - 1) * member, axis=1)
    target = jnp.where(regular, destination, seq_count)
    requests = (
        jnp.full((seq_count, capacity), -1, jnp.int32)
        .at[target, slot_index]
        .set(item_row, mode="drop")
    )
    received = lax.all_to_all(requests, "seq", split_axis=0, concat_axis=0, tiled=True)
    valid = received >= 0
    picked = jnp.take(item_table, jnp.clip(received, 0, item_table.shape[0] - 1), axis=0)
    picked = jnp.where(valid[..., None], picked, jnp.zeros_like(picked))
    returned = lax.all_to_all(picked, "seq", split_axis=0, concat_axis=0, tiled=True)
    cold_rows = returned[jnp.clip(target, 0, seq_count - 1), slot_index]
    hot_pick = (hot_row[:, None] == jnp.arange(hot_count)[None, :]).astype(jnp.bfloat16)
    hot_rows = jnp.dot(hot_pick, hot_table, preferred_element_type=jnp.float32).astype(jnp.bfloat16)
    column_rows = jnp.where(regular[:, None], cold_rows, hot_rows)
    embedded = lax.all_to_all(column_rows, "col", split_axis=0, concat_axis=1, tiled=True)
    allowed = causal_mask(segment[0])

    def stack_here(emb_here, first, second):
        return run_stack(emb_here, first, second, allowed)

    encoded, pullback = jax.vjp(stack_here, embedded, weight_in, weight_out)
    grad_emb, grad_first, grad_second = pullback(cotangent)
    grad_columns = lax.all_to_all(grad_emb, "col", split_axis=1, concat_axis=0, tiled=True)
    hot_only = hot_pick * hot_flag[:, None].astype(jnp.bfloat16)
    hot_part = jnp.dot(hot_only.T, grad_columns, preferred_element_type=jnp.float32)
    hot_grad = lax.psum(hot_part.astype(jnp.bfloat16), "seq").astype(jnp.float32)
    outgoing = jnp.zeros((seq_count, capacity, grad_columns.shape[1]), jnp.bfloat16)
    outgoing = outgoing.at[target, slot_index].set(grad_columns, mode="drop")
    incoming = lax.all_to_all(outgoing, "seq", split_axis=0, concat_axis=0, tiled=True)
    row_target = jnp.where(received >= 0, received, item_table.shape[0])
    table_grad = (
        jnp.zeros(item_table.shape, jnp.float32)
        .at[row_target]
        .add(incoming.astype(jnp.float32), mode="drop")
    )
    local_in = grad_first.astype(jnp.float32)
    local_out = grad_second.astype(jnp.float32)
    grad_in, grad_out = lax.psum((local_in, local_out), ("seq", "col"))
    return (encoded, table_grad, hot_grad, grad_in, grad_out)


def solution(mesh):
    in_specs = (
        P("seq", "col"),
        P(None, "col"),
        P(),
        P(),
        P("seq", None),
        P("seq"),
        P("seq"),
        P("seq"),
        P(("seq", "col"), None),
        P(("seq", "col"), None),
    )
    out_specs = (P(("seq", "col"), None), P("seq", "col"), P(None, "col"), P(), P())
    return jax.shard_map(
        on_device, mesh=mesh, in_specs=in_specs, out_specs=out_specs, check_vma=False
    )
```

profile of v0, /device:TPU:1, one launch (start us, length us, event | category | flops | bytes accessed | tf_op | source)
XLA Modules:
  0.0 329.7 jit_solution(1849301794980950927)
XLA Ops:
  9.4 4.5 %reduce-window.6 = s32[16,16,128]{2,1,0:T(8,128)S(1)} reduce-window(s32[16,16,128]{2,1,0:T(8,128)S(1)} %fusion.91, s32[]{:T(128)} %constant.63.clone.1), window={size=1x1x128 pad=0_0x0_0x127_0}, to_apply=%region_0.0 | reduce-window | flops 4161536 | bytes 262148 | tf_op jit(solution)/shard_map/reduce-window
  17.0 8.8 %scatter_custom_fusion.1 = s32[4096]{0:T(1024)} fusion(s32[2048]{0:T(1024)S(1)} %broadcast_select_fusion, s32[2048]{0:T(1024)} %param.15, s32[]{:T(128)} %constant.64.clone.1), kind=kCustom, calls=%fused_computation.182 | custom fusion | bytes 16896
  25.8 8.6 %all-to-all-start = ((s32[16,1,256]{2,1,0:T(1,128)}), s32[16,1,256]{2,1,0:T(1,128)S(1)}, u32[]{:S(2)}, u32[]{:S(2)}) async-start(s32[16,1,256]{2,1,0:T(1,128)} %bitcast.6), calls=%async_computation | async-start | bytes 32768 | tf_op jit(solution)/shard_map/all_to_all | solution.py:78
  34.4 1.5 copy.113
  35.9 4.9 %all-to-all-done = s32[16,1,256]{2,1,0:T(1,128)S(1)} async-done(((s32[16,1,256]{2,1,0:T(1,128)}), s32[16,1,256]{2,1,0:T(1,128)S(1)}, u32[]{:S(2)}, u32[]{:S(2)}) %all-to-all-start) | async-done | bytes 16416 | tf_op jit(solution)/shard_map/all_to_all | solution.py:78
  40.9 12.1 %gather_fusion = bf16[4096,64]{1,0:T(8,128)(2,1)S(1)} fusion(bf16[4096,64]{1,0:T(8,128)(2,1)S(1)} %copy.113, s32[4096]{0:T(1024)S(1)} %broadcast_clamp_fusion), kind=kCustom, calls=%fused_computation | custom fusion | bytes 1064960 | tf_op jit(solution)/shard_map/jit(_take)/gather | solution.py:80
  53.5 12.6 %all_to_all.54 = bf16[16,256,64]{1,2,0:T(8,128)(2,1)S(1)} all-to-all(bf16[16,256,64]{1,2,0:T(8,128)(2,1)S(1)} %select_select_fusion), channel_id=1, replica_groups=mesh['seq'=16,'col'=8] {'seq'}, dimensions={0} | all-to-all | bytes 1048576 | tf_op jit(solution)/shard_map/all_to_all | solution.py:82
  66.6 11.1 %gather_fusion.1 = bf16[2048,64]{1,0:T(8,128)(2,1)S(1)} fusion(bf16[16,256,64]{2,1,0:T(8,128)(2,1)S(1)} %copy.115, s32[2048]{0:T(1024)S(1)} %bitcast.218), kind=kCustom, calls=%fused_computation.1 | custom fusion | bytes 540672 | tf_op jit(solution)/shard_map/gather | solution.py:83
  79.2 7.3 %all-to-all-start.2 = ((bf16[8,256,64]{1,2,0:T(8,128)(2,1)}), bf16[8,256,64]{1,2,0:T(8,128)(2,1)S(1)}, u32[]{:S(2)}, u32[]{:S(2)}) async-start(bf16[8,256,64]{1,2,0:T(8,128)(2,1)} %bitcast.214), calls=%async_computation.2 | async-start | bytes 524288 | tf_op jit(solution)/shard_map/all_to_all | solution.py:87
  86.6 6.4 %all-to-all-done.2 = bf16[8,256,64]{1,2,0:T(8,128)(2,1)S(1)} async-done(((bf16[8,256,64]{1,2,0:T(8,128)(2,1)}), bf16[8,256,64]{1,2,0:T(8,128)(2,1)S(1)}, u32[]{:S(2)}, u32[]{:S(2)}) %all-to-all-start.2) | async-done | bytes 262176 | tf_op jit(solution)/shard_map/all_to_all | solution.py:87
  93.6 3.9 %multiply_convert_fusion.1 = (bf16[256,2048]{1,0:T(8,128)(2,1)S(1)}, f32[256,2048]{1,0:T(8,128)}) fusion(bf16[256,512]{0,1:T(8,128)(2,1)S(1)} %bitcast.244, bf16[2,512,2048]{2,1,0:T(8,128)(2,1)} %param.12), kind=kOutput, calls=%fused_computation.32 | convolution fusion | flops 539492352 | bytes 5505024 | tf_op jit(solution)/shard_map/jvp()/dot_general | solution.py:25
  97.4 1.0 copy-done.9
  98.8 1.5 select_convert_fusion.1
  101.3 1.1 fusion.52
  103.1 3.7 %multiply_convert_fusion = (bf16[256,2048]{1,0:T(8,128)(2,1)S(1)}, f32[256,2048]{1,0:T(8,128)}) fusion(bf16[2,512,2048]{2,1,0:T(8,128)(2,1)} %param.12, f32[256,512]{1,0:T(8,128)S(1)} %get-tuple-element.55, f32[256]{0:T(256)S(1)} %fusion.98, f32[256]{0:T(256)S(1)} %broadcast_multiply_fusion.1), kind=kOutput, calls=%fused_computation.30 | convolution fusion | flops 539885568 | bytes 5769216 | tf_op jit(solution)/shard_map/jvp()/dot_general | solution.py:25
  106.8 0.9 slice_bitcast_fusion
  108.6 2.5 select_convert_fusion
  112.1 1.5 multiply_reduce_fusion.3
  113.7 2.2 fusion.108
  115.9 1.1 convolution_convert_fusion.14
  119.3 3.6 %multiply_reduce_fusion.2 = (f32[256]{0:T(256)S(1)}, f32[256,512]{1,0:T(8,128)S(1)}) fusion(f32[256,512]{1,0:T(8,128)S(1)} %get-tuple-element.55, f32[256]{0:T(256)S(1)} %broadcast_multiply_fusion.1, bf16[2,512,2048]{2,1,0:T(8,128)(2,1)} %param.12, f32[256,2048]{1,0:T(8,128)} %get-tuple-element.57, bf16[256,512]{1,0:T(8,128)(2,1)S(1)} %copy.159, ...), kind=kOutput, calls=%fused_computation.120 | convolution fusion | flops 546438912 | bytes 6293504 | tf_op jit(solution)/shard_map/transpose(jvp())/dot_general | solution.py:25
  122.9 2.7 fusion
  125.9 1.2 fusion.25
  127.7 0.9 fusion.106
  128.6 1.0 convolution_convert_fusion.12
  130.6 1.1 fusion.112
  131.8 1.0 fusion.113
  132.8 1.1 fusion.24
  133.9 1.1 copy.162
  135.0 1.8 copy.163
  137.7 2.9 add_convert_fusion.1
  140.6 1.4 fusion.1
  142.2 3.9 %add_convert_fusion = f32[2,512,2048]{2,1,0:T(8,128)} fusion(bf16[1,512,2048]{2,1,0:T(8,128)(2,1)S(1)} %fusion.1, bf16[1,512,2048]{2,1,0:T(8,128)(2,1)S(1)} %copy-done.14), kind=kLoop, calls=%fused_computation.5 | loop fusion | flops 4194304 | bytes 12582912 | tf_op jit(solution)/shard_map/convert_element_type | solution.py:108
  146.1 3.5 %multiply_reduce_fusion = (f32[256]{0:T(256)S(1)}, f32[256,512]{1,0:T(8,128)S(1)}) fusion(f32[256,512]{1,0:T(8,128)S(1)} %copy.122, f32[256]{0:T(256)S(1)} %broadcast_multiply_fusion.3, bf16[2,512,2048]{2,1,0:T(8,128)(2,1)} %param.12, f32[256,2048]{1,0:T(8,128)} %get-tuple-element.49, bf16[256,512]{1,0:T(8,128)(2,1)} %copy.164, ...), kind=kOutput, calls=%fused_computation.115 | convolution fusion | flops 546438912 | bytes 6293504 | tf_op jit(solution)/shard_map/transpose(jvp())/dot_general | solution.py:25
  150.2 11.7 %all_to_all.55 = bf16[256,8,64]{0,2,1:T(8,128)(2,1)S(1)} all-to-all(bf16[256,8,64]{0,2,1:T(8,128)(2,1)S(1)} %bitcast.227), channel_id=1, replica_groups=mesh['seq'=16,'col'=8] {'col'}, dimensions={1} | all-to-all | bytes 524288 | tf_op jit(solution)/shard_map/all_to_all | solution.py:95
  162.0 1.0 copy.146
  163.0 6.4 %scatter_custom_fusion.2 = bf16[4096,64]{1,0:T(8,128)(2,1)S(1)} fusion(s32[2048]{0:T(1024)S(1)} %broadcast_select_fusion, bf16[2048,64]{1,0:T(8,128)(2,1)} %copy.146, bf16[]{:T(256)} %constant.70.clone.1), kind=kCustom, calls=%fused_computation.109 | custom fusion | bytes 524800
  169.4 1.1 copy.147
  170.5 3.6 %all-to-all-start.4 = ((bf16[16,256,64]{1,2,0:T(8,128)(2,1)}), bf16[16,256,64]{1,2,0:T(8,128)(2,1)S(1)}, u32[]{:S(2)}, u32[]{:S(2)}) async-start(bf16[16,256,64]{1,2,0:T(8,128)(2,1)} %copy.147), calls=%async_computation.4 | async-start | bytes 1048576 | tf_op jit(solution)/shard_map/all_to_all | solution.py:101
  174.1 1.0 fusion.38
  175.1 1.7 convolution_convert_fusion.15
  176.9 60.5 %psum.21 = bf16[256,64]{0,1:T(8,128)(2,1)S(1)} all-reduce(bf16[256,64]{0,1:T(8,128)(2,1)S(1)} %convolution_convert_fusion.15), channel_id=1, replica_groups=mesh['seq'=16,'col'=8] {'seq'}, use_global_device_ids=true, to_apply=%region_22.23 | all-reduce | flops 16384 | bytes 65536 | tf_op jit(solution)/shard_map/psum | solution.py:98
  238.0 1.7 copy.165
  239.7 23.2 %scatter_custom_fusion = f32[4096,64]{1,0:T(8,128)S(1)} fusion(s32[4096]{0:T(1024)S(1)} %bitcast.257, f32[4096,64]{1,0:T(8,128)} %bitcast.223, f32[]{:T(128)} %constant.72.clone.1), kind=kCustom, calls=%fused_computation.79 | custom fusion | flops 262144 | bytes 1049088 | tf_op jit(solution)/shard_map/scatter-add | solution.py:106
  262.9 1.6 copy.150
  264.4 49.1 %all-reduce.7.cloned.1.call-done = (f32[2,512,2048]{2,1,0:T(8,128)}, f32[2,512,512]{2,1,0:T(8,128)}) async-done(((f32[2,512,2048]{2,1,0:T(8,128)}, f32[2,512,512]{2,1,0:T(8,128)}), (f32[2,512,2048]{2,1,0:T(8,128)}, f32[2,512,512]{2,1,0:T(8,128)})) %all-reduce.7.cloned.1.call-update) | async-done | bytes 10485776 | tf_op jit(solution)/shard_map/psum | solution.py:110
  313.5 8.0 %copy.221 = f32[2,512,2048]{2,1,0:T(8,128)} copy(f32[2,512,2048]{2,1,0:T(8,128)} %get-tuple-element.73) | data formatting | bytes 16777216
  321.5 1.3 copy.222
  (152 shorter events, 18.5 us)
Async XLA Ops:
  7.2 70.8 %copy-start = (bf16[256,64]{0,1:T(8,128)(2,1)S(1)}, bf16[256,64]{0,1:T(8,128)(2,1)}, u32[]{:S(2)}) copy-start(bf16[256,64]{0,1:T(8,128)(2,1)} %param.11) | copy-start | bytes 98308
  25.8 15.0 %all-to-all-start = ((s32[16,1,256]{2,1,0:T(1,128)}), s32[16,1,256]{2,1,0:T(1,128)S(1)}, u32[]{:S(2)}, u32[]{:S(2)}) async-start(s32[16,1,256]{2,1,0:T(1,128)} %bitcast.6), calls=%async_computation | async-start | bytes 32768 | tf_op jit(solution)/shard_map/all_to_all | solution.py:78
  66.6 11.4 %copy-start.35 = (s32[2048]{0:T(1024)S(1)}, s32[2048]{0:T(1024)}, u32[]{:S(2)}) copy-start(s32[2048]{0:T(1024)} %param.17) | copy-start | bytes 24580
  77.7 8.8 %copy-start.34 = (s32[1,256]{1,0:T(1,128)S(1)}, s32[1,256]{1,0:T(1,128)}, u32[]{:S(2)}) copy-start(s32[1,256]{1,0:T(1,128)} %param.18) | copy-start | bytes 3076
  79.2 13.8 %all-to-all-start.2 = ((bf16[8,256,64]{1,2,0:T(8,128)(2,1)}), bf16[8,256,64]{1,2,0:T(8,128)(2,1)S(1)}, u32[]{:S(2)}, u32[]{:S(2)}) async-start(bf16[8,256,64]{1,2,0:T(8,128)(2,1)} %bitcast.214), calls=%async_computation.2 | async-start | bytes 524288 | tf_op jit(solution)/shard_map/all_to_all | solution.py:87
  86.5 227.0 %all-reduce.7.cloned.1.call-start = ((), (), s32[]{:S(2)}) async-start(), calls=%async_computation.5 | async-start | bytes 20971520 | tf_op jit(solution)/shard_map/psum | solution.py:110
  97.4 1.0 copy-start.9
  98.5 1.9 copy-start.26
  98.6 1.7 copy-start.17
  98.8 1.6 copy-start.19
  100.3 0.8 copy-start.12
  100.3 2.1 copy-start.3
  102.4 4.3 %copy-start.7 = (bf16[256,512]{1,0:T(8,128)(2,1)}, bf16[256,512]{1,0:T(8,128)(2,1)S(1)}, u32[]{:S(2)}) copy-start(bf16[256,512]{1,0:T(8,128)(2,1)S(1)} %fusion.52) | copy-start | bytes 786436
  106.8 1.9 copy-start.15
  107.8 3.4 %copy-start.21 = (bf16[256,512]{0,1:T(8,128)(2,1)}, bf16[256,512]{0,1:T(8,128)(2,1)S(1)}, u32[]{:S(2)}) copy-start(bf16[256,512]{0,1:T(8,128)(2,1)S(1)} %copy.170) | copy-start | bytes 786436
  108.6 2.6 copy-start.28
  111.2 1.0 copy-start.2
  113.7 3.3 copy-start.29
  113.7 3.3 copy-start.37
  117.0 1.0 copy-start.23
  117.0 1.2 copy-start.22
  117.9 1.0 copy-start.24
  119.3 3.6 %copy-start.30 = (bf16[256,512]{1,0:T(8,128)(2,1)S(1)}, bf16[256,512]{1,0:T(8,128)(2,1)}, u32[]{:S(2)}) copy-start(bf16[256,512]{1,0:T(8,128)(2,1)} %get-tuple-element.34) | copy-start | bytes 786436
  119.3 3.6 %copy-start.39 = (f32[256,2048]{1,0:T(8,128)S(1)}, f32[256,2048]{1,0:T(8,128)}, u32[]{:S(2)}) copy-start(f32[256,2048]{1,0:T(8,128)} %get-tuple-element.57) | copy-start | bytes 6291460
  122.9 3.0 copy-start.8
  125.6 1.5 copy-start.4
  125.6 1.5 copy-start.10
  127.2 1.4 copy-start.13
  127.6 2.0 copy-start.27
  127.7 2.0 copy-start.36
  129.7 1.0 copy-start.20
  129.7 2.1 copy-start.18
  130.6 2.2 copy-start.5
  132.8 4.0 %copy-start.25 = (bf16[4,256,128]{1,2,0:T(8,128)(2,1)S(1)}, bf16[4,256,128]{1,2,0:T(8,128)(2,1)}, u32[]{:S(2)}) copy-start(bf16[4,256,128]{1,2,0:T(8,128)(2,1)} %fusion.112) | copy-start | bytes 786436
  137.7 2.9 copy-start.31
  137.7 2.9 copy-start.32
  137.7 2.9 copy-start.33
  137.7 2.9 copy-start.38
  140.6 1.6 copy-start.14
  162.0 8.6 %copy-start.16 = (bf16[8,8,8,256]{3,2,0,1:T(8,128)(2,1)}, bf16[8,8,8,256]{3,2,0,1:T(8,128)(2,1)S(1)}, u32[]{:S(2)}) copy-start(bf16[8,8,8,256]{3,2,0,1:T(8,128)(2,1)S(1)} %copy.176) | copy-start | bytes 786436
  162.0 12.1 %copy-start.6 = (bf16[256,512]{1,0:T(8,128)(2,1)S(1)}, bf16[256,512]{1,0:T(8,128)(2,1)}, u32[]{:S(2)}) copy-start(bf16[256,512]{1,0:T(8,128)(2,1)} %get-tuple-element.32) | copy-start | bytes 786436
  170.5 67.5 %all-to-all-start.4 = ((bf16[16,256,64]{1,2,0:T(8,128)(2,1)}), bf16[16,256,64]{1,2,0:T(8,128)(2,1)S(1)}, u32[]{:S(2)}, u32[]{:S(2)}) async-start(bf16[16,256,64]{1,2,0:T(8,128)(2,1)} %copy.147), calls=%async_computation.4 | async-start | bytes 1048576 | tf_op jit(solution)/shard_map/all_to_all | solution.py:101
  313.5 8.0 %copy-start.11 = (f32[2,512,512]{2,1,0:T(8,128)S(1)}, f32[2,512,512]{2,1,0:T(8,128)}, u32[]{:S(2)}) copy-start(f32[2,512,512]{2,1,0:T(8,128)} %get-tuple-element.74) | copy-start | bytes 6291460
  313.5 9.4 %copy-start.1 = (bf16[256,64]{0,1:T(8,128)(2,1)S(1)}, bf16[256,64]{0,1:T(8,128)(2,1)}, u32[]{:S(2)}) copy-start(bf16[256,64]{0,1:T(8,128)(2,1)} %param.11) | copy-start | bytes 98308
Sparse Core Ops, SparseCore 0:
  146.3 167.1 all-reduce.6
where the time goes:
time: 331 us; the launch traced here: 330 us
  blocking collectives  84.8 us (26%)
  local copies, waits for them, and re-layouts  66.8 us (20%)
  waiting for transfers between devices  60.4 us (18%)
  other arithmetic  45.9 us (14%)
  matrix products  37.6 us (11%)
  starting transfers between devices  19.5 us (6%)
  between operations  14.7 us (4%)
    psum x1, blocking collectives, on_device(): lax.psum(hot_part.astype(jnp.bfloat16), 'seq').astype(jnp.float32)  60.5 us
    psum x1, waiting for transfers between devices, on_device(): grad_in, grad_out = lax.psum((local_in, local_out), ('seq', 'col'))  49.1 us
    unnamed x88, local copies, waits for them, and re-layouts  31.5 us
    scatter-add x1, other arithmetic, on_device(): table_grad = jnp.zeros(item_table.shape, jnp.float32).at[row_target].add(...  23.2 us
    dot_general x6, matrix products, hstu_layer(): jnp.dot(normed, proj_in, preferred_element_type=jnp.float32)  18.7 us
    all_to_all x1, blocking collectives, on_device(): lax.all_to_all(picked, 'seq', split_axis=0, concat_axis=0, tiled=True)  12.6 us
    gather x2, local copies, waits for them, and re-layouts, on_device(): jnp.take(item_table, jnp.clip(received, 0, item_table.shape[0] - 1), axis=0)  12.5 us
    all_to_all x1, blocking collectives, on_device(): lax.all_to_all(grad_emb, 'col', split_axis=1, concat_axis=0, tiled=True)  11.7 us
  transfers between devices with their start and end apart: 4, of which 3 were waited for; matrix products, arithmetic and copies ran while one was open for 13% of the time, Pallas kernels for 0%

commit v1 on v0

v1 whole, which is shorter than its diff:
```python
import jax
import jax.numpy as jnp
from jax import lax
from jax.experimental import pallas as pl
from jax.experimental.pallas import tpu as pltpu
from jax.sharding import PartitionSpec as P

F32 = jnp.float32
BF16 = jnp.bfloat16
I32 = jnp.int32

D = 512
HEADS = 4
HEAD_DIM = 128
LAYERS = 2
TOK = 256
N_SEQ = 16
N_COL = 8
SEQ_TOK = TOK * N_COL
CAP = 256
SLOTS = N_SEQ * CAP
ITEMS_DEV = 4096
HOT = 256
COLS = 64
CHUNK = 176
VMEM_LIMIT = 56 * 1024 * 1024

NT = (((1,), (1,)), ((), ()))
TN = (((0,), (0,)), ((), ()))


def params(**more):
    return pltpu.CompilerParams(vmem_limit_bytes=VMEM_LIMIT, **more)


def vmem(count):
    return [pl.BlockSpec(memory_space=pltpu.VMEM)] * count


SMEM = pl.BlockSpec(memory_space=pltpu.SMEM)
ANY = pl.BlockSpec(memory_space=pl.ANY)


def mm(a, b, dims=None):
    if dims is None:
        return jnp.dot(a, b, preferred_element_type=F32)
    return lax.dot_general(a, b, dims, preferred_element_type=F32)


def slot_kernel(owner_ref, item_ref, flag_ref, hot_ref, request_ref, index_ref):
    owner = owner_ref[...]
    regular = flag_ref[...] == 0
    owners = lax.broadcasted_iota(I32, (N_SEQ, SEQ_TOK), 0)
    member = jnp.where((owners == owner) & regular, 1.0, 0.0)
    member_b = member.astype(BF16)
    upper = jnp.where(
        lax.broadcasted_iota(I32, (TOK, TOK), 0) <= lax.broadcasted_iota(I32, (TOK, TOK), 1), 1.0, 0.0
    ).astype(BF16)
    carry = jnp.zeros((N_SEQ, 1), F32)
    requests = jnp.zeros((3 * N_SEQ, CAP), F32)
    item = item_ref[...]
    high = (item >> 6).astype(F32)
    low = (item & 63).astype(F32)
    for block in range(N_COL):
        span = slice(block * TOK, (block + 1) * TOK)
        here = member[:, span]
        count = mm(member_b[:, span], upper) + carry
        carry = count[:, TOK - 1 : TOK]
        slot = jnp.sum((count - 1.0) * here, axis=0, keepdims=True).astype(I32)
        place = jnp.where(
            regular[:, span], owner[:, span] * CAP + slot, SLOTS + hot_ref[:, span]
        )
        index_ref[block : block + 1, :] = place
        slots = lax.broadcasted_iota(I32, (CAP, TOK), 0)
        pick = jnp.where(slots == slot, 1.0, 0.0).astype(BF16)
        parts = jnp.concatenate([here * high[:, span], here * low[:, span], here], axis=0)
        requests += mm(parts.astype(BF16), pick, NT)
    rows = requests[:N_SEQ] * 64.0 + requests[N_SEQ : 2 * N_SEQ]
    rows = jnp.where(requests[2 * N_SEQ :] > 0.5, rows, float(ITEMS_DEV))
    request_ref[...] = rows.astype(I32)


def make_slots(owner, item, flag, hot):
    return pl.pallas_call(
        slot_kernel,
        out_shape=(
            jax.ShapeDtypeStruct((N_SEQ, CAP), I32),
            jax.ShapeDtypeStruct((N_COL, TOK), I32),
        ),
        in_specs=vmem(4),
        out_specs=tuple(vmem(2)),
        compiler_params=params(),
        name="slots",
    )(owner, item, flag, hot)


def widen(packed):
    wide = packed.astype(F32)
    return wide[:, :COLS], wide[:, COLS:]


def narrow(rows):
    return jnp.concatenate([rows[:128], rows[128:]], axis=1).astype(BF16)


def copy_rows(count, unroll, body):
    def step(i, carry):
        for u in range(unroll):
            body(i * unroll + u)
        return carry

    lax.fori_loop(0, count // unroll, step, 0)


def pick_kernel(request_ref, table_ref, out_ref, rows):
    for requester in range(N_SEQ):

        def one(slot):
            row = jnp.minimum(request_ref[requester, slot], ITEMS_DEV - 1)
            rows[pl.ds(requester * CAP + slot, 1), :] = table_ref[pl.ds(row, 1), :]

        copy_rows(CAP, 16, one)
        out_ref[requester] = narrow(rows[requester * CAP : (requester + 1) * CAP, :])


def pick_rows(requests, table):
    return pl.pallas_call(
        pick_kernel,
        out_shape=jax.ShapeDtypeStruct((N_SEQ, 128, 128), BF16),
        in_specs=[SMEM] + vmem(1),
        out_specs=vmem(1)[0],
        scratch_shapes=[pltpu.VMEM((SLOTS, COLS), F32)],
        compiler_params=params(),
        name="pick_rows",
    )(requests, table)


def place_kernel(index_ref, returned_ref, hot_ref, out_ref, source, rows):
    for owner in range(N_SEQ):
        first, second = widen(returned_ref[owner])
        source[owner * CAP : owner * CAP + 128, :] = first
        source[owner * CAP + 128 : (owner + 1) * CAP, :] = second
    source[SLOTS : SLOTS + HOT, :] = hot_ref[...].astype(F32)
    for block in range(N_COL):

        def one(token):
            rows[pl.ds(token, 1), :] = source[pl.ds(index_ref[block, token], 1), :]

        copy_rows(TOK, 16, one)
        out_ref[block] = narrow(rows[...])


def place_rows(index, returned, hot_table):
    return pl.pallas_call(
        place_kernel,
        out_shape=jax.ShapeDtypeStruct((N_COL, 128, 128), BF16),
        in_specs=[SMEM] + vmem(2),
        out_specs=vmem(1)[0],
        scratch_shapes=[pltpu.VMEM((SLOTS + HOT, COLS), F32), pltpu.VMEM((TOK, COLS), F32)],
        compiler_params=params(),
        name="place_rows",
    )(index, returned, hot_table)


def return_kernel(index_ref, grad_ref, out_ref, rows, target):
    target[...] = jnp.zeros_like(target)
    for block in range(N_COL):
        first, second = widen(grad_ref[block])
        rows[block, :128, :] = first
        rows[block, 128:, :] = second
    for block in range(N_COL):

        def one(token):
            target[pl.ds(index_ref[block, token], 1), :] = rows[block, pl.ds(token, 1), :]

        copy_rows(TOK, 16, one)
    for owner in range(N_SEQ):
        out_ref[owner] = narrow(target[owner * CAP : (owner + 1) * CAP, :])


def return_rows(index, grads):
    return pl.pallas_call(
        return_kernel,
        out_shape=jax.ShapeDtypeStruct((N_SEQ, 128, 128), BF16),
        in_specs=[SMEM] + vmem(1),
        out_specs=vmem(1)[0],
        scratch_shapes=[
            pltpu.VMEM((N_COL, TOK, COLS), F32),
            pltpu.VMEM((SLOTS + HOT, COLS), F32),
        ],
        compiler_params=params(),
        name="return_rows",
    )(index, grads)


def scatter_kernel(request_ref, incoming_ref, out_ref, rows, *totals):
    for total in totals:
        total[...] = jnp.zeros_like(total)
    for requester in range(N_SEQ):
        first, second = widen(incoming_ref[requester])
        rows[requester * CAP : requester * CAP + 128, :] = first
        rows[requester * CAP + 128 : (requester + 1) * CAP, :] = second
    part = SLOTS // len(totals)
    per = N_SEQ // len(totals)

    def step(i, carry):
        for u in range(4):
            for t, total in enumerate(totals):
                slot = i * 4 + u
                row = request_ref[t * per + slot // CAP, slot % CAP]
                total[pl.ds(row, 1), :] += rows[pl.ds(t * part + slot, 1), :]
        return carry

    lax.fori_loop(0, part // 4, step, 0)
    for block in range(ITEMS_DEV // 128):
        span = slice(block * 128, (block + 1) * 128)
        value = totals[0][span, :]
        for total in totals[1:]:
            value = value + total[span, :]
        out_ref[:, span] = value.T


def scatter_rows(requests, incoming):
    return pl.pallas_call(
        scatter_kernel,
        out_shape=jax.ShapeDtypeStruct((COLS, ITEMS_DEV), F32),
        in_specs=[SMEM] + vmem(1),
        out_specs=vmem(1)[0],
        scratch_shapes=[pltpu.VMEM((SLOTS, COLS), F32)]
        + [pltpu.VMEM((ITEMS_DEV + 8, COLS), F32)] * 4,
        compiler_params=params(),
        cost_estimate=pl.CostEstimate(flops=0, bytes_accessed=20_000_000, transcendentals=0),
        name="scatter_rows",
    )(requests, incoming).T


def norm(value):
    center = value - jnp.mean(value, axis=-1, keepdims=True)
    scale = lax.rsqrt(jnp.mean(center * center, axis=-1, keepdims=True) + 1e-05)
    return center * scale, scale


def norm_back(grad, normed, scale):
    shift = jnp.mean(grad, axis=-1, keepdims=True)
    tilt = jnp.mean(grad * normed, axis=-1, keepdims=True)
    return scale * (grad - shift - normed * tilt)


def silu_parts(value):
    gate = jax.nn.sigmoid(value)
    return value * gate, gate * (1.0 + value * (1.0 - gate))


def places():
    seq, col = lax.axis_index("seq"), lax.axis_index("col")
    y, x, core = seq & 3, col >> 1, col & 1
    return x, y, core


def stack_kernel(
    index_ref, emb_ref, win_ref, wout_ref, segment_ref, cot_ref,
    enc_ref, grad_ref, *refs
):
    outs, refs = refs[:8], refs[8:]
    stream, normed, normed_scale, proj, slope, attn, attn_slope, mixed, mixed_scale, gated, dproj, pay, sems = refs
    keep, send = outs[:4], outs[4:]
    x, y, core = places()
    col = lax.axis_index("col")

    segment = jnp.broadcast_to(segment_ref[...].astype(F32), (TOK, TOK))
    row = lax.broadcasted_iota(I32, (TOK, TOK), 0)
    column = lax.broadcasted_iota(I32, (TOK, TOK), 1)
    allowed = (segment == segment.T) & (column <= row)

    for pair in range(N_COL // 2):
        a0, a1 = widen(emb_ref[2 * pair])
        b0, b1 = widen(emb_ref[2 * pair + 1])
        lanes = slice(pair * 128, (pair + 1) * 128)
        stream[:128, lanes] = jnp.concatenate([a0, b0], axis=1)
        stream[128:, lanes] = jnp.concatenate([a1, b1], axis=1)

    def lanes_of(head):
        return slice(head * HEAD_DIM, (head + 1) * HEAD_DIM)

    scaling = HEAD_DIM ** (-0.5)
    for l in range(LAYERS):
        value, scale = norm(stream[...])
        normed[l] = value
        normed_scale[l] = scale
        rounded = value.astype(BF16)
        for part in range(4):
            pre = mm(rounded, win_ref[l, :, part * D : (part + 1) * D])
            out, tilt = silu_parts(pre)
            proj[l, part] = out.astype(BF16)
            slope[l, part] = tilt
        for head in range(HEADS):
            lanes = lanes_of(head)
            score = mm(proj[l, 2, :, lanes], proj[l, 3, :, lanes], NT) * scaling
            out, tilt = silu_parts(score)
            weight = jnp.where(allowed, out, 0.0).astype(BF16)
            attn[l, head] = weight
            attn_slope[l, head] = jnp.where(allowed, tilt * scaling, 0.0)
            mixed[l, :, lanes] = mm(weight, proj[l, 1, :, lanes])
        value, scale = norm(mixed[l])
        mixed[l] = value
        mixed_scale[l] = scale
        product = (value * proj[l, 0].astype(F32)).astype(BF16)
        gated[l] = product
        stream[...] += mm(product, wout_ref[l])
    enc_ref[...] = stream[...].astype(BF16)

    stream[...] = cot_ref[...].astype(F32)
    for l in reversed(range(LAYERS)):
        first, second = (x, y) if l == 0 else (y, x)

        def put(part, value):
            for a in range(4):
                for b in range(4):
                    chunk = 4 * a + b
                    place = 4 * ((a - first) & 3) + ((b - second) & 3)
                    pay[l, place, part * 32 : (part + 1) * 32, :] = value[chunk * 32 : (chunk + 1) * 32, :]

        grad = stream[...]
        grad_b = grad.astype(BF16)
        put(4, mm(gated[l], grad_b, TN).astype(BF16))
        dgated = mm(grad_b, wout_ref[l], NT).astype(BF16).astype(F32)
        hat = mixed[l]
        dproj[0] = ((dgated * hat).astype(BF16).astype(F32) * slope[l, 0]).astype(BF16)
        dmixed = norm_back(dgated * proj[l, 0].astype(F32), hat, mixed_scale[l]).astype(BF16)
        for head in range(HEADS):
            lanes = lanes_of(head)
            dmix = dmixed[:, lanes]
            dvalue = mm(attn[l, head], dmix, TN).astype(BF16).astype(F32)
            dproj[1, :, lanes] = (dvalue * slope[l, 1, :, lanes]).astype(BF16)
            dattn = mm(dmix, proj[l, 1, :, lanes], NT).astype(BF16).astype(F32)
            dscore = (dattn * attn_slope[l, head]).astype(BF16)
            dquery = mm(dscore, proj[l, 3, :, lanes]).astype(BF16).astype(F32)
            dproj[2, :, lanes] = (dquery * slope[l, 2, :, lanes]).astype(BF16)
            dkey = mm(dscore, proj[l, 2, :, lanes], TN).astype(BF16).astype(F32)
            dproj[3, :, lanes] = (dkey * slope[l, 3, :, lanes]).astype(BF16)
        value = normed[l]
        rounded = value.astype(BF16)
        dnormed = jnp.zeros((TOK, D), F32)
        for part in range(4):
            dpre = dproj[part]
            put(part, mm(rounded, dpre, TN).astype(BF16))
            dnormed += mm(dpre, win_ref[l, :, part * D : (part + 1) * D], NT)
        dnormed = dnormed.astype(BF16).astype(F32)
        stream[...] = grad + norm_back(dnormed, value, normed_scale[l])

    grad = stream[...]
    for pair in range(N_COL // 2):
        top = grad[:128, pair * 128 : (pair + 1) * 128]
        bottom = grad[128:, pair * 128 : (pair + 1) * 128]
        grad_ref[2 * pair] = jnp.concatenate([top[:, :COLS], bottom[:, :COLS]], axis=1).astype(BF16)
        grad_ref[2 * pair + 1] = jnp.concatenate([top[:, COLS:], bottom[:, COLS:]], axis=1).astype(BF16)
    hot_row = index_ref[pl.ds(col, 1), :] - SLOTS
    pick = jnp.where(lax.broadcasted_iota(I32, (HOT, TOK), 0) == hot_row, 1.0, 0.0).astype(BF16)
    hot_part = mm(pick, grad.astype(BF16)).astype(BF16)
    for l in range(LAYERS):
        first, second = (x, y) if l == 0 else (y, x)
        for a in range(4):
            for b in range(4):
                chunk = 4 * a + b
                place = 4 * ((a - first) & 3) + ((b - second) & 3)
                pay[l, place, 160:CHUNK, :] = hot_part[chunk * 16 : (chunk + 1) * 16, :]
    copies = []
    for a in range(4):
        for i, (outs_here, layer) in enumerate(((send, 1 - core), (keep, core))):
            copies.append(
                pltpu.make_async_copy(pay.at[layer, pl.ds(4 * a, 4)], outs_here[a], sems.at[i, a])
            )
    for copy in copies:
        copy.start()
    for copy in copies:
        copy.wait()


def run_stack(index, emb, weight_in, weight_out, segment, cotangent):
    piece = jax.ShapeDtypeStruct((4, CHUNK, D), BF16)
    return pl.pallas_call(
        stack_kernel,
        out_shape=(
            jax.ShapeDtypeStruct((TOK, D), BF16),
            jax.ShapeDtypeStruct((N_COL, 128, 128), BF16),
        )
        + (piece,) * 8,
        in_specs=vmem(6),
        out_specs=tuple(vmem(2)) + (ANY,) * 8,
        scratch_shapes=[
            pltpu.VMEM((TOK, D), F32),
            pltpu.VMEM((LAYERS, TOK, D), F32),
            pltpu.VMEM((LAYERS, TOK, 1), F32),
            pltpu.VMEM((LAYERS, 4, TOK, D), BF16),
            pltpu.VMEM((LAYERS, 4, TOK, D), F32),
            pltpu.VMEM((LAYERS, HEADS, TOK, TOK), BF16),
            pltpu.VMEM((LAYERS, HEADS, TOK, TOK), F32),
            pltpu.VMEM((LAYERS, TOK, D), F32),
            pltpu.VMEM((LAYERS, TOK, 1), F32),
            pltpu.VMEM((LAYERS, TOK, D), BF16),
            pltpu.VMEM((4, TOK, D), BF16),
            pltpu.VMEM((LAYERS, 16, CHUNK, D), BF16),
            pltpu.SemaphoreType.DMA((2, 4)),
        ],
        compiler_params=params(),
        name="layers",
    )(index, emb, weight_in, weight_out, segment, cotangent)


def device_pairs(move):
    pairs = []
    for z in range(4):
        for y in range(4):
            for x in range(4):
                for core in range(2):
                    tz, ty, tx, tcore = move(z, y, x, core)
                    pairs.append(
                        (((z * 4 + y) * 4 + x) * 2 + core, ((tz * 4 + ty) * 4 + tx) * 2 + tcore)
                    )
    return pairs


BOTH = ("seq", "col")


def to_core(value):
    return lax.ppermute(value, BOTH, device_pairs(lambda z, y, x, c: (z, y, x, 1 - c)))


def along_first(value, k):
    def move(z, y, x, c):
        return (z, y, (x + k) % 4, c) if c == 0 else (z, (y + k) % 4, x, c)

    return lax.ppermute(value, BOTH, device_pairs(move))


def along_second(value, k):
    def move(z, y, x, c):
        return (z, (y + k) % 4, x, c) if c == 0 else (z, y, (x + k) % 4, c)

    return lax.ppermute(value, BOTH, device_pairs(move))


def along_z(value, k):
    return lax.ppermute(value, BOTH, device_pairs(lambda z, y, x, c: ((z + k) % 4, y, x, c)))


def add_all(*terms):
    terms = [t.astype(F32) for t in terms]
    while len(terms) > 1:
        terms = [a + b for a, b in zip(terms[::2], terms[1::2])]
    return terms[0].astype(BF16)


def sum_everywhere(keep, send):
    order = (1, 3, 2, 0)
    got = {k: to_core(send[k]) for k in order}
    chip = {k: add_all(keep[k], got[k]) for k in order}
    came = {k: along_first(chip[k], k) for k in (1, 3, 2)}
    line = add_all(chip[0], came[2], came[1], came[3])
    came = {k: along_second(line[k], k) for k in (1, 3, 2)}
    plane = add_all(line[0], came[2], came[1], came[3])
    came = {k: along_z(plane, k) for k in (1, 3, 2)}
    total = add_all(plane, came[2], came[1], came[3])
    row = jnp.stack([total] + [along_second(total, -k) for k in (1, 2, 3)])
    mine = [row] + [along_first(row, -k) for k in (1, 2, 3)]
    other = [to_core(value) for value in mine]
    return mine, other


def finish_kernel(*refs):
    mine, other = refs[:4], refs[4:8]
    win_ref, wout_ref, hot_ref = refs[8:11]
    stage_in, stage_out, hot_rows, sems = refs[11:]
    x, y, core = places()
    col = lax.axis_index("col")
    pending = [None, None]
    step = 0
    for source, layer, own in ((mine, core, True), (other, 1 - core, False)):
        straight = layer == 0
        first = jnp.where(straight, x, y)
        second = jnp.where(straight, y, x)
        for a in range(4):
            for b in range(4):
                slot = step % 2
                if pending[slot] is not None:
                    for copy in pending[slot]:
                        copy.wait()
                chunk = 4 * ((a + first) & 3) + ((b + second) & 3)
                for part in range(4):
                    stage_in[slot, :, part * D : (part + 1) * D] = source[a][
                        b, part * 32 : (part + 1) * 32, :
                    ].astype(F32)
                stage_out[slot] = source[a][b, 128:160, :].astype(F32)
                if own:
                    hot_rows[pl.ds(pl.multiple_of(chunk * 16, 16), 16), :] = source[a][b, 160:CHUNK, :]
                rows = pl.ds(pl.multiple_of(chunk * 32, 32), 32)
                pending[slot] = [
                    pltpu.make_async_copy(stage_in.at[slot], win_ref.at[layer, rows], sems.at[slot, 0]),
                    pltpu.make_async_copy(stage_out.at[slot], wout_ref.at[layer, rows], sems.at[slot, 1]),
                ]
                for copy in pending[slot]:
                    copy.start()
                step += 1
    pick = jnp.where(
        lax.broadcasted_iota(I32, (D, COLS), 0) == lax.broadcasted_iota(I32, (D, COLS), 1) + col * COLS,
        1.0,
        0.0,
    ).astype(BF16)
    hot_ref[...] = mm(hot_rows[...], pick)
    for copies in pending:
        for copy in copies:
            copy.wait()


def finish(mine, other):
    return pl.pallas_call(
        finish_kernel,
        out_shape=(
            jax.ShapeDtypeStruct((LAYERS, D, 4 * D), F32),
            jax.ShapeDtypeStruct((LAYERS, D, D), F32),
            jax.ShapeDtypeStruct((HOT, COLS), F32),
        ),
        in_specs=vmem(8),
        out_specs=(ANY, ANY, vmem(1)[0]),
        scratch_shapes=[
            pltpu.VMEM((2, 32, 4 * D), F32),
            pltpu.VMEM((2, 32, D), F32),
            pltpu.VMEM((HOT, D), BF16),
            pltpu.SemaphoreType.DMA((2, 2)),
        ],
        compiler_params=params(),
        name="finish",
    )(*mine, *other)


def on_device(
    item_table, hot_table, weight_in, weight_out, row_owner, item_row, hot_flag, hot_row, segment, cotangent
):
    line = (1, SEQ_TOK)
    requests, index = make_slots(
        row_owner.reshape(line), item_row.reshape(line), hot_flag.reshape(line), hot_row.reshape(line)
    )
    received = lax.all_to_all(requests, "seq", split_axis=0, concat_axis=0, tiled=True)
    picked = pick_rows(received, item_table.astype(F32))
    returned = lax.all_to_all(picked, "seq", split_axis=0, concat_axis=0, tiled=True)
    placed = place_rows(index, returned, hot_table)
    emb = lax.all_to_all(placed, "col", split_axis=0, concat_axis=0, tiled=True)
    outs = run_stack(index, emb, weight_in, weight_out, segment, cotangent)
    encoded, grad_emb, keep, send = outs[0], outs[1], outs[2:6], outs[6:10]
    mine, other = sum_everywhere(keep, send)
    grad_columns = lax.all_to_all(grad_emb, "col", split_axis=0, concat_axis=0, tiled=True)
    outgoing = return_rows(index, grad_columns)
    incoming = lax.all_to_all(outgoing, "seq", split_axis=0, concat_axis=0, tiled=True)
    table_grad = scatter_rows(received, incoming)
    grad_in, grad_out, hot_grad = finish(mine, other)
    return (encoded, table_grad, hot_grad, grad_in, grad_out)


def solution(mesh):
    in_specs = (
        P("seq", "col"),
        P(None, "col"),
        P(),
        P(),
        P("seq", None),
        P("seq"),
        P("seq"),
        P("seq"),
        P(("seq", "col"), None),
        P(("seq", "col"), None),
    )
    out_specs = (P(("seq", "col"), None), P("seq", "col"), P(None, "col"), P(), P())
    return jax.shard_map(
        on_device, mesh=mesh, in_specs=in_specs, out_specs=out_specs, check_vma=False
    )
```

time: 331 us -> 230 us (0.69)
  Pallas kernels: 0 us -> 87.5 us
  local copies, waits for them, and re-layouts: 66.8 us -> 8.57 us
  blocking collectives: 84.8 us -> 28.7 us
  other arithmetic: 45.9 us -> 2.44 us
  matrix products: 37.6 us -> 0 us
  starting transfers between devices: 19.5 us -> 46.7 us
  between operations: 14.7 us -> 0.84 us
  waiting for transfers between devices: 60.4 us -> 53.9 us
    pallas_call x0 -> x7, Pallas kernels: none -> 87.5 us  [the longest x1 22.5 us: scatter_rows(): pl.pallas_call(scatter_kernel, out_shape=jax.ShapeDtypeStruct((COLS, ITEM...]
    psum x1 -> x0, blocking collectives: 60.5 us -> none  [on_device(): lax.psum(hot_part.astype(jnp.bfloat16), 'seq').astype(jnp.float32)]
    psum x1 -> x0, waiting for transfers between devices: 49.1 us -> none  [on_device(): grad_in, grad_out = lax.psum((local_in, local_out), ('seq', 'col'))]
    ppermute x0 -> x23, waiting for transfers between devices: none -> 41 us  [the longest x6 19.5 us: along_first(): return lax.ppermute(value, BOTH, device_pairs(move))]
    dot_general x26 -> x0, matrix products: 37.6 us -> none  [the longest x6 18.7 us: hstu_layer(): jnp.dot(normed, proj_in, preferred_element_type=jnp.float32)]
    unnamed x88 -> x23, local copies, waits for them, and re-layouts: 31.5 us -> 4.49 us
    ppermute x0 -> x23, starting transfers between devices: none -> 26.8 us  [the longest x8 13.6 us: to_core(): lax.ppermute(value, BOTH, device_pairs(lambda z, y, x, c: (z, y, x, 1 - c)))]
    gather x4 -> x0, local copies, waits for them, and re-layouts: 23.8 us -> none  [the longest x2 12.5 us: on_device(): jnp.take(item_table, jnp.clip(received, 0, item_table.shape[0] - 1), axis=0)]
  transfers between devices with their start and end apart: 4 -> 26, of which waited for: 3 -> 15; matrix products, arithmetic and copies ran while one was open for 13% -> 2% of each run, Pallas kernels for 0% -> 13%
where the time goes in v1:
time: 230 us; the launch traced here: 229 us
  Pallas kernels  87.5 us (38%)
  waiting for transfers between devices  53.9 us (23%)
  starting transfers between devices  46.7 us (20%)
  blocking collectives  28.7 us (12%)
  local copies, waits for them, and re-layouts  8.57 us (4%)
  other arithmetic  2.44 us (1%)
    pallas_call x1, Pallas kernels, scatter_rows(): pl.pallas_call(scatter_kernel, out_shape=jax.ShapeDtypeStruct((COLS, ITEM...  22.5 us
    ppermute x6, waiting for transfers between devices, along_first(): return lax.ppermute(value, BOTH, device_pairs(move))  19.5 us
    pallas_call x1, Pallas kernels, run_stack(): pl.pallas_call(stack_kernel, out_shape=(jax.ShapeDtypeStruct((TOK, D), BF...  16.8 us
    pallas_call x1, Pallas kernels, pick_rows(): pl.pallas_call(pick_kernel, out_shape=jax.ShapeDtypeStruct((N_SEQ, 128, 1...  16.2 us
    pallas_call x1, Pallas kernels, finish(): pl.pallas_call(finish_kernel, out_shape=(jax.ShapeDtypeStruct((LAYERS, D,...  15.2 us
    all_to_all x1, blocking collectives, on_device(): lax.all_to_all(outgoing, 'seq', split_axis=0, concat_axis=0, tiled=True)  14.8 us
    all_to_all x1, blocking collectives, on_device(): emb = lax.all_to_all(placed, 'col', split_axis=0, concat_axis=0, tiled=True)  13.9 us
    ppermute x8, starting transfers between devices, to_core(): lax.ppermute(value, BOTH, device_pairs(lambda z, y, x, c: (z, y, x, 1 - c)))  13.6 us
  transfers between devices with their start and end apart: 26, of which 15 were waited for; matrix products, arithmetic and copies ran while one was open for 2% of the time, Pallas kernels for 13%

profile of v1, /device:TPU:1, one launch (start us, length us, event | category | flops | bytes accessed | tf_op | source)
XLA Modules:
  0.0 228.7 jit_solution(14135282702402759570)
XLA Ops:
  0.6 2.4 %slots.1 = (s32[16,256]{1,0:T(8,128)}, s32[8,256]{1,0:T(8,128)}) custom-call(s32[1,2048]{1,0:T(1,128)} %bitcast.32, s32[1,2048]{1,0:T(1,128)} %bitcast.33, s32[1,2048]{1,0:T(1,128)} %bitcast.34, s32[1,2048]{1,0:T(1,128)} %bitcast.35), custom_call_target="tpu_custom_call" | custom-call | tf_op jit(solution)/shard_map/slots/pallas_call | solution.py:84
  3.1 1.3 copy.22
  4.4 8.6 %all-to-all-start = ((s32[16,1,256]{2,1,0:T(1,128)}), s32[16,1,256]{2,1,0:T(1,128)S(1)}, u32[]{:S(2)}, u32[]{:S(2)}) async-start(s32[16,1,256]{2,1,0:T(1,128)} %copy.22), calls=%async_computation | async-start | bytes 32768 | tf_op jit(solution)/shard_map/all_to_all | solution.py:544
  13.0 2.7 %copy.23.table_ref = f32[4096,64]{1,0:T(8,128)} copy(bf16[4096,64]{0,1:T(8,128)(2,1)} %param.10) | data formatting | bytes 1572864 | tf_op jit(solution)/shard_map/convert_element_type | solution.py:545
  15.7 3.7 %all-to-all-done = s32[16,1,256]{2,1,0:T(1,128)S(1)} async-done(((s32[16,1,256]{2,1,0:T(1,128)}), s32[16,1,256]{2,1,0:T(1,128)S(1)}, u32[]{:S(2)}, u32[]{:S(2)}) %all-to-all-start) | async-done | bytes 16416 | tf_op jit(solution)/shard_map/all_to_all | solution.py:544
  19.4 0.6 copy.28
  20.0 16.2 %pick_rows.1 = bf16[16,128,128]{2,1,0:T(8,128)(2,1)} custom-call(s32[16,256]{1,0:T(8,128)} %bitcast.29, f32[4096,64]{1,0:T(8,128)} %copy.23.table_ref), custom_call_target="tpu_custom_call" | custom-call | tf_op jit(solution)/shard_map/pick_rows/pallas_call | solution.py:127
  36.2 3.6 %all-to-all-start.1 = ((bf16[16,128,128]{2,1,0:T(8,128)(2,1)}), bf16[16,128,128]{2,1,0:T(8,128)(2,1)S(1)}, u32[]{:S(2)}, u32[]{:S(2)}) async-start(bf16[16,128,128]{2,1,0:T(8,128)(2,1)} %pick_rows.1), calls=%async_computation.1 | async-start | bytes 1048576 | tf_op jit(solution)/shard_map/all_to_all | solution.py:546
  39.8 0.7 copy.24.hot_ref
  40.5 8.7 %all-to-all-done.1.returned_ref = bf16[16,128,128]{2,1,0:T(8,128)(2,1)S(1)} async-done(((bf16[16,128,128]{2,1,0:T(8,128)(2,1)}), bf16[16,128,128]{2,1,0:T(8,128)(2,1)S(1)}, u32[]{:S(2)}, u32[]{:S(2)}) %all-to-all-start.1) | async-done | bytes 524320 | tf_op jit(solution)/shard_map/all_to_all | solution.py:546
  49.3 0.8 copy-done.1
  50.0 7.5 %place_rows.1 = bf16[8,128,128]{2,1,0:T(8,128)(2,1)} custom-call(s32[8,256]{1,0:T(8,128)} %get-tuple-element.20.index_ref, bf16[16,128,128]{2,1,0:T(8,128)(2,1)} %copy-done.1, bf16[256,64]{1,0:T(8,128)(2,1)} %copy.24.hot_ref), custom_call_target="tpu_custom_call" | custom-call | tf_op jit(solution)/shard_map/place_rows/pallas_call | solution.py:154
  57.5 13.9 %all_to_all.31.emb_ref = bf16[8,128,128]{2,1,0:T(8,128)(2,1)} all-to-all(bf16[8,128,128]{2,1,0:T(8,128)(2,1)} %place_rows.1), channel_id=1, replica_groups=mesh['seq'=16,'col'=8] {'col'}, dimensions={0} | all-to-all | bytes 524288 | tf_op jit(solution)/shard_map/all_to_all | solution.py:548
  71.5 16.8 %layers.1 = (bf16[256,512]{1,0:T(8,128)(2,1)}, bf16[8,128,128]{2,1,0:T(8,128)(2,1)}, bf16[4,176,512]{2,1,0:T(8,128)(2,1)}, bf16[4,176,512]{2,1,0:T(8,128)(2,1)},...) custom-call(s32[8,256]{1,0:T(8,128)} %get-tuple-element.20.index_ref, ...), custom_call_target="tpu_custom_call" | custom-call | tf_op jit(solution)/shard_map/layers/pallas_call | solution.py:381
  88.3 1.1 collective-permute-start.1
  90.0 1.4 collective-permute-done.1
  91.4 1.3 add_convert_fusion.3
  92.7 0.5 collective-permute-start.2
  94.0 2.7 %collective-permute-start.6 = (bf16[4,176,512]{2,1,0:T(8,128)(2,1)S(1)}, bf16[4,176,512]{2,1,0:T(8,128)(2,1)S(1)}, u32[]{:S(2)}, u32[]{:S(2)}) collective-permute-start(bf16[4,176,512]{2,1,0:T(8,128)(2,1)S(1)} %add_convert_fusion.1), channel_id=1, source_target_pairs={{0,6},{1,25},{2,0},{3,27},{4,2},{5,29},{6,4},{7,31},{8,14},{9,1},{... | collective-permute-start | bytes 2162696 | tf_op jit(solution)/shard_map/ppermute | solution.py:434
  96.7 8.1 %collective-permute-done.2 = bf16[4,176,512]{2,1,0:T(8,128)(2,1)S(1)} collective-permute-done((bf16[4,176,512]{2,1,0:T(8,128)(2,1)S(1)}, bf16[4,176,512]{2,1,0:T(8,128)(2,1)S(1)}, u32[]{:S(2)}, u32[]{:S(2)}) %collective-permute-start.2) | collective-permute-done | bytes 720928 | tf_op jit(solution)/shard_map/ppermute | solution.py:434
  104.8 7.7 %collective-permute-done.4 = bf16[4,176,512]{2,1,0:T(8,128)(2,1)S(1)} collective-permute-done((bf16[4,176,512]{2,1,0:T(8,128)(2,1)S(1)}, bf16[4,176,512]{2,1,0:T(8,128)(2,1)S(1)}, u32[]{:S(2)}, u32[]{:S(2)}) %collective-permute-start.4) | collective-permute-done | bytes 720928 | tf_op jit(solution)/shard_map/ppermute | solution.py:434
  113.1 1.5 collective-permute-start.8
  114.6 1.3 collective-permute-start.9
  115.9 3.4 %collective-permute-done.7 = bf16[176,512]{1,0:T(8,128)(2,1)S(1)} collective-permute-done((bf16[176,512]{1,0:T(8,128)(2,1)S(1)}, bf16[176,512]{1,0:T(8,128)(2,1)S(1)}, u32[]{:S(2)}, u32[]{:S(2)}) %collective-permute-start.7) | collective-permute-done | bytes 180256 | tf_op jit(solution)/shard_map/ppermute | solution.py:441
  119.3 1.7 collective-permute-done.8
  121.1 0.6 collective-permute-start.10
  121.7 0.6 collective-permute-start.11
  122.3 2.1 collective-permute-start.12
  124.3 2.7 %collective-permute-done.10 = bf16[176,512]{1,0:T(8,128)(2,1)S(1)} collective-permute-done((bf16[176,512]{1,0:T(8,128)(2,1)S(1)}, bf16[176,512]{1,0:T(8,128)(2,1)S(1)}, u32[]{:S(2)}, u32[]{:S(2)}) %collective-permute-start.10) | collective-permute-done | bytes 180256 | tf_op jit(solution)/shard_map/ppermute | solution.py:445
  127.1 4.8 %collective-permute-done.11 = bf16[176,512]{1,0:T(8,128)(2,1)S(1)} collective-permute-done((bf16[176,512]{1,0:T(8,128)(2,1)S(1)}, bf16[176,512]{1,0:T(8,128)(2,1)S(1)}, u32[]{:S(2)}, u32[]{:S(2)}) %collective-permute-start.11) | collective-permute-done | bytes 180256 | tf_op jit(solution)/shard_map/ppermute | solution.py:445
  132.0 1.4 collective-permute-start.13
  133.4 0.6 collective-permute-start.14
  134.0 2.4 %collective-permute-done.13 = bf16[176,512]{1,0:T(8,128)(2,1)S(1)} collective-permute-done((bf16[176,512]{1,0:T(8,128)(2,1)S(1)}, bf16[176,512]{1,0:T(8,128)(2,1)S(1)}, u32[]{:S(2)}, u32[]{:S(2)}) %collective-permute-start.13) | collective-permute-done | bytes 180256 | tf_op jit(solution)/shard_map/ppermute | solution.py:441
  136.4 3.1 %collective-permute-done.14 = bf16[176,512]{1,0:T(8,128)(2,1)S(1)} collective-permute-done((bf16[176,512]{1,0:T(8,128)(2,1)S(1)}, bf16[176,512]{1,0:T(8,128)(2,1)S(1)}, u32[]{:S(2)}, u32[]{:S(2)}) %collective-permute-start.14) | collective-permute-done | bytes 180256 | tf_op jit(solution)/shard_map/ppermute | solution.py:441
  139.5 1.9 collective-permute-done.15
  141.6 1.4 collective-permute-start.17
  143.1 7.7 %all-to-all-start.3 = ((bf16[8,128,128]{2,1,0:T(8,128)(2,1)}), bf16[8,128,128]{2,1,0:T(8,128)(2,1)S(1)}, u32[]{:S(2)}, u32[]{:S(2)}) async-start(bf16[8,128,128]{2,1,0:T(8,128)(2,1)} %get-tuple-element.23), calls=%async_computation.3 | async-start | bytes 524288 | tf_op jit(solution)/shard_map/all_to_all | solution.py:552
  150.8 1.2 collective-permute-done.16.refs_1_
  152.1 3.2 %collective-permute-start.20 = (bf16[4,176,512]{2,1,0:T(8,128)(2,1)S(1)}, bf16[4,176,512]{2,1,0:T(8,128)(2,1)}, u32[]{:S(2)}, u32[]{:S(2)}) collective-permute-start(bf16[4,176,512]{2,1,0:T(8,128)(2,1)S(1)} %collective-permute-done.16.refs_1_), channel_id=1, source_target_pairs={{0,1},{1,0},{2,3},{3,2},{4,5},{5,4},{6,7},{7,6},{8,9},{9,8},{10,11... | collective-permute-start | bytes 2162696 | tf_op jit(solution)/shard_map/ppermute | solution.py:427
  155.2 3.6 %collective-permute-start.21 = (bf16[4,176,512]{2,1,0:T(8,128)(2,1)S(1)}, bf16[4,176,512]{2,1,0:T(8,128)(2,1)}, u32[]{:S(2)}, u32[]{:S(2)}) collective-permute-start(bf16[4,176,512]{2,1,0:T(8,128)(2,1)S(1)} %collective-permute-done.17.refs_2_), channel_id=1, source_target_pairs={{0,1},{1,0},{2,3},{3,2},{4,5},{5,4},{6,7},{7,6},{8,9},{9,8},{10,11... | collective-permute-start | bytes 2162696 | tf_op jit(solution)/shard_map/ppermute | solution.py:427
  158.8 2.5 %collective-permute-done.18.refs_3_ = bf16[4,176,512]{2,1,0:T(8,128)(2,1)S(1)} collective-permute-done((bf16[4,176,512]{2,1,0:T(8,128)(2,1)S(1)}, bf16[4,176,512]{2,1,0:T(8,128)(2,1)S(1)}, u32[]{:S(2)}, u32[]{:S(2)}) %collective-permute-start.18) | collective-permute-done | bytes 720928 | tf_op jit(solution)/shard_map/ppermute | solution.py:434
  161.4 5.1 %collective-permute-start.22 = (bf16[4,176,512]{2,1,0:T(8,128)(2,1)S(1)}, bf16[4,176,512]{2,1,0:T(8,128)(2,1)}, u32[]{:S(2)}, u32[]{:S(2)}) collective-permute-start(bf16[4,176,512]{2,1,0:T(8,128)(2,1)S(1)} %collective-permute-done.18.refs_3_), channel_id=1, source_target_pairs={{0,1},{1,0},{2,3},{3,2},{4,5},{5,4},{6,7},{7,6},{8,9},{9,8},{10,11... | collective-permute-start | bytes 2162696 | tf_op jit(solution)/shard_map/ppermute | solution.py:427
  166.9 0.7 copy-done.2
  167.6 7.0 %return_rows.1 = bf16[16,128,128]{2,1,0:T(8,128)(2,1)} custom-call(s32[8,256]{1,0:T(8,128)} %get-tuple-element.20.index_ref, bf16[8,128,128]{2,1,0:T(8,128)(2,1)} %copy-done.2), custom_call_target="tpu_custom_call" | custom-call | tf_op jit(solution)/shard_map/return_rows/pallas_call | solution.py:182
  174.6 14.8 %all_to_all.32.incoming_ref = bf16[16,128,128]{2,1,0:T(8,128)(2,1)} all-to-all(bf16[16,128,128]{2,1,0:T(8,128)(2,1)} %return_rows.1), channel_id=1, replica_groups=mesh['seq'=16,'col'=8] {'seq'}, dimensions={0} | all-to-all | bytes 1048576 | tf_op jit(solution)/shard_map/all_to_all | solution.py:554
  189.4 22.5 %scatter_rows.1 = f32[64,4096]{1,0:T(8,128)} custom-call(s32[16,256]{1,0:T(8,128)} %bitcast.30, bf16[16,128,128]{2,1,0:T(8,128)(2,1)} %all_to_all.32.incoming_ref), custom_call_target="tpu_custom_call" | custom-call | bytes 20000000 | tf_op jit(solution)/shard_map/scatter_rows/pallas_call | solution.py:224
  211.9 15.2 %finish.1 = (f32[2,512,2048]{2,1,0:T(8,128)}, f32[2,512,512]{2,1,0:T(8,128)}, f32[256,64]{1,0:T(8,128)}) custom-call(bf16[4,176,512]{2,1,0:T(8,128)(2,1)} %copy-done, bf16[4,176,512]{2,1,0:T(8,128)(2,1)} %copy-done.6, bf16[4,176,512]{2,1,0:T(8,128)(2,1)} %copy-done.7, bf16[4,176,512]{2,1,0:T(8,128)(2,1)} %copy-done.8, ...), custom_call_target="tpu_custom_call" | custom-call | tf_op jit(solution)/shard_map/finish/pallas_call | solution.py:517
  227.1 1.6 copy.25
  (46 shorter events, 2.9 us)
Async XLA Ops:
  4.4 15.0 %all-to-all-start = ((s32[16,1,256]{2,1,0:T(1,128)}), s32[16,1,256]{2,1,0:T(1,128)S(1)}, u32[]{:S(2)}, u32[]{:S(2)}) async-start(s32[16,1,256]{2,1,0:T(1,128)} %copy.22), calls=%async_computation | async-start | bytes 32768 | tf_op jit(solution)/shard_map/all_to_all | solution.py:544
  20.0 19.7 %copy-start.9 = (bf16[256,64]{0,1:T(8,128)(2,1)S(1)}, bf16[256,64]{0,1:T(8,128)(2,1)}, u32[]{:S(2)}) copy-start(bf16[256,64]{0,1:T(8,128)(2,1)} %param.11) | copy-start | bytes 98308
  36.2 13.0 %all-to-all-start.1 = ((bf16[16,128,128]{2,1,0:T(8,128)(2,1)}), bf16[16,128,128]{2,1,0:T(8,128)(2,1)S(1)}, u32[]{:S(2)}, u32[]{:S(2)}) async-start(bf16[16,128,128]{2,1,0:T(8,128)(2,1)} %pick_rows.1), calls=%async_computation.1 | async-start | bytes 1048576 | tf_op jit(solution)/shard_map/all_to_all | solution.py:546
  49.3 0.8 copy-start.1
  88.3 5.0 %copy-start.4 = (bf16[4,176,512]{2,1,0:T(8,128)(2,1)S(1)}, bf16[4,176,512]{2,1,0:T(8,128)(2,1)}, u32[]{:S(2)}) copy-start(bf16[4,176,512]{2,1,0:T(8,128)(2,1)} %get-tuple-element.28) | copy-start | bytes 2162692
  88.3 3.2 %collective-permute-start.1 = (bf16[4,176,512]{2,1,0:T(8,128)(2,1)}, bf16[4,176,512]{2,1,0:T(8,128)(2,1)S(1)}, u32[]{:S(2)}, u32[]{:S(2)}) collective-permute-start(bf16[4,176,512]{2,1,0:T(8,128)(2,1)} %get-tuple-element.27), channel_id=1, source_target_pairs={{0,1},{1,0},{2,3},{3,2},{4,5},{5,4},{6,7},{7,6},{8,9},{9,8},{10,11... | collective-permute-start | bytes 2162696 | tf_op jit(solution)/shard_map/ppermute | solution.py:427
  89.4 3.9 %collective-permute-start.3 = (bf16[4,176,512]{2,1,0:T(8,128)(2,1)}, bf16[4,176,512]{2,1,0:T(8,128)(2,1)S(1)}, u32[]{:S(2)}, u32[]{:S(2)}) collective-permute-start(bf16[4,176,512]{2,1,0:T(8,128)(2,1)} %get-tuple-element.29), channel_id=1, source_target_pairs={{0,1},{1,0},{2,3},{3,2},{4,5},{5,4},{6,7},{7,6},{8,9},{9,8},{10,11... | collective-permute-start | bytes 2162696 | tf_op jit(solution)/shard_map/ppermute | solution.py:427
  89.5 4.4 %collective-permute-start.5 = (bf16[4,176,512]{2,1,0:T(8,128)(2,1)}, bf16[4,176,512]{2,1,0:T(8,128)(2,1)S(1)}, u32[]{:S(2)}, u32[]{:S(2)}) collective-permute-start(bf16[4,176,512]{2,1,0:T(8,128)(2,1)} %get-tuple-element.31), channel_id=1, source_target_pairs={{0,1},{1,0},{2,3},{3,2},{4,5},{5,4},{6,7},{7,6},{8,9},{9,8},{10,11... | collective-permute-start | bytes 2162696 | tf_op jit(solution)/shard_map/ppermute | solution.py:427
  89.9 6.8 %collective-permute-start = (bf16[4,176,512]{2,1,0:T(8,128)(2,1)}, bf16[4,176,512]{2,1,0:T(8,128)(2,1)S(1)}, u32[]{:S(2)}, u32[]{:S(2)}) collective-permute-start(bf16[4,176,512]{2,1,0:T(8,128)(2,1)} %get-tuple-element.25), channel_id=1, source_target_pairs={{0,1},{1,0},{2,3},{3,2},{4,5},{5,4},{6,7},{7,6},{8,9},{9,8},{10,11... | collective-permute-start | bytes 2162696 | tf_op jit(solution)/shard_map/ppermute | solution.py:427
  92.7 1.1 copy-start.3
  92.7 12.1 %collective-permute-start.2 = (bf16[4,176,512]{2,1,0:T(8,128)(2,1)S(1)}, bf16[4,176,512]{2,1,0:T(8,128)(2,1)S(1)}, u32[]{:S(2)}, u32[]{:S(2)}) collective-permute-start(bf16[4,176,512]{2,1,0:T(8,128)(2,1)S(1)} %add_convert_fusion.3), channel_id=1, source_target_pairs={{0,4},{1,17},{2,6},{3,19},{4,0},{5,21},{6,2},{7,23},{8,12},{9,25},... | collective-permute-start | bytes 2162696 | tf_op jit(solution)/shard_map/ppermute | solution.py:434
  93.5 19.0 %copy-start.5 = (bf16[4,176,512]{2,1,0:T(8,128)(2,1)S(1)}, bf16[4,176,512]{2,1,0:T(8,128)(2,1)}, u32[]{:S(2)}) copy-start(bf16[4,176,512]{2,1,0:T(8,128)(2,1)} %get-tuple-element.24) | copy-start | bytes 2162692
  93.5 19.0 %collective-permute-start.4 = (bf16[4,176,512]{2,1,0:T(8,128)(2,1)S(1)}, bf16[4,176,512]{2,1,0:T(8,128)(2,1)S(1)}, u32[]{:S(2)}, u32[]{:S(2)}) collective-permute-start(bf16[4,176,512]{2,1,0:T(8,128)(2,1)S(1)} %add_convert_fusion.2), channel_id=1, source_target_pairs={{0,2},{1,9},{2,4},{3,11},{4,6},{5,13},{6,0},{7,15},{8,10},{9,17},{... | collective-permute-start | bytes 2162696 | tf_op jit(solution)/shard_map/ppermute | solution.py:434
  94.0 18.4 %collective-permute-start.6 = (bf16[4,176,512]{2,1,0:T(8,128)(2,1)S(1)}, bf16[4,176,512]{2,1,0:T(8,128)(2,1)S(1)}, u32[]{:S(2)}, u32[]{:S(2)}) collective-permute-start(bf16[4,176,512]{2,1,0:T(8,128)(2,1)S(1)} %add_convert_fusion.1), channel_id=1, source_target_pairs={{0,6},{1,25},{2,0},{3,27},{4,2},{5,29},{6,4},{7,31},{8,14},{9,1},{... | collective-permute-start | bytes 2162696 | tf_op jit(solution)/shard_map/ppermute | solution.py:434
  113.0 6.3 %collective-permute-start.7 = (bf16[176,512]{1,0:T(8,128)(2,1)S(1)}, bf16[176,512]{1,0:T(8,128)(2,1)S(1)}, u32[]{:S(2)}, u32[]{:S(2)}) collective-permute-start(bf16[176,512]{1,0:T(8,128)(2,1)S(1)} %get-tuple-element.50), channel_id=1, source_target_pairs={{0,16},{1,5},{2,18},{3,7},{4,20},{5,1},{6,22},{7,3},{8,24},{9,13},... | collective-permute-start | bytes 540680 | tf_op jit(solution)/shard_map/ppermute | solution.py:441
  113.1 7.9 %collective-permute-start.8 = (bf16[176,512]{1,0:T(8,128)(2,1)S(1)}, bf16[176,512]{1,0:T(8,128)(2,1)S(1)}, u32[]{:S(2)}, u32[]{:S(2)}) collective-permute-start(bf16[176,512]{1,0:T(8,128)(2,1)S(1)} %get-tuple-element.52), channel_id=1, source_target_pairs={{0,8},{1,3},{2,10},{3,5},{4,12},{5,7},{6,14},{7,1},{8,16},{9,11},{... | collective-permute-start | bytes 540680 | tf_op jit(solution)/shard_map/ppermute | solution.py:441
  114.6 6.4 %collective-permute-start.9 = (bf16[176,512]{1,0:T(8,128)(2,1)S(1)}, bf16[176,512]{1,0:T(8,128)(2,1)S(1)}, u32[]{:S(2)}, u32[]{:S(2)}) collective-permute-start(bf16[176,512]{1,0:T(8,128)(2,1)S(1)} %get-tuple-element.51), channel_id=1, source_target_pairs={{0,24},{1,7},{2,26},{3,1},{4,28},{5,3},{6,30},{7,5},{8,0},{9,15},{... | collective-permute-start | bytes 540680 | tf_op jit(solution)/shard_map/ppermute | solution.py:441
  121.1 6.0 %collective-permute-start.10 = (bf16[176,512]{1,0:T(8,128)(2,1)S(1)}, bf16[176,512]{1,0:T(8,128)(2,1)S(1)}, u32[]{:S(2)}, u32[]{:S(2)}) collective-permute-start(bf16[176,512]{1,0:T(8,128)(2,1)S(1)} %fusion.1), channel_id=1, source_target_pairs={{0,64},{1,65},{2,66},{3,67},{4,68},{5,69},{6,70},{7,71},{8,72},{9,... | collective-permute-start | bytes 540680 | tf_op jit(solution)/shard_map/ppermute | solution.py:445
  121.7 10.2 %collective-permute-start.11 = (bf16[176,512]{1,0:T(8,128)(2,1)S(1)}, bf16[176,512]{1,0:T(8,128)(2,1)S(1)}, u32[]{:S(2)}, u32[]{:S(2)}) collective-permute-start(bf16[176,512]{1,0:T(8,128)(2,1)S(1)} %fusion.1), channel_id=1, source_target_pairs={{0,32},{1,33},{2,34},{3,35},{4,36},{5,37},{6,38},{7,39},{8,40},{9,... | collective-permute-start | bytes 540680 | tf_op jit(solution)/shard_map/ppermute | solution.py:445
  122.3 9.6 %collective-permute-start.12 = (bf16[176,512]{1,0:T(8,128)(2,1)S(1)}, bf16[176,512]{1,0:T(8,128)(2,1)S(1)}, u32[]{:S(2)}, u32[]{:S(2)}) collective-permute-start(bf16[176,512]{1,0:T(8,128)(2,1)S(1)} %fusion.1), channel_id=1, source_target_pairs={{0,96},{1,97},{2,98},{3,99},{4,100},{5,101},{6,102},{7,103},{8,104... | collective-permute-start | bytes 540680 | tf_op jit(solution)/shard_map/ppermute | solution.py:445
  132.0 4.4 %collective-permute-start.13 = (bf16[176,512]{1,0:T(8,128)(2,1)S(1)}, bf16[176,512]{1,0:T(8,128)(2,1)S(1)}, u32[]{:S(2)}, u32[]{:S(2)}) collective-permute-start(bf16[176,512]{1,0:T(8,128)(2,1)S(1)} %add_convert_fusion.5), channel_id=1, source_target_pairs={{0,24},{1,7},{2,26},{3,1},{4,28},{5,3},{6,30},{7,5},{8,0},{9,15},{... | collective-permute-start | bytes 540680 | tf_op jit(solution)/shard_map/ppermute | solution.py:441
  133.4 6.2 %collective-permute-start.14 = (bf16[176,512]{1,0:T(8,128)(2,1)S(1)}, bf16[176,512]{1,0:T(8,128)(2,1)S(1)}, u32[]{:S(2)}, u32[]{:S(2)}) collective-permute-start(bf16[176,512]{1,0:T(8,128)(2,1)S(1)} %add_convert_fusion.5), channel_id=1, source_target_pairs={{0,16},{1,5},{2,18},{3,7},{4,20},{5,1},{6,22},{7,3},{8,24},{9,13},... | collective-permute-start | bytes 540680 | tf_op jit(solution)/shard_map/ppermute | solution.py:441
  134.0 7.5 %collective-permute-start.15 = (bf16[176,512]{1,0:T(8,128)(2,1)S(1)}, bf16[176,512]{1,0:T(8,128)(2,1)S(1)}, u32[]{:S(2)}, u32[]{:S(2)}) collective-permute-start(bf16[176,512]{1,0:T(8,128)(2,1)S(1)} %add_convert_fusion.5), channel_id=1, source_target_pairs={{0,8},{1,3},{2,10},{3,5},{4,12},{5,7},{6,14},{7,1},{8,16},{9,11},{... | collective-permute-start | bytes 540680 | tf_op jit(solution)/shard_map/ppermute | solution.py:441
  141.5 70.3 %copy-start = (bf16[4,176,512]{2,1,0:T(8,128)(2,1)}, bf16[4,176,512]{2,1,0:T(8,128)(2,1)S(1)}, u32[]{:S(2)}) copy-start(bf16[4,176,512]{2,1,0:T(8,128)(2,1)S(1)} %pad_maximum_fusion.refs_0_) | copy-start | bytes 2162692
  141.6 10.5 %collective-permute-start.16 = (bf16[4,176,512]{2,1,0:T(8,128)(2,1)S(1)}, bf16[4,176,512]{2,1,0:T(8,128)(2,1)S(1)}, u32[]{:S(2)}, u32[]{:S(2)}) collective-permute-start(bf16[4,176,512]{2,1,0:T(8,128)(2,1)S(1)} %pad_maximum_fusion.refs_0_), channel_id=1, source_target_pairs={{0,6},{1,25},{2,0},{3,27},{4,2},{5,29},{6,4},{7,31},{8,14},{9,1},{... | collective-permute-start | bytes 2162696 | tf_op jit(solution)/shard_map/ppermute | solution.py:434
  141.6 13.6 %collective-permute-start.17 = (bf16[4,176,512]{2,1,0:T(8,128)(2,1)S(1)}, bf16[4,176,512]{2,1,0:T(8,128)(2,1)S(1)}, u32[]{:S(2)}, u32[]{:S(2)}) collective-permute-start(bf16[4,176,512]{2,1,0:T(8,128)(2,1)S(1)} %pad_maximum_fusion.refs_0_), channel_id=1, source_target_pairs={{0,4},{1,17},{2,6},{3,19},{4,0},{5,21},{6,2},{7,23},{8,12},{9,25},... | collective-permute-start | bytes 2162696 | tf_op jit(solution)/shard_map/ppermute | solution.py:434
  143.1 18.3 %collective-permute-start.18 = (bf16[4,176,512]{2,1,0:T(8,128)(2,1)S(1)}, bf16[4,176,512]{2,1,0:T(8,128)(2,1)S(1)}, u32[]{:S(2)}, u32[]{:S(2)}) collective-permute-start(bf16[4,176,512]{2,1,0:T(8,128)(2,1)S(1)} %pad_maximum_fusion.refs_0_), channel_id=1, source_target_pairs={{0,2},{1,9},{2,4},{3,11},{4,6},{5,13},{6,0},{7,15},{8,10},{9,17},{... | collective-permute-start | bytes 2162696 | tf_op jit(solution)/shard_map/ppermute | solution.py:434
  143.1 23.8 %all-to-all-start.3 = ((bf16[8,128,128]{2,1,0:T(8,128)(2,1)}), bf16[8,128,128]{2,1,0:T(8,128)(2,1)S(1)}, u32[]{:S(2)}, u32[]{:S(2)}) async-start(bf16[8,128,128]{2,1,0:T(8,128)(2,1)} %get-tuple-element.23), calls=%async_computation.3 | async-start | bytes 524288 | tf_op jit(solution)/shard_map/all_to_all | solution.py:552
  150.8 61.1 %collective-permute-start.19 = (bf16[4,176,512]{2,1,0:T(8,128)(2,1)S(1)}, bf16[4,176,512]{2,1,0:T(8,128)(2,1)}, u32[]{:S(2)}, u32[]{:S(2)}) collective-permute-start(bf16[4,176,512]{2,1,0:T(8,128)(2,1)S(1)} %pad_maximum_fusion.refs_0_), channel_id=1, source_target_pairs={{0,1},{1,0},{2,3},{3,2},{4,5},{5,4},{6,7},{7,6},{8,9},{9,8},{10,11... | collective-permute-start | bytes 2162696 | tf_op jit(solution)/shard_map/ppermute | solution.py:427
  152.1 59.8 %copy-start.6 = (bf16[4,176,512]{2,1,0:T(8,128)(2,1)}, bf16[4,176,512]{2,1,0:T(8,128)(2,1)S(1)}, u32[]{:S(2)}) copy-start(bf16[4,176,512]{2,1,0:T(8,128)(2,1)S(1)} %collective-permute-done.16.refs_1_) | copy-start | bytes 2162692
  152.1 59.8 %collective-permute-start.20 = (bf16[4,176,512]{2,1,0:T(8,128)(2,1)S(1)}, bf16[4,176,512]{2,1,0:T(8,128)(2,1)}, u32[]{:S(2)}, u32[]{:S(2)}) collective-permute-start(bf16[4,176,512]{2,1,0:T(8,128)(2,1)S(1)} %collective-permute-done.16.refs_1_), channel_id=1, source_target_pairs={{0,1},{1,0},{2,3},{3,2},{4,5},{5,4},{6,7},{7,6},{8,9},{9,8},{10,11... | collective-permute-start | bytes 2162696 | tf_op jit(solution)/shard_map/ppermute | solution.py:427
  155.2 56.7 %copy-start.7 = (bf16[4,176,512]{2,1,0:T(8,128)(2,1)}, bf16[4,176,512]{2,1,0:T(8,128)(2,1)S(1)}, u32[]{:S(2)}) copy-start(bf16[4,176,512]{2,1,0:T(8,128)(2,1)S(1)} %collective-permute-done.17.refs_2_) | copy-start | bytes 2162692
  155.2 56.7 %collective-permute-start.21 = (bf16[4,176,512]{2,1,0:T(8,128)(2,1)S(1)}, bf16[4,176,512]{2,1,0:T(8,128)(2,1)}, u32[]{:S(2)}, u32[]{:S(2)}) collective-permute-start(bf16[4,176,512]{2,1,0:T(8,128)(2,1)S(1)} %collective-permute-done.17.refs_2_), channel_id=1, source_target_pairs={{0,1},{1,0},{2,3},{3,2},{4,5},{5,4},{6,7},{7,6},{8,9},{9,8},{10,11... | collective-permute-start | bytes 2162696 | tf_op jit(solution)/shard_map/ppermute | solution.py:427
  161.4 50.5 %copy-start.8 = (bf16[4,176,512]{2,1,0:T(8,128)(2,1)}, bf16[4,176,512]{2,1,0:T(8,128)(2,1)S(1)}, u32[]{:S(2)}) copy-start(bf16[4,176,512]{2,1,0:T(8,128)(2,1)S(1)} %collective-permute-done.18.refs_3_) | copy-start | bytes 2162692
  161.4 50.5 %collective-permute-start.22 = (bf16[4,176,512]{2,1,0:T(8,128)(2,1)S(1)}, bf16[4,176,512]{2,1,0:T(8,128)(2,1)}, u32[]{:S(2)}, u32[]{:S(2)}) collective-permute-start(bf16[4,176,512]{2,1,0:T(8,128)(2,1)S(1)} %collective-permute-done.18.refs_3_), channel_id=1, source_target_pairs={{0,1},{1,0},{2,3},{3,2},{4,5},{5,4},{6,7},{7,6},{8,9},{9,8},{10,11... | collective-permute-start | bytes 2162696 | tf_op jit(solution)/shard_map/ppermute | solution.py:427
  166.9 0.7 copy-start.2

commit v2 on v1

--- a/solution.py
+++ b/solution.py
@@ -1,3 +1,5 @@
+import functools
+
 import jax
 import jax.numpy as jnp
 from jax import lax
@@ -31,6 +33,12 @@
 
 def params(**more):
     return pltpu.CompilerParams(vmem_limit_bytes=VMEM_LIMIT, **more)
+
+
+def cost(microseconds):
+    return pl.CostEstimate(
+        flops=int(microseconds * 1.1e9), bytes_accessed=int(microseconds * 3.6e6), transcendentals=0
+    )
 
 
 def vmem(count):
@@ -70,26 +78,30 @@
         place = jnp.where(
             regular[:, span], owner[:, span] * CAP + slot, SLOTS + hot_ref[:, span]
         )
-        index_ref[block : block + 1, :] = place
+        index_ref[block, 0:1, :] = place[:, :128]
+        index_ref[block, 1:2, :] = place[:, 128:]
         slots = lax.broadcasted_iota(I32, (CAP, TOK), 0)
         pick = jnp.where(slots == slot, 1.0, 0.0).astype(BF16)
         parts = jnp.concatenate([here * high[:, span], here * low[:, span], here], axis=0)
         requests += mm(parts.astype(BF16), pick, NT)
     rows = requests[:N_SEQ] * 64.0 + requests[N_SEQ : 2 * N_SEQ]
     rows = jnp.where(requests[2 * N_SEQ :] > 0.5, rows, float(ITEMS_DEV))
-    request_ref[...] = rows.astype(I32)
+    rows = rows.astype(I32)
+    request_ref[:, 0, :] = rows[:, :128]
+    request_ref[:, 1, :] = rows[:, 128:]
 
 
 def make_slots(owner, item, flag, hot):
     return pl.pallas_call(
         slot_kernel,
         out_shape=(
-            jax.ShapeDtypeStruct((N_SEQ, CAP), I32),
-            jax.ShapeDtypeStruct((N_COL, TOK), I32),
+            jax.ShapeDtypeStruct((N_SEQ, 2, 128), I32),
+            jax.ShapeDtypeStruct((N_COL, 2, 128), I32),
         ),
         in_specs=vmem(4),
         out_specs=tuple(vmem(2)),
         compiler_params=params(),
+        cost_estimate=cost(2.5),
         name="slots",
     )(owner, item, flag, hot)
 
@@ -103,7 +115,7 @@
     return jnp.concatenate([rows[:128], rows[128:]], axis=1).astype(BF16)
 
 
-def copy_rows(count, unroll, body):
+def each_row(count, body, unroll=32):
     def step(i, carry):
         for u in range(unroll):
             body(i * unroll + u)
@@ -113,13 +125,12 @@
 
 
 def pick_kernel(request_ref, table_ref, out_ref, rows):
+    def one(slot):
+        row = jnp.minimum(request_ref[slot], ITEMS_DEV - 1)
+        rows[pl.ds(slot, 1), :] = table_ref[pl.ds(row, 1), :]
+
+    each_row(SLOTS, one)
     for requester in range(N_SEQ):
-
-        def one(slot):
-            row = jnp.minimum(request_ref[requester, slot], ITEMS_DEV - 1)
-            rows[pl.ds(requester * CAP + slot, 1), :] = table_ref[pl.ds(row, 1), :]
-
-        copy_rows(CAP, 16, one)
         out_ref[requester] = narrow(rows[requester * CAP : (requester + 1) * CAP, :])
 
 
@@ -131,8 +142,9 @@
         out_specs=vmem(1)[0],
         scratch_shapes=[pltpu.VMEM((SLOTS, COLS), F32)],
         compiler_params=params(),
+        cost_estimate=cost(7),
         name="pick_rows",
-    )(requests, table)
+    )(requests.reshape(SLOTS), table)
 
 
 def place_kernel(index_ref, returned_ref, hot_ref, out_ref, source, rows):
@@ -140,14 +152,14 @@
         first, second = widen(returned_ref[owner])
         source[owner * CAP : owner * CAP + 128, :] = first
         source[owner * CAP + 128 : (owner + 1) * CAP, :] = second
-    source[SLOTS : SLOTS + HOT, :] = hot_ref[...].astype(F32)
+    source[SLOTS : SLOTS + HOT, :] = hot_ref[...].astype(F32).T
+
+    def one(token):
+        rows[pl.ds(token, 1), :] = source[pl.ds(index_ref[token], 1), :]
+
+    each_row(SEQ_TOK, one)
     for block in range(N_COL):
-
-        def one(token):
-            rows[pl.ds(token, 1), :] = source[pl.ds(index_ref[block, token], 1), :]
-
-        copy_rows(TOK, 16, one)
-        out_ref[block] = narrow(rows[...])
+        out_ref[block] = narrow(rows[block * TOK : (block + 1) * TOK, :])
 
 
 def place_rows(index, returned, hot_table):
@@ -156,24 +168,24 @@
         out_shape=jax.ShapeDtypeStruct((N_COL, 128, 128), BF16),
         in_specs=[SMEM] + vmem(2),
         out_specs=vmem(1)[0],
-        scratch_shapes=[pltpu.VMEM((SLOTS + HOT, COLS), F32), pltpu.VMEM((TOK, COLS), F32)],
+        scratch_shapes=[pltpu.VMEM((SLOTS + HOT, COLS), F32), pltpu.VMEM((SEQ_TOK, COLS), F32)],
         compiler_params=params(),
+        cost_estimate=cost(4),
         name="place_rows",
-    )(index, returned, hot_table)
+    )(index.reshape(SEQ_TOK), returned, hot_table.T)
 
 
 def return_kernel(index_ref, grad_ref, out_ref, rows, target):
     target[...] = jnp.zeros_like(target)
     for block in range(N_COL):
         first, second = widen(grad_ref[block])
-        rows[block, :128, :] = first
-        rows[block, 128:, :] = second
-    for block in range(N_COL):
-
-        def one(token):
-            target[pl.ds(index_ref[block, token], 1), :] = rows[block, pl.ds(token, 1), :]
-
-        copy_rows(TOK, 16, one)
+        rows[block * TOK : block * TOK + 128, :] = first
+        rows[block * TOK + 128 : (block + 1) * TOK, :] = second
+
+    def one(token):
+        target[pl.ds(index_ref[token], 1), :] = rows[pl.ds(token, 1), :]
+
+    each_row(SEQ_TOK, one)
     for owner in range(N_SEQ):
         out_ref[owner] = narrow(target[owner * CAP : (owner + 1) * CAP, :])
 
@@ -185,12 +197,13 @@
         in_specs=[SMEM] + vmem(1),
         out_specs=vmem(1)[0],
         scratch_shapes=[
-            pltpu.VMEM((N_COL, TOK, COLS), F32),
+            pltpu.VMEM((SEQ_TOK, COLS), F32),
             pltpu.VMEM((SLOTS + HOT, COLS), F32),
         ],
         compiler_params=params(),
+        cost_estimate=cost(4),
         name="return_rows",
-    )(index, grads)
+    )(index.reshape(SEQ_TOK), grads)
 
 
 def scatter_kernel(request_ref, incoming_ref, out_ref, rows, *totals):
@@ -201,17 +214,15 @@
         rows[requester * CAP : requester * CAP + 128, :] = first
         rows[requester * CAP + 128 : (requester + 1) * CAP, :] = second
     part = SLOTS // len(totals)
-    per = N_SEQ // len(totals)
 
     def step(i, carry):
-        for u in range(4):
+        for u in range(8):
             for t, total in enumerate(totals):
-                slot = i * 4 + u
-                row = request_ref[t * per + slot // CAP, slot % CAP]
-                total[pl.ds(row, 1), :] += rows[pl.ds(t * part + slot, 1), :]
+                slot = t * part + i * 8 + u
+                total[pl.ds(request_ref[slot], 1), :] += rows[pl.ds(slot, 1), :]
         return carry
 
-    lax.fori_loop(0, part // 4, step, 0)
+    lax.fori_loop(0, part // 8, step, 0)
     for block in range(ITEMS_DEV // 128):
         span = slice(block * 128, (block + 1) * 128)
         value = totals[0][span, :]
@@ -229,9 +240,9 @@
         scratch_shapes=[pltpu.VMEM((SLOTS, COLS), F32)]
         + [pltpu.VMEM((ITEMS_DEV + 8, COLS), F32)] * 4,
         compiler_params=params(),
-        cost_estimate=pl.CostEstimate(flops=0, bytes_accessed=20_000_000, transcendentals=0),
+        cost_estimate=cost(11),
         name="scatter_rows",
-    )(requests, incoming).T
+    )(requests.reshape(SLOTS), incoming).T
 
 
 def norm(value):
@@ -253,18 +264,42 @@
 
 def places():
     seq, col = lax.axis_index("seq"), lax.axis_index("col")
-    y, x, core = seq & 3, col >> 1, col & 1
-    return x, y, core
+    return (col >> 1, seq & 3, seq >> 2), col & 1
 
 
 def stack_kernel(
-    index_ref, emb_ref, win_ref, wout_ref, segment_ref, cot_ref,
+    index_ref, emb_ref, segment_ref, cot_ref, win_hbm, wout_hbm,
     enc_ref, grad_ref, *refs
 ):
     outs, refs = refs[:8], refs[8:]
-    stream, normed, normed_scale, proj, slope, attn, attn_slope, mixed, mixed_scale, gated, dproj, pay, sems = refs
+    stream, normed, normed_scale, proj, slope, attn, attn_slope, mixed, mixed_scale, gated, dproj, pay, win_ref, wout_ref, sems, win_sems, wout_sems = refs
     keep, send = outs[:4], outs[4:]
-    x, y, core = places()
+    loads = {}
+    for l in range(LAYERS):
+        for part in range(4):
+            span = slice(part * D, (part + 1) * D)
+            loads[l, part] = pltpu.make_async_copy(
+                win_hbm.at[l, :, span], win_ref.at[l, :, span], win_sems.at[l, part]
+            )
+        loads[l, 4] = pltpu.make_async_copy(wout_hbm.at[l], wout_ref.at[l], wout_sems.at[l])
+    for l in range(LAYERS):
+        for part in range(5):
+            loads[l, part].start()
+    (x, y, z), core = places()
+
+    def leave(l, part, act):
+        span = slice(part * 32, min(part * 32 + 32, CHUNK))
+
+        def each(targets):
+            for a in range(4):
+                copy = pltpu.make_async_copy(
+                    pay.at[l, 4 * a : 4 * a + 4, span], targets[a].at[:, span], sems.at[l, part, a]
+                )
+                getattr(copy, act)()
+
+        pl.when(core == l)(lambda: each(keep))
+        pl.when(core != l)(lambda: each(send))
+
     col = lax.axis_index("col")
 
     segment = jnp.broadcast_to(segment_ref[...].astype(F32), (TOK, TOK))
@@ -289,6 +324,7 @@
         normed_scale[l] = scale
         rounded = value.astype(BF16)
         for part in range(4):
+            loads[l, part].wait()
             pre = mm(rounded, win_ref[l, :, part * D : (part + 1) * D])
             out, tilt = silu_parts(pre)
             proj[l, part] = out.astype(BF16)
@@ -306,12 +342,13 @@
         mixed_scale[l] = scale
         product = (value * proj[l, 0].astype(F32)).astype(BF16)
         gated[l] = product
+        loads[l, 4].wait()
         stream[...] += mm(product, wout_ref[l])
     enc_ref[...] = stream[...].astype(BF16)
 
     stream[...] = cot_ref[...].astype(F32)
     for l in reversed(range(LAYERS)):
-        first, second = (x, y) if l == 0 else (y, x)
+        first, second = (x, y) if l == 0 else (y, z)
 
         def put(part, value):
             for a in range(4):
@@ -319,6 +356,7 @@
                     chunk = 4 * a + b
                     place = 4 * ((a - first) & 3) + ((b - second) & 3)
                     pay[l, place, part * 32 : (part + 1) * 32, :] = value[chunk * 32 : (chunk + 1) * 32, :]
+            leave(l, part, "start")
 
         grad = stream[...]
         grad_b = grad.astype(BF16)
@@ -354,26 +392,20 @@
         bottom = grad[128:, pair * 128 : (pair + 1) * 128]
         grad_ref[2 * pair] = jnp.concatenate([top[:, :COLS], bottom[:, :COLS]], axis=1).astype(BF16)
         grad_ref[2 * pair + 1] = jnp.concatenate([top[:, COLS:], bottom[:, COLS:]], axis=1).astype(BF16)
-    hot_row = index_ref[pl.ds(col, 1), :] - SLOTS
+    hot_row = jnp.concatenate([index_ref[col, 0:1, :], index_ref[col, 1:2, :]], axis=1) - SLOTS
     pick = jnp.where(lax.broadcasted_iota(I32, (HOT, TOK), 0) == hot_row, 1.0, 0.0).astype(BF16)
     hot_part = mm(pick, grad.astype(BF16)).astype(BF16)
     for l in range(LAYERS):
-        first, second = (x, y) if l == 0 else (y, x)
+        first, second = (x, y) if l == 0 else (y, z)
         for a in range(4):
             for b in range(4):
                 chunk = 4 * a + b
                 place = 4 * ((a - first) & 3) + ((b - second) & 3)
                 pay[l, place, 160:CHUNK, :] = hot_part[chunk * 16 : (chunk + 1) * 16, :]
-    copies = []
-    for a in range(4):
-        for i, (outs_here, layer) in enumerate(((send, 1 - core), (keep, core))):
-            copies.append(
-                pltpu.make_async_copy(pay.at[layer, pl.ds(4 * a, 4)], outs_here[a], sems.at[i, a])
-            )
-    for copy in copies:
-        copy.start()
-    for copy in copies:
-        copy.wait()
+        leave(l, 5, "start")
+    for l in range(LAYERS):
+        for part in range(6):
+            leave(l, part, "wait")
 
 
 def run_stack(index, emb, weight_in, weight_out, segment, cotangent):
@@ -385,7 +417,7 @@
             jax.ShapeDtypeStruct((N_COL, 128, 128), BF16),
         )
         + (piece,) * 8,
-        in_specs=vmem(6),
+        in_specs=vmem(4) + [ANY] * 2,
         out_specs=tuple(vmem(2)) + (ANY,) * 8,
         scratch_shapes=[
             pltpu.VMEM((TOK, D), F32),
@@ -400,11 +432,16 @@
             pltpu.VMEM((LAYERS, TOK, D), BF16),
             pltpu.VMEM((4, TOK, D), BF16),
             pltpu.VMEM((LAYERS, 16, CHUNK, D), BF16),
-            pltpu.SemaphoreType.DMA((2, 4)),
+            pltpu.VMEM((LAYERS, D, 4 * D), BF16),
+            pltpu.VMEM((LAYERS, D, D), BF16),
+            pltpu.SemaphoreType.DMA((LAYERS, 6, 4)),
+            pltpu.SemaphoreType.DMA((LAYERS, 4)),
+            pltpu.SemaphoreType.DMA((LAYERS,)),
         ],
         compiler_params=params(),
+        cost_estimate=cost(16),
         name="layers",
-    )(index, emb, weight_in, weight_out, segment, cotangent)
+    )(index, emb, segment, cotangent, weight_in, weight_out)
 
 
 def device_pairs(move):
@@ -427,22 +464,14 @@
     return lax.ppermute(value, BOTH, device_pairs(lambda z, y, x, c: (z, y, x, 1 - c)))
 
 
-def along_first(value, k):
+def along(value, stage, k):
     def move(z, y, x, c):
-        return (z, y, (x + k) % 4, c) if c == 0 else (z, (y + k) % 4, x, c)
+        place = [x, y, z]
+        axis = (stage + c) % 3
+        place[axis] = (place[axis] + k) % 4
+        return (place[2], place[1], place[0], c)
 
     return lax.ppermute(value, BOTH, device_pairs(move))
-
-
-def along_second(value, k):
-    def move(z, y, x, c):
-        return (z, (y + k) % 4, x, c) if c == 0 else (z, y, (x + k) % 4, c)
-
-    return lax.ppermute(value, BOTH, device_pairs(move))
-
-
-def along_z(value, k):
-    return lax.ppermute(value, BOTH, device_pairs(lambda z, y, x, c: ((z + k) % 4, y, x, c)))
 
 
 def add_all(*terms):
@@ -452,86 +481,89 @@
     return terms[0].astype(BF16)
 
 
-def sum_everywhere(keep, send):
+def sum_everywhere(keep, send, gather_columns, send_back, exchange, scatter):
     order = (1, 3, 2, 0)
     got = {k: to_core(send[k]) for k in order}
     chip = {k: add_all(keep[k], got[k]) for k in order}
-    came = {k: along_first(chip[k], k) for k in (1, 3, 2)}
+    came = {k: along(chip[k], 0, k) for k in (1, 3, 2)}
     line = add_all(chip[0], came[2], came[1], came[3])
-    came = {k: along_second(line[k], k) for k in (1, 3, 2)}
+    line, columns = lax.optimization_barrier((line, gather_columns()))
+    outgoing = send_back(columns)
+    came = {k: along(line[k], 1, k) for k in (1, 3, 2)}
     plane = add_all(line[0], came[2], came[1], came[3])
-    came = {k: along_z(plane, k) for k in (1, 3, 2)}
+    came = {k: along(plane, 2, k) for k in (1, 3, 2)}
     total = add_all(plane, came[2], came[1], came[3])
-    row = jnp.stack([total] + [along_second(total, -k) for k in (1, 2, 3)])
-    mine = [row] + [along_first(row, -k) for k in (1, 2, 3)]
-    other = [to_core(value) for value in mine]
-    return mine, other
-
-
-def finish_kernel(*refs):
-    mine, other = refs[:4], refs[4:8]
-    win_ref, wout_ref, hot_ref = refs[8:11]
-    stage_in, stage_out, hot_rows, sems = refs[11:]
-    x, y, core = places()
-    col = lax.axis_index("col")
-    pending = [None, None]
-    step = 0
-    for source, layer, own in ((mine, core, True), (other, 1 - core, False)):
-        straight = layer == 0
-        first = jnp.where(straight, x, y)
-        second = jnp.where(straight, y, x)
-        for a in range(4):
-            for b in range(4):
-                slot = step % 2
-                if pending[slot] is not None:
-                    for copy in pending[slot]:
-                        copy.wait()
-                chunk = 4 * ((a + first) & 3) + ((b + second) & 3)
-                for part in range(4):
-                    stage_in[slot, :, part * D : (part + 1) * D] = source[a][
-                        b, part * 32 : (part + 1) * 32, :
-                    ].astype(F32)
-                stage_out[slot] = source[a][b, 128:160, :].astype(F32)
-                if own:
-                    hot_rows[pl.ds(pl.multiple_of(chunk * 16, 16), 16), :] = source[a][b, 160:CHUNK, :]
-                rows = pl.ds(pl.multiple_of(chunk * 32, 32), 32)
-                pending[slot] = [
-                    pltpu.make_async_copy(stage_in.at[slot], win_ref.at[layer, rows], sems.at[slot, 0]),
-                    pltpu.make_async_copy(stage_out.at[slot], wout_ref.at[layer, rows], sems.at[slot, 1]),
-                ]
-                for copy in pending[slot]:
-                    copy.start()
-                step += 1
-    pick = jnp.where(
-        lax.broadcasted_iota(I32, (D, COLS), 0) == lax.broadcasted_iota(I32, (D, COLS), 1) + col * COLS,
-        1.0,
-        0.0,
-    ).astype(BF16)
-    hot_ref[...] = mm(hot_rows[...], pick)
-    for copies in pending:
-        for copy in copies:
-            copy.wait()
-
-
-def finish(mine, other):
+    row = jnp.stack([total] + [along(total, 1, -k) for k in (1, 2, 3)])
+    row, incoming = lax.optimization_barrier((row, exchange(outgoing)))
+    mine = [row] + [along(row, 0, -k) for k in (1, 2, 3)]
+    table_grad = scatter(incoming)
+    last, table_grad = lax.optimization_barrier((mine[2], table_grad))
+    other = [to_core(value) for value in (mine[0], mine[1], last, mine[3])]
+    return mine, other, table_grad
+
+
+def finish_kernel(own, *refs):
+    sources = refs[:4]
+    if own:
+        win_ref, wout_ref, hot_ref, stage_in, stage_out, hot_rows, sems = refs[4:]
+    else:
+        win_ref, wout_ref, stage_in, stage_out, sems = refs[6:]
+    (x, y, z), core = places()
+    layer = core if own else 1 - core
+    first = jnp.where(layer == 0, x, y)
+    second = jnp.where(layer == 0, y, z)
+    copies = []
+    for a in range(4):
+        for b in range(4):
+            chunk = 4 * ((a + first) & 3) + ((b + second) & 3)
+            step = 4 * a + b
+            for part in range(4):
+                stage_in[step, :, part * D : (part + 1) * D] = sources[a][
+                    b, part * 32 : (part + 1) * 32, :
+                ].astype(F32)
+            stage_out[step] = sources[a][b, 128:160, :].astype(F32)
+            if own:
+                hot_rows[pl.ds(pl.multiple_of(chunk * 16, 16), 16), :] = sources[a][b, 160:CHUNK, :]
+            rows = pl.ds(pl.multiple_of(chunk * 32, 32), 32)
+            here = [
+                pltpu.make_async_copy(stage_in.at[step], win_ref.at[layer, rows], sems.at[step, 0]),
+                pltpu.make_async_copy(stage_out.at[step], wout_ref.at[layer, rows], sems.at[step, 1]),
+            ]
+            for copy in here:
+                copy.start()
+            copies += here
+    if own:
+        col = lax.axis_index("col")
+        pick = jnp.where(
+            lax.broadcasted_iota(I32, (COLS, D), 1) == lax.broadcasted_iota(I32, (COLS, D), 0) + col * COLS,
+            1.0,
+            0.0,
+        ).astype(BF16)
+        hot_ref[...] = mm(pick, hot_rows[...], NT)
+    for copy in copies:
+        copy.wait()
+
+
+def finish(own, sources, *partial):
+    shapes = (
+        jax.ShapeDtypeStruct((LAYERS, D, 4 * D), F32),
+        jax.ShapeDtypeStruct((LAYERS, D, D), F32),
+    )
+    scratch = [pltpu.VMEM((16, 32, 4 * D), F32), pltpu.VMEM((16, 32, D), F32)]
+    if own:
+        shapes += (jax.ShapeDtypeStruct((COLS, HOT), F32),)
+        scratch += [pltpu.VMEM((HOT, D), BF16)]
     return pl.pallas_call(
-        finish_kernel,
-        out_shape=(
-            jax.ShapeDtypeStruct((LAYERS, D, 4 * D), F32),
-            jax.ShapeDtypeStruct((LAYERS, D, D), F32),
-            jax.ShapeDtypeStruct((HOT, COLS), F32),
-        ),
-        in_specs=vmem(8),
-        out_specs=(ANY, ANY, vmem(1)[0]),
-        scratch_shapes=[
-            pltpu.VMEM((2, 32, 4 * D), F32),
-            pltpu.VMEM((2, 32, D), F32),
-            pltpu.VMEM((HOT, D), BF16),
-            pltpu.SemaphoreType.DMA((2, 2)),
-        ],
+        functools.partial(finish_kernel, own),
+        out_shape=shapes,
+        in_specs=vmem(4) + [ANY] * len(partial),
+        out_specs=(ANY, ANY) + tuple(vmem(1) if own else ()),
+        scratch_shapes=scratch + [pltpu.SemaphoreType.DMA((16, 2))],
+        input_output_aliases={} if own else {4: 0, 5: 1},
         compiler_params=params(),
-        name="finish",
-    )(*mine, *other)
+        cost_estimate=cost(4),
+        name="finish_own" if own else "finish_other",
+    )(*sources, *partial)
 
 
 def on_device(
@@ -548,13 +580,25 @@
     emb = lax.all_to_all(placed, "col", split_axis=0, concat_axis=0, tiled=True)
     outs = run_stack(index, emb, weight_in, weight_out, segment, cotangent)
     encoded, grad_emb, keep, send = outs[0], outs[1], outs[2:6], outs[6:10]
-    mine, other = sum_everywhere(keep, send)
-    grad_columns = lax.all_to_all(grad_emb, "col", split_axis=0, concat_axis=0, tiled=True)
-    outgoing = return_rows(index, grad_columns)
-    incoming = lax.all_to_all(outgoing, "seq", split_axis=0, concat_axis=0, tiled=True)
-    table_grad = scatter_rows(received, incoming)
-    grad_in, grad_out, hot_grad = finish(mine, other)
-    return (encoded, table_grad, hot_grad, grad_in, grad_out)
+
+    def gather_columns():
+        return lax.all_to_all(grad_emb, "col", split_axis=0, concat_axis=0, tiled=True)
+
+    def send_back(columns):
+        return return_rows(index, columns)
+
+    def exchange(outgoing):
+        return lax.all_to_all(outgoing, "seq", split_axis=0, concat_axis=0, tiled=True)
+
+    def scatter(incoming):
+        return scatter_rows(received, incoming)
+
+    mine, other, table_grad = sum_everywhere(
+        keep, send, gather_columns, send_back, exchange, scatter
+    )
+    grad_in, grad_out, hot_grad = finish(True, mine)
+    grad_in, grad_out = finish(False, other, grad_in, grad_out)
+    return (encoded, table_grad, hot_grad.T, grad_in, grad_out)
 
 
 def solution(mesh):

time: 230 us -> 171 us (0.74)
  Pallas kernels: 87.5 us -> 54.2 us
  waiting for transfers between devices: 53.9 us -> 41 us
  starting transfers between devices: 46.7 us -> 37.9 us
  local copies, waits for them, and re-layouts: 8.57 us -> 4.18 us
    pallas_call x1, Pallas kernels: 22.5 us -> 9.38 us  [scatter_rows(): pl.pallas_call(scatter_kernel, out_shape=jax.ShapeDtypeStruct((COLS, ITEM...]
    all_to_all x2, waiting for transfers between devices: 9.13 us -> 0.69 us  [the longest x1 0.68 us: gather_columns(): lax.all_to_all(grad_emb, 'col', split_axis=0, concat_axis=0, tiled=True)]
    pallas_call x1, Pallas kernels: 16.2 us -> 8.79 us  [pick_rows(): pl.pallas_call(pick_kernel, out_shape=jax.ShapeDtypeStruct((N_SEQ, 128, 1...]
    ppermute x8, starting transfers between devices: 13.6 us -> 6.4 us  [to_core(): lax.ppermute(value, BOTH, device_pairs(lambda z, y, x, c: (z, y, x, 1 - c)))]
    ppermute x15, waiting for transfers between devices: 39.6 us -> 33.5 us  [along(): return lax.ppermute(value, BOTH, device_pairs(move))]
    pallas_call x2 -> x3, Pallas kernels: 17.6 us -> 11.9 us  [the longest x2 9.39 us: finish(): pl.pallas_call(functools.partial(finish_kernel, own), out_shape=shapes, i...]
    all_to_all x2, starting transfers between devices: 11.3 us -> 7.82 us  [the longest x1 4.25 us: gather_columns(): lax.all_to_all(grad_emb, 'col', split_axis=0, concat_axis=0, tiled=True)]
    pallas_call x1, Pallas kernels: 7.5 us -> 4.06 us  [place_rows(): pl.pallas_call(place_kernel, out_shape=jax.ShapeDtypeStruct((N_COL, 128,...]
  transfers between devices with their start and end apart: 26 -> 26, of which waited for: 15 -> 14; matrix products, arithmetic and copies ran while one was open for 2% -> 3% of each run, Pallas kernels for 13% -> 11%
where the time goes in v2:
time: 171 us; the launch traced here: 170 us
  Pallas kernels  54.2 us (32%)
  waiting for transfers between devices  41 us (24%)
  starting transfers between devices  37.9 us (22%)
  blocking collectives  27.7 us (16%)
  other arithmetic  4.2 us (2%)
  local copies, waits for them, and re-layouts  4.18 us (2%)
    ppermute x15, waiting for transfers between devices, along(): return lax.ppermute(value, BOTH, device_pairs(move))  33.5 us
    pallas_call x1, Pallas kernels, run_stack(): pl.pallas_call(stack_kernel, out_shape=(jax.ShapeDtypeStruct((TOK, D), BF...  16 us
    ppermute x15, starting transfers between devices, along(): return lax.ppermute(value, BOTH, device_pairs(move))  15.1 us
    all_to_all x1, blocking collectives, on_device(): emb = lax.all_to_all(placed, 'col', split_axis=0, concat_axis=0, tiled=True)  13.9 us
    all_to_all x1, blocking collectives, on_device(): lax.all_to_all(picked, 'seq', split_axis=0, concat_axis=0, tiled=True)  13.7 us
    pallas_call x2, Pallas kernels, finish(): pl.pallas_call(functools.partial(finish_kernel, own), out_shape=shapes, i...  9.39 us
    pallas_call x1, Pallas kernels, scatter_rows(): pl.pallas_call(scatter_kernel, out_shape=jax.ShapeDtypeStruct((COLS, ITEM...  9.38 us
    pallas_call x1, Pallas kernels, pick_rows(): pl.pallas_call(pick_kernel, out_shape=jax.ShapeDtypeStruct((N_SEQ, 128, 1...  8.79 us
  transfers between devices with their start and end apart: 26, of which 14 were waited for; matrix products, arithmetic and copies ran while one was open for 3% of the time, Pallas kernels for 11%

profile of v2, /device:TPU:1, one launch (start us, length us, event | category | flops | bytes accessed | tf_op | source)
XLA Modules:
  0.0 170.2 jit_solution(3759919917535363503)
XLA Ops:
  0.6 2.5 %slots.1 = (s32[16,2,128]{2,1,0:T(2,128)}, s32[8,2,128]{2,1,0:T(2,128)}) custom-call(s32[1,2048]{1,0:T(1,128)} %bitcast.29, s32[1,2048]{1,0:T(1,128)} %bitcast.30, s32[1,2048]{1,0:T(1,128)} %bitcast.31, s32[1,2048]{1,0:T(1,128)} %bitcast.32), custom_call_target="tpu_custom_call" | custom-call | flops 2750000128 | bytes 9000000 | tf_op jit(solution)/shard_map/slots/pallas_call | solution.py:95
  3.1 8.6 %all-to-all-start = ((s32[16,2,128]{2,1,0:T(2,128)}), s32[16,2,128]{2,1,0:T(2,128)S(1)}, u32[]{:S(2)}, u32[]{:S(2)}) async-start(s32[16,2,128]{2,1,0:T(2,128)} %get-tuple-element.29), calls=%async_computation | async-start | bytes 32768 | tf_op jit(solution)/shard_map/all_to_all | solution.py:576
  11.7 1.7 copy.18.table_ref
  13.4 4.8 %all-to-all-done = s32[16,2,128]{2,1,0:T(2,128)S(1)} async-done(((s32[16,2,128]{2,1,0:T(2,128)}), s32[16,2,128]{2,1,0:T(2,128)S(1)}, u32[]{:S(2)}, u32[]{:S(2)}) %all-to-all-start) | async-done | bytes 16416 | tf_op jit(solution)/shard_map/all_to_all | solution.py:576
  18.2 0.6 copy-done.7
  18.8 8.8 %pick_rows.1 = bf16[16,128,128]{2,1,0:T(8,128)(2,1)} custom-call(s32[4096]{0:T(1024)} %bitcast.26, f32[4096,64]{1,0:T(8,128)} %copy.18.table_ref), custom_call_target="tpu_custom_call" | custom-call | flops 7699999744 | bytes 25200000 | tf_op jit(solution)/shard_map/pick_rows/pallas_call | solution.py:138
  27.6 13.7 %all_to_all.25.returned_ref = bf16[16,128,128]{2,1,0:T(8,128)(2,1)} all-to-all(bf16[16,128,128]{2,1,0:T(8,128)(2,1)} %pick_rows.1), channel_id=1, replica_groups=mesh['seq'=16,'col'=8] {'seq'}, dimensions={0} | all-to-all | bytes 1048576 | tf_op jit(solution)/shard_map/all_to_all | solution.py:578
  41.3 4.1 %place_rows.1 = bf16[8,128,128]{2,1,0:T(8,128)(2,1)} custom-call(s32[2048]{0:T(1024)} %bitcast.35, bf16[16,128,128]{2,1,0:T(8,128)(2,1)} %all_to_all.25.returned_ref, bf16[64,256]{1,0:T(8,128)(2,1)} %bitcast.28), custom_call_target="tpu_custom_call" | custom-call | flops 4400000000 | bytes 14400000 | tf_op jit(solution)/shard_map/place_rows/pallas_call | solution.py:166
  45.4 13.9 %all_to_all.26.emb_ref = bf16[8,128,128]{2,1,0:T(8,128)(2,1)} all-to-all(bf16[8,128,128]{2,1,0:T(8,128)(2,1)} %place_rows.1), channel_id=1, replica_groups=mesh['seq'=16,'col'=8] {'col'}, dimensions={0} | all-to-all | bytes 524288 | tf_op jit(solution)/shard_map/all_to_all | solution.py:580
  59.3 16.0 %layers.1 = (bf16[256,512]{1,0:T(8,128)(2,1)}, bf16[8,128,128]{2,1,0:T(8,128)(2,1)}, bf16[4,176,512]{2,1,0:T(8,128)(2,1)}, bf16[4,176,512]{2,1,0:T(8,128)(2,1)},...) custom-call(s32[8,2,128]{2,1,0:T(2,128)} %get-tuple-element.28.index, ...), custom_call_target="tpu_custom_call" | custom-call | flops 17600000000 | bytes 57600000 | tf_op jit(solution)/shard_map/layers/pallas_call | solution.py:413
  75.3 1.1 collective-permute-start.1
  76.5 0.4 collective-permute-start.5
  77.1 1.4 collective-permute-done.1
  78.5 1.3 add_convert_fusion.3
  79.8 0.5 collective-permute-start.2
  80.8 0.5 collective-permute-start.4
  81.8 2.2 %collective-permute-start.6 = (bf16[4,176,512]{2,1,0:T(8,128)(2,1)S(1)}, bf16[4,176,512]{2,1,0:T(8,128)(2,1)}, u32[]{:S(2)}, u32[]{:S(2)}) collective-permute-start(bf16[4,176,512]{2,1,0:T(8,128)(2,1)S(1)} %add_convert_fusion.1), channel_id=1, source_target_pairs={{0,6},{1,25},{2,0},{3,27},{4,2},{5,29},{6,4},{7,31},{8,14},{9,1},{... | collective-permute-start | bytes 2162696 | tf_op jit(solution)/shard_map/ppermute | solution.py:474
  84.0 4.2 %all-to-all-start.3 = ((bf16[8,128,128]{2,1,0:T(8,128)(2,1)}), bf16[8,128,128]{2,1,0:T(8,128)(2,1)S(1)}, u32[]{:S(2)}, u32[]{:S(2)}) async-start(bf16[8,128,128]{2,1,0:T(8,128)(2,1)} %get-tuple-element.39), calls=%async_computation.3 | async-start | bytes 524288 | tf_op jit(solution)/shard_map/all_to_all | solution.py:585
  88.2 3.8 %collective-permute-done.2 = bf16[4,176,512]{2,1,0:T(8,128)(2,1)} collective-permute-done((bf16[4,176,512]{2,1,0:T(8,128)(2,1)S(1)}, bf16[4,176,512]{2,1,0:T(8,128)(2,1)}, u32[]{:S(2)}, u32[]{:S(2)}) %collective-permute-start.2) | collective-permute-done | bytes 720928 | tf_op jit(solution)/shard_map/ppermute | solution.py:474
  92.0 7.7 %collective-permute-done.4 = bf16[4,176,512]{2,1,0:T(8,128)(2,1)} collective-permute-done((bf16[4,176,512]{2,1,0:T(8,128)(2,1)S(1)}, bf16[4,176,512]{2,1,0:T(8,128)(2,1)}, u32[]{:S(2)}, u32[]{:S(2)}) %collective-permute-start.4) | collective-permute-done | bytes 720928 | tf_op jit(solution)/shard_map/ppermute | solution.py:474
  99.7 2.2 %add_convert_fusion = bf16[4,176,512]{2,1,0:T(8,128)(2,1)S(1)} fusion(bf16[4,176,512]{2,1,0:T(8,128)(2,1)} %collective-permute-done.6, bf16[4,176,512]{2,1,0:T(8,128)(2,1)} %collective-permute-done.4, bf16[4,176,512]{2,1,0:T(8,128)(2,1)} %collective-permute-done.2, bf16[4,176,512]{2,1,0:T(8,128)(2,1)} %collective-permute-done, bf16[4,176,512]{2,1,0:T(8,128)(2,1)S(1)} %copy-done.3), kind=kLoop, calls=%fused_computation | loop fusion | flops 4325376 | bytes 4325376 | tf_op jit(solution)/shard_map/convert_element_type | solution.py:481
  101.9 0.7 all-to-all-done.3.grad_ref
  102.6 0.6 collective-permute-start.7
  103.2 1.3 collective-permute-start.9
  104.7 3.9 %collective-permute-done.7 = bf16[176,512]{1,0:T(8,128)(2,1)S(1)} collective-permute-done((bf16[176,512]{1,0:T(8,128)(2,1)S(1)}, bf16[176,512]{1,0:T(8,128)(2,1)S(1)}, u32[]{:S(2)}, u32[]{:S(2)}) %collective-permute-start.7) | collective-permute-done | bytes 180256 | tf_op jit(solution)/shard_map/ppermute | solution.py:474
  108.6 2.2 %collective-permute-done.8 = bf16[176,512]{1,0:T(8,128)(2,1)S(1)} collective-permute-done((bf16[176,512]{1,0:T(8,128)(2,1)S(1)}, bf16[176,512]{1,0:T(8,128)(2,1)S(1)}, u32[]{:S(2)}, u32[]{:S(2)}) %collective-permute-start.8) | collective-permute-done | bytes 180256 | tf_op jit(solution)/shard_map/ppermute | solution.py:474
  110.9 1.0 collective-permute-start.12
  111.8 0.6 collective-permute-start.11
  112.4 0.7 collective-permute-start.10
  113.1 4.1 %return_rows.1 = bf16[16,128,128]{2,1,0:T(8,128)(2,1)} custom-call(s32[2048]{0:T(1024)} %bitcast.36, bf16[8,128,128]{2,1,0:T(8,128)(2,1)} %copy-done.6), custom_call_target="tpu_custom_call" | custom-call | flops 4400000000 | bytes 14400000 | tf_op jit(solution)/shard_map/return_rows/pallas_call | solution.py:194
  117.2 3.6 %all-to-all-start.4 = ((bf16[16,128,128]{2,1,0:T(8,128)(2,1)}), bf16[16,128,128]{2,1,0:T(8,128)(2,1)S(1)}, u32[]{:S(2)}, u32[]{:S(2)}) async-start(bf16[16,128,128]{2,1,0:T(8,128)(2,1)} %return_rows.1), calls=%async_computation.4 | async-start | bytes 1048576 | tf_op jit(solution)/shard_map/all_to_all | solution.py:591
  120.9 1.3 collective-permute-start.15
  122.2 2.4 %collective-permute-start.14 = (bf16[176,512]{1,0:T(8,128)(2,1)S(1)}, bf16[176,512]{1,0:T(8,128)(2,1)S(1)}, u32[]{:S(2)}, u32[]{:S(2)}) collective-permute-start(bf16[176,512]{1,0:T(8,128)(2,1)S(1)} %add_convert_fusion.5), channel_id=1, source_target_pairs={{0,16},{1,65},{2,18},{3,67},{4,20},{5,69},{6,22},{7,71},{8,24},{9,... | collective-permute-start | bytes 540680 | tf_op jit(solution)/shard_map/ppermute | solution.py:474
  124.7 1.2 collective-permute-start.13
  125.8 3.0 %collective-permute-done.15 = bf16[176,512]{1,0:T(8,128)(2,1)S(1)} collective-permute-done((bf16[176,512]{1,0:T(8,128)(2,1)S(1)}, bf16[176,512]{1,0:T(8,128)(2,1)S(1)}, u32[]{:S(2)}, u32[]{:S(2)}) %collective-permute-start.15) | collective-permute-done | bytes 180256 | tf_op jit(solution)/shard_map/ppermute | solution.py:474
  128.8 4.0 %collective-permute-done.14 = bf16[176,512]{1,0:T(8,128)(2,1)S(1)} collective-permute-done((bf16[176,512]{1,0:T(8,128)(2,1)S(1)}, bf16[176,512]{1,0:T(8,128)(2,1)S(1)}, u32[]{:S(2)}, u32[]{:S(2)}) %collective-permute-start.14) | collective-permute-done | bytes 180256 | tf_op jit(solution)/shard_map/ppermute | solution.py:474
  132.8 1.8 %collective-permute-done.13 = bf16[176,512]{1,0:T(8,128)(2,1)S(1)} collective-permute-done((bf16[176,512]{1,0:T(8,128)(2,1)S(1)}, bf16[176,512]{1,0:T(8,128)(2,1)S(1)}, u32[]{:S(2)}, u32[]{:S(2)}) %collective-permute-start.13) | collective-permute-done | bytes 180256 | tf_op jit(solution)/shard_map/ppermute | solution.py:474
  134.7 3.2 %collective-permute-start.19 = (bf16[4,176,512]{2,1,0:T(8,128)(2,1)S(1)}, bf16[4,176,512]{2,1,0:T(8,128)(2,1)S(1)}, u32[]{:S(2)}, u32[]{:S(2)}) collective-permute-start(bf16[4,176,512]{2,1,0:T(8,128)(2,1)S(1)} %pad_maximum_fusion.refs_0_), channel_id=1, source_target_pairs={{0,1},{1,0},{2,3},{3,2},{4,5},{5,4},{6,7},{7,6},{8,9},{9,8},{10,11... | collective-permute-start | bytes 2162696 | tf_op jit(solution)/shard_map/ppermute | solution.py:464
  137.9 2.7 %collective-permute-start.17 = (bf16[4,176,512]{2,1,0:T(8,128)(2,1)S(1)}, bf16[4,176,512]{2,1,0:T(8,128)(2,1)S(1)}, u32[]{:S(2)}, u32[]{:S(2)}) collective-permute-start(bf16[4,176,512]{2,1,0:T(8,128)(2,1)S(1)} %pad_maximum_fusion.refs_0_), channel_id=1, source_target_pairs={{0,6},{1,25},{2,0},{3,27},{4,2},{5,29},{6,4},{7,31},{8,14},{9,1},{... | collective-permute-start | bytes 2162696 | tf_op jit(solution)/shard_map/ppermute | solution.py:474
  140.6 9.4 %scatter_rows.1 = f32[64,4096]{1,0:T(8,128)} custom-call(s32[4096]{0:T(1024)} %bitcast.27, bf16[16,128,128]{2,1,0:T(8,128)(2,1)} %copy-done.5), custom_call_target="tpu_custom_call" | custom-call | flops 12099999744 | bytes 39600000 | tf_op jit(solution)/shard_map/scatter_rows/pallas_call | solution.py:235
  150.0 6.7 %collective-permute-done.16.refs_2_ = bf16[4,176,512]{2,1,0:T(8,128)(2,1)S(1)} collective-permute-done((bf16[4,176,512]{2,1,0:T(8,128)(2,1)S(1)}, bf16[4,176,512]{2,1,0:T(8,128)(2,1)S(1)}, u32[]{:S(2)}, u32[]{:S(2)}) %collective-permute-start.16) | collective-permute-done | bytes 720928 | tf_op jit(solution)/shard_map/ppermute | solution.py:474
  156.7 0.6 collective-permute-done.18.refs_3_
  157.3 0.9 collective-permute-start.22
  158.3 0.4 collective-permute-start.21
  158.7 0.3 copy-done.10
  159.1 5.0 %finish_own.1 = (f32[2,512,2048]{2,1,0:T(8,128)}, f32[2,512,512]{2,1,0:T(8,128)}, f32[64,256]{1,0:T(8,128)}) custom-call(bf16[4,176,512]{2,1,0:T(8,128)(2,1)} %copy-done, bf16[4,176,512]{2,1,0:T(8,128)(2,1)} %copy-done.10, bf16[4,176,512]{2,1,0:T(8,128)(2,1)} %copy-done.11, bf16[4,176,512]{2,1,0:T(8,128)(2,1)} %copy-done.9), custom_call_target="tpu_custom_call" | custom-call | flops 4400000000 | bytes 14400000 | tf_op jit(solution)/shard_map/finish_own/pallas_call | solution.py:556
  164.2 0.8 copy-done.8
  165.7 4.4 %finish_other.1 = (f32[2,512,2048]{2,1,0:T(8,128)}, f32[2,512,512]{2,1,0:T(8,128)}) custom-call(bf16[4,176,512]{2,1,0:T(8,128)(2,1)} %copy-done.8, bf16[4,176,512]{2,1,0:T(8,128)(2,1)} %copy-done.13, bf16[4,176,512]{2,1,0:T(8,128)(2,1)} %copy-done.14, bf16[4,176,512]{2,1,0:T(8,128)(2,1)} %copy-done.12, ...), custom_call_target="tpu_custom_call", output_to_operand_aliasing={{0}: (4, {}), {1}: (5, {})} | custom-call | flops 4400000000 | bytes 14400000 | tf_op jit(solution)/shard_map/finish_other/pallas_call | solution.py:556
  (53 shorter events, 2.4 us)
Async XLA Ops:
  0.6 11.1 %copy-start.4 = (bf16[4096,64]{0,1:T(8,128)(2,1)S(1)}, bf16[4096,64]{0,1:T(8,128)(2,1)}, u32[]{:S(2)}) copy-start(bf16[4096,64]{0,1:T(8,128)(2,1)} %param.10) | copy-start | bytes 1572868
  3.1 15.0 %all-to-all-start = ((s32[16,2,128]{2,1,0:T(2,128)}), s32[16,2,128]{2,1,0:T(2,128)S(1)}, u32[]{:S(2)}, u32[]{:S(2)}) async-start(s32[16,2,128]{2,1,0:T(2,128)} %get-tuple-element.29), calls=%async_computation | async-start | bytes 32768 | tf_op jit(solution)/shard_map/all_to_all | solution.py:576
  18.2 0.6 copy-start.7
  75.3 5.2 %copy-start.2 = (bf16[4,176,512]{2,1,0:T(8,128)(2,1)S(1)}, bf16[4,176,512]{2,1,0:T(8,128)(2,1)}, u32[]{:S(2)}) copy-start(bf16[4,176,512]{2,1,0:T(8,128)(2,1)} %get-tuple-element.35) | copy-start | bytes 2162692
  75.3 3.2 %collective-permute-start.1 = (bf16[4,176,512]{2,1,0:T(8,128)(2,1)}, bf16[4,176,512]{2,1,0:T(8,128)(2,1)S(1)}, u32[]{:S(2)}, u32[]{:S(2)}) collective-permute-start(bf16[4,176,512]{2,1,0:T(8,128)(2,1)} %get-tuple-element.34), channel_id=1, source_target_pairs={{0,1},{1,0},{2,3},{3,2},{4,5},{5,4},{6,7},{7,6},{8,9},{9,8},{10,11... | collective-permute-start | bytes 2162696 | tf_op jit(solution)/shard_map/ppermute | solution.py:464
  76.5 4.1 %collective-permute-start.3 = (bf16[4,176,512]{2,1,0:T(8,128)(2,1)}, bf16[4,176,512]{2,1,0:T(8,128)(2,1)S(1)}, u32[]{:S(2)}, u32[]{:S(2)}) collective-permute-start(bf16[4,176,512]{2,1,0:T(8,128)(2,1)} %get-tuple-element.36), channel_id=1, source_target_pairs={{0,1},{1,0},{2,3},{3,2},{4,5},{5,4},{6,7},{7,6},{8,9},{9,8},{10,11... | collective-permute-start | bytes 2162696 | tf_op jit(solution)/shard_map/ppermute | solution.py:464
  76.5 5.0 %collective-permute-start.5 = (bf16[4,176,512]{2,1,0:T(8,128)(2,1)}, bf16[4,176,512]{2,1,0:T(8,128)(2,1)S(1)}, u32[]{:S(2)}, u32[]{:S(2)}) collective-permute-start(bf16[4,176,512]{2,1,0:T(8,128)(2,1)} %get-tuple-element.38), channel_id=1, source_target_pairs={{0,1},{1,0},{2,3},{3,2},{4,5},{5,4},{6,7},{7,6},{8,9},{9,8},{10,11... | collective-permute-start | bytes 2162696 | tf_op jit(solution)/shard_map/ppermute | solution.py:464
  77.0 11.2 %collective-permute-start = (bf16[4,176,512]{2,1,0:T(8,128)(2,1)}, bf16[4,176,512]{2,1,0:T(8,128)(2,1)}, u32[]{:S(2)}, u32[]{:S(2)}) collective-permute-start(bf16[4,176,512]{2,1,0:T(8,128)(2,1)} %get-tuple-element.32), channel_id=1, source_target_pairs={{0,1},{1,0},{2,3},{3,2},{4,5},{5,4},{6,7},{7,6},{8,9},{9,8},{10,11... | collective-permute-start | bytes 2162696 | tf_op jit(solution)/shard_map/ppermute | solution.py:464
  79.8 1.8 %copy-start.1 = (bf16[4,176,512]{2,1,0:T(8,128)(2,1)S(1)}, bf16[4,176,512]{2,1,0:T(8,128)(2,1)}, u32[]{:S(2)}) copy-start(bf16[4,176,512]{2,1,0:T(8,128)(2,1)} %get-tuple-element.37) | copy-start | bytes 2162692
  79.8 12.2 %collective-permute-start.2 = (bf16[4,176,512]{2,1,0:T(8,128)(2,1)S(1)}, bf16[4,176,512]{2,1,0:T(8,128)(2,1)}, u32[]{:S(2)}, u32[]{:S(2)}) collective-permute-start(bf16[4,176,512]{2,1,0:T(8,128)(2,1)S(1)} %add_convert_fusion.3), channel_id=1, source_target_pairs={{0,4},{1,17},{2,6},{3,19},{4,0},{5,21},{6,2},{7,23},{8,12},{9,25},... | collective-permute-start | bytes 2162696 | tf_op jit(solution)/shard_map/ppermute | solution.py:474
  80.7 18.9 %copy-start.3 = (bf16[4,176,512]{2,1,0:T(8,128)(2,1)S(1)}, bf16[4,176,512]{2,1,0:T(8,128)(2,1)}, u32[]{:S(2)}) copy-start(bf16[4,176,512]{2,1,0:T(8,128)(2,1)} %get-tuple-element.31) | copy-start | bytes 2162692
  80.8 18.9 %collective-permute-start.4 = (bf16[4,176,512]{2,1,0:T(8,128)(2,1)S(1)}, bf16[4,176,512]{2,1,0:T(8,128)(2,1)}, u32[]{:S(2)}, u32[]{:S(2)}) collective-permute-start(bf16[4,176,512]{2,1,0:T(8,128)(2,1)S(1)} %add_convert_fusion.2), channel_id=1, source_target_pairs={{0,2},{1,9},{2,4},{3,11},{4,6},{5,13},{6,0},{7,15},{8,10},{9,17},{... | collective-permute-start | bytes 2162696 | tf_op jit(solution)/shard_map/ppermute | solution.py:474
  81.8 17.9 %collective-permute-start.6 = (bf16[4,176,512]{2,1,0:T(8,128)(2,1)S(1)}, bf16[4,176,512]{2,1,0:T(8,128)(2,1)}, u32[]{:S(2)}, u32[]{:S(2)}) collective-permute-start(bf16[4,176,512]{2,1,0:T(8,128)(2,1)S(1)} %add_convert_fusion.1), channel_id=1, source_target_pairs={{0,6},{1,25},{2,0},{3,27},{4,2},{5,29},{6,4},{7,31},{8,14},{9,1},{... | collective-permute-start | bytes 2162696 | tf_op jit(solution)/shard_map/ppermute | solution.py:474
  84.0 18.6 %all-to-all-start.3 = ((bf16[8,128,128]{2,1,0:T(8,128)(2,1)}), bf16[8,128,128]{2,1,0:T(8,128)(2,1)S(1)}, u32[]{:S(2)}, u32[]{:S(2)}) async-start(bf16[8,128,128]{2,1,0:T(8,128)(2,1)} %get-tuple-element.39), calls=%async_computation.3 | async-start | bytes 524288 | tf_op jit(solution)/shard_map/all_to_all | solution.py:585
  102.6 10.5 %copy-start.6 = (bf16[8,128,128]{2,1,0:T(8,128)(2,1)}, bf16[8,128,128]{2,1,0:T(8,128)(2,1)S(1)}, u32[]{:S(2)}) copy-start(bf16[8,128,128]{2,1,0:T(8,128)(2,1)S(1)} %all-to-all-done.3.grad_ref) | copy-start | bytes 786436
  102.6 6.0 %collective-permute-start.7 = (bf16[176,512]{1,0:T(8,128)(2,1)S(1)}, bf16[176,512]{1,0:T(8,128)(2,1)S(1)}, u32[]{:S(2)}, u32[]{:S(2)}) collective-permute-start(bf16[176,512]{1,0:T(8,128)(2,1)S(1)} %get-tuple-element.51), channel_id=1, source_target_pairs={{0,16},{1,65},{2,18},{3,67},{4,20},{5,69},{6,22},{7,71},{8,24},{9,... | collective-permute-start | bytes 540680 | tf_op jit(solution)/shard_map/ppermute | solution.py:474
  103.2 5.4 %collective-permute-start.9 = (bf16[176,512]{1,0:T(8,128)(2,1)S(1)}, bf16[176,512]{1,0:T(8,128)(2,1)S(1)}, u32[]{:S(2)}, u32[]{:S(2)}) collective-permute-start(bf16[176,512]{1,0:T(8,128)(2,1)S(1)} %get-tuple-element.52), channel_id=1, source_target_pairs={{0,24},{1,97},{2,26},{3,99},{4,28},{5,101},{6,30},{7,103},{8,0},{9... | collective-permute-start | bytes 540680 | tf_op jit(solution)/shard_map/ppermute | solution.py:474
  104.6 6.2 %collective-permute-start.8 = (bf16[176,512]{1,0:T(8,128)(2,1)S(1)}, bf16[176,512]{1,0:T(8,128)(2,1)S(1)}, u32[]{:S(2)}, u32[]{:S(2)}) collective-permute-start(bf16[176,512]{1,0:T(8,128)(2,1)S(1)} %get-tuple-element.53), channel_id=1, source_target_pairs={{0,8},{1,33},{2,10},{3,35},{4,12},{5,37},{6,14},{7,39},{8,16},{9,4... | collective-permute-start | bytes 540680 | tf_op jit(solution)/shard_map/ppermute | solution.py:474
  110.9 9.9 %collective-permute-start.12 = (bf16[176,512]{1,0:T(8,128)(2,1)S(1)}, bf16[176,512]{1,0:T(8,128)(2,1)S(1)}, u32[]{:S(2)}, u32[]{:S(2)}) collective-permute-start(bf16[176,512]{1,0:T(8,128)(2,1)S(1)} %fusion.1), channel_id=1, source_target_pairs={{0,96},{1,7},{2,98},{3,1},{4,100},{5,3},{6,102},{7,5},{8,104},{9,1... | collective-permute-start | bytes 540680 | tf_op jit(solution)/shard_map/ppermute | solution.py:474
  111.8 9.0 %collective-permute-start.11 = (bf16[176,512]{1,0:T(8,128)(2,1)S(1)}, bf16[176,512]{1,0:T(8,128)(2,1)S(1)}, u32[]{:S(2)}, u32[]{:S(2)}) collective-permute-start(bf16[176,512]{1,0:T(8,128)(2,1)S(1)} %fusion.1), channel_id=1, source_target_pairs={{0,32},{1,3},{2,34},{3,5},{4,36},{5,7},{6,38},{7,1},{8,40},{9,11},... | collective-permute-start | bytes 540680 | tf_op jit(solution)/shard_map/ppermute | solution.py:474
  112.4 8.4 %collective-permute-start.10 = (bf16[176,512]{1,0:T(8,128)(2,1)S(1)}, bf16[176,512]{1,0:T(8,128)(2,1)S(1)}, u32[]{:S(2)}, u32[]{:S(2)}) collective-permute-start(bf16[176,512]{1,0:T(8,128)(2,1)S(1)} %fusion.1), channel_id=1, source_target_pairs={{0,64},{1,5},{2,66},{3,7},{4,68},{5,1},{6,70},{7,3},{8,72},{9,13},... | collective-permute-start | bytes 540680 | tf_op jit(solution)/shard_map/ppermute | solution.py:474
  117.2 17.5 %all-to-all-start.4 = ((bf16[16,128,128]{2,1,0:T(8,128)(2,1)}), bf16[16,128,128]{2,1,0:T(8,128)(2,1)S(1)}, u32[]{:S(2)}, u32[]{:S(2)}) async-start(bf16[16,128,128]{2,1,0:T(8,128)(2,1)} %return_rows.1), calls=%async_computation.4 | async-start | bytes 1048576 | tf_op jit(solution)/shard_map/all_to_all | solution.py:591
  120.9 7.9 %collective-permute-start.15 = (bf16[176,512]{1,0:T(8,128)(2,1)S(1)}, bf16[176,512]{1,0:T(8,128)(2,1)S(1)}, u32[]{:S(2)}, u32[]{:S(2)}) collective-permute-start(bf16[176,512]{1,0:T(8,128)(2,1)S(1)} %add_convert_fusion.5), channel_id=1, source_target_pairs={{0,8},{1,33},{2,10},{3,35},{4,12},{5,37},{6,14},{7,39},{8,16},{9,4... | collective-permute-start | bytes 540680 | tf_op jit(solution)/shard_map/ppermute | solution.py:474
  122.2 10.6 %collective-permute-start.14 = (bf16[176,512]{1,0:T(8,128)(2,1)S(1)}, bf16[176,512]{1,0:T(8,128)(2,1)S(1)}, u32[]{:S(2)}, u32[]{:S(2)}) collective-permute-start(bf16[176,512]{1,0:T(8,128)(2,1)S(1)} %add_convert_fusion.5), channel_id=1, source_target_pairs={{0,16},{1,65},{2,18},{3,67},{4,20},{5,69},{6,22},{7,71},{8,24},{9,... | collective-permute-start | bytes 540680 | tf_op jit(solution)/shard_map/ppermute | solution.py:474
  124.7 9.9 %collective-permute-start.13 = (bf16[176,512]{1,0:T(8,128)(2,1)S(1)}, bf16[176,512]{1,0:T(8,128)(2,1)S(1)}, u32[]{:S(2)}, u32[]{:S(2)}) collective-permute-start(bf16[176,512]{1,0:T(8,128)(2,1)S(1)} %add_convert_fusion.5), channel_id=1, source_target_pairs={{0,24},{1,97},{2,26},{3,99},{4,28},{5,101},{6,30},{7,103},{8,0},{9... | collective-permute-start | bytes 540680 | tf_op jit(solution)/shard_map/ppermute | solution.py:474
  134.7 15.3 %copy-start = (bf16[4,176,512]{2,1,0:T(8,128)(2,1)}, bf16[4,176,512]{2,1,0:T(8,128)(2,1)S(1)}, u32[]{:S(2)}) copy-start(bf16[4,176,512]{2,1,0:T(8,128)(2,1)S(1)} %pad_maximum_fusion.refs_0_) | copy-start | bytes 2162692
  134.7 5.9 %copy-start.5 = (bf16[16,128,128]{2,1,0:T(8,128)(2,1)}, bf16[16,128,128]{2,1,0:T(8,128)(2,1)S(1)}, u32[]{:S(2)}) copy-start(bf16[16,128,128]{2,1,0:T(8,128)(2,1)S(1)} %all-to-all-done.4.incoming_ref) | copy-start | bytes 1572868
  134.7 29.4 %collective-permute-start.19 = (bf16[4,176,512]{2,1,0:T(8,128)(2,1)S(1)}, bf16[4,176,512]{2,1,0:T(8,128)(2,1)S(1)}, u32[]{:S(2)}, u32[]{:S(2)}) collective-permute-start(bf16[4,176,512]{2,1,0:T(8,128)(2,1)S(1)} %pad_maximum_fusion.refs_0_), channel_id=1, source_target_pairs={{0,1},{1,0},{2,3},{3,2},{4,5},{5,4},{6,7},{7,6},{8,9},{9,8},{10,11... | collective-permute-start | bytes 2162696 | tf_op jit(solution)/shard_map/ppermute | solution.py:464
  137.9 19.4 %collective-permute-start.18 = (bf16[4,176,512]{2,1,0:T(8,128)(2,1)S(1)}, bf16[4,176,512]{2,1,0:T(8,128)(2,1)S(1)}, u32[]{:S(2)}, u32[]{:S(2)}) collective-permute-start(bf16[4,176,512]{2,1,0:T(8,128)(2,1)S(1)} %pad_maximum_fusion.refs_0_), channel_id=1, source_target_pairs={{0,2},{1,9},{2,4},{3,11},{4,6},{5,13},{6,0},{7,15},{8,10},{9,17},{... | collective-permute-start | bytes 2162696 | tf_op jit(solution)/shard_map/ppermute | solution.py:474
  137.9 20.3 %collective-permute-start.17 = (bf16[4,176,512]{2,1,0:T(8,128)(2,1)S(1)}, bf16[4,176,512]{2,1,0:T(8,128)(2,1)S(1)}, u32[]{:S(2)}, u32[]{:S(2)}) collective-permute-start(bf16[4,176,512]{2,1,0:T(8,128)(2,1)S(1)} %pad_maximum_fusion.refs_0_), channel_id=1, source_target_pairs={{0,6},{1,25},{2,0},{3,27},{4,2},{5,29},{6,4},{7,31},{8,14},{9,1},{... | collective-permute-start | bytes 2162696 | tf_op jit(solution)/shard_map/ppermute | solution.py:474
  140.6 16.1 %collective-permute-start.16 = (bf16[4,176,512]{2,1,0:T(8,128)(2,1)S(1)}, bf16[4,176,512]{2,1,0:T(8,128)(2,1)S(1)}, u32[]{:S(2)}, u32[]{:S(2)}) collective-permute-start(bf16[4,176,512]{2,1,0:T(8,128)(2,1)S(1)} %pad_maximum_fusion.refs_0_), channel_id=1, source_target_pairs={{0,4},{1,17},{2,6},{3,19},{4,0},{5,21},{6,2},{7,23},{8,12},{9,25},... | collective-permute-start | bytes 2162696 | tf_op jit(solution)/shard_map/ppermute | solution.py:474
  156.7 2.1 %copy-start.11 = (bf16[4,176,512]{2,1,0:T(8,128)(2,1)}, bf16[4,176,512]{2,1,0:T(8,128)(2,1)S(1)}, u32[]{:S(2)}) copy-start(bf16[4,176,512]{2,1,0:T(8,128)(2,1)S(1)} %collective-permute-done.16.refs_2_) | copy-start | bytes 2162692
  157.3 1.5 copy-start.9
  157.3 6.9 %collective-permute-start.22 = (bf16[4,176,512]{2,1,0:T(8,128)(2,1)S(1)}, bf16[4,176,512]{2,1,0:T(8,128)(2,1)S(1)}, u32[]{:S(2)}, u32[]{:S(2)}) collective-permute-start(bf16[4,176,512]{2,1,0:T(8,128)(2,1)S(1)} %collective-permute-done.18.refs_3_), channel_id=1, source_target_pairs={{0,1},{1,0},{2,3},{3,2},{4,5},{5,4},{6,7},{7,6},{8,9},{9,8},{10,11... | collective-permute-start | bytes 2162696 | tf_op jit(solution)/shard_map/ppermute | solution.py:464
  158.2 0.9 copy-start.10
  158.2 5.9 %collective-permute-start.20 = (bf16[4,176,512]{2,1,0:T(8,128)(2,1)S(1)}, bf16[4,176,512]{2,1,0:T(8,128)(2,1)S(1)}, u32[]{:S(2)}, u32[]{:S(2)}) collective-permute-start(bf16[4,176,512]{2,1,0:T(8,128)(2,1)S(1)} %collective-permute-done.17.refs_1_), channel_id=1, source_target_pairs={{0,1},{1,0},{2,3},{3,2},{4,5},{5,4},{6,7},{7,6},{8,9},{9,8},{10,11... | collective-permute-start | bytes 2162696 | tf_op jit(solution)/shard_map/ppermute | solution.py:464
  158.3 5.9 %collective-permute-start.21 = (bf16[4,176,512]{2,1,0:T(8,128)(2,1)S(1)}, bf16[4,176,512]{2,1,0:T(8,128)(2,1)S(1)}, u32[]{:S(2)}, u32[]{:S(2)}) collective-permute-start(bf16[4,176,512]{2,1,0:T(8,128)(2,1)S(1)} %collective-permute-done.16.refs_2_), channel_id=1, source_target_pairs={{0,1},{1,0},{2,3},{3,2},{4,5},{5,4},{6,7},{7,6},{8,9},{9,8},{10,11... | collective-permute-start | bytes 2162696 | tf_op jit(solution)/shard_map/ppermute | solution.py:464
  164.1 0.9 copy-start.8
  164.2 1.1 copy-start.12
  164.2 1.3 copy-start.13
  164.2 1.5 copy-start.14

commit v3 on v2

--- a/solution.py
+++ b/solution.py
@@ -25,14 +25,14 @@
 HOT = 256
 COLS = 64
 CHUNK = 176
-VMEM_LIMIT = 56 * 1024 * 1024
+MIB = 1024 * 1024
 
 NT = (((1,), (1,)), ((), ()))
 TN = (((0,), (0,)), ((), ()))
 
 
-def params(**more):
-    return pltpu.CompilerParams(vmem_limit_bytes=VMEM_LIMIT, **more)
+def params(mib):
+    return pltpu.CompilerParams(vmem_limit_bytes=mib * MIB)
 
 
 def cost(microseconds):
@@ -47,6 +47,7 @@
 
 SMEM = pl.BlockSpec(memory_space=pltpu.SMEM)
 ANY = pl.BlockSpec(memory_space=pl.ANY)
+HBM = pl.BlockSpec(memory_space=pltpu.HBM)
 
 
 def mm(a, b, dims=None):
@@ -100,7 +101,7 @@
         ),
         in_specs=vmem(4),
         out_specs=tuple(vmem(2)),
-        compiler_params=params(),
+        compiler_params=params(60),
         cost_estimate=cost(2.5),
         name="slots",
     )(owner, item, flag, hot)
@@ -141,7 +142,7 @@
         in_specs=[SMEM] + vmem(1),
         out_specs=vmem(1)[0],
         scratch_shapes=[pltpu.VMEM((SLOTS, COLS), F32)],
-        compiler_params=params(),
+        compiler_params=params(16),
         cost_estimate=cost(7),
         name="pick_rows",
     )(requests.reshape(SLOTS), table)
@@ -169,7 +170,7 @@
         in_specs=[SMEM] + vmem(2),
         out_specs=vmem(1)[0],
         scratch_shapes=[pltpu.VMEM((SLOTS + HOT, COLS), F32), pltpu.VMEM((SEQ_TOK, COLS), F32)],
-        compiler_params=params(),
+        compiler_params=params(16),
         cost_estimate=cost(4),
         name="place_rows",
     )(index.reshape(SEQ_TOK), returned, hot_table.T)
@@ -200,7 +201,7 @@
             pltpu.VMEM((SEQ_TOK, COLS), F32),
             pltpu.VMEM((SLOTS + HOT, COLS), F32),
         ],
-        compiler_params=params(),
+        compiler_params=params(16),
         cost_estimate=cost(4),
         name="return_rows",
     )(index.reshape(SEQ_TOK), grads)
@@ -239,7 +240,7 @@
         out_specs=vmem(1)[0],
         scratch_shapes=[pltpu.VMEM((SLOTS, COLS), F32)]
         + [pltpu.VMEM((ITEMS_DEV + 8, COLS), F32)] * 4,
-        compiler_params=params(),
+        compiler_params=params(24),
         cost_estimate=cost(11),
         name="scatter_rows",
     )(requests.reshape(SLOTS), incoming).T
@@ -268,38 +269,26 @@
 
 
 def stack_kernel(
-    index_ref, emb_ref, segment_ref, cot_ref, win_hbm, wout_hbm,
+    index_ref, emb_ref, segment_ref, cot_ref, win_ref, wout_ref,
     enc_ref, grad_ref, *refs
 ):
     outs, refs = refs[:8], refs[8:]
-    stream, normed, normed_scale, proj, slope, attn, attn_slope, mixed, mixed_scale, gated, dproj, pay, win_ref, wout_ref, sems, win_sems, wout_sems = refs
+    stream, normed, normed_scale, proj, slope, attn, attn_slope, mixed, mixed_scale, gated, dproj, pay, sems = refs
     keep, send = outs[:4], outs[4:]
-    loads = {}
-    for l in range(LAYERS):
-        for part in range(4):
-            span = slice(part * D, (part + 1) * D)
-            loads[l, part] = pltpu.make_async_copy(
-                win_hbm.at[l, :, span], win_ref.at[l, :, span], win_sems.at[l, part]
-            )
-        loads[l, 4] = pltpu.make_async_copy(wout_hbm.at[l], wout_ref.at[l], wout_sems.at[l])
-    for l in range(LAYERS):
-        for part in range(5):
-            loads[l, part].start()
     (x, y, z), core = places()
 
-    def leave(l, part, act):
-        span = slice(part * 32, min(part * 32 + 32, CHUNK))
-
+    def leave(l, span, sem, act):
         def each(targets):
             for a in range(4):
                 copy = pltpu.make_async_copy(
-                    pay.at[l, 4 * a : 4 * a + 4, span], targets[a].at[:, span], sems.at[l, part, a]
+                    pay.at[l, 4 * a : 4 * a + 4, span], targets[a].at[:, span], sems.at[sem, a]
                 )
                 getattr(copy, act)()
 
         pl.when(core == l)(lambda: each(keep))
         pl.when(core != l)(lambda: each(send))
 
+    moves = ((1, slice(0, 160), 0), (1, slice(160, CHUNK), 1), (0, slice(0, CHUNK), 2))
     col = lax.axis_index("col")
 
     segment = jnp.broadcast_to(segment_ref[...].astype(F32), (TOK, TOK))
@@ -324,7 +313,6 @@
         normed_scale[l] = scale
         rounded = value.astype(BF16)
         for part in range(4):
-            loads[l, part].wait()
             pre = mm(rounded, win_ref[l, :, part * D : (part + 1) * D])
             out, tilt = silu_parts(pre)
             proj[l, part] = out.astype(BF16)
@@ -342,7 +330,6 @@
         mixed_scale[l] = scale
         product = (value * proj[l, 0].astype(F32)).astype(BF16)
         gated[l] = product
-        loads[l, 4].wait()
         stream[...] += mm(product, wout_ref[l])
     enc_ref[...] = stream[...].astype(BF16)
 
@@ -356,7 +343,6 @@
                     chunk = 4 * a + b
                     place = 4 * ((a - first) & 3) + ((b - second) & 3)
                     pay[l, place, part * 32 : (part + 1) * 32, :] = value[chunk * 32 : (chunk + 1) * 32, :]
-            leave(l, part, "start")
 
         grad = stream[...]
         grad_b = grad.astype(BF16)
@@ -385,6 +371,8 @@
             dnormed += mm(dpre, win_ref[l, :, part * D : (part + 1) * D], NT)
         dnormed = dnormed.astype(BF16).astype(F32)
         stream[...] = grad + norm_back(dnormed, value, normed_scale[l])
+        if l == 1:
+            leave(*moves[0], "start")
 
     grad = stream[...]
     for pair in range(N_COL // 2):
@@ -402,10 +390,10 @@
                 chunk = 4 * a + b
                 place = 4 * ((a - first) & 3) + ((b - second) & 3)
                 pay[l, place, 160:CHUNK, :] = hot_part[chunk * 16 : (chunk + 1) * 16, :]
-        leave(l, 5, "start")
-    for l in range(LAYERS):
-        for part in range(6):
-            leave(l, part, "wait")
+    for move in moves[1:]:
+        leave(*move, "start")
+    for move in moves:
+        leave(*move, "wait")
 
 
 def run_stack(index, emb, weight_in, weight_out, segment, cotangent):
@@ -417,8 +405,8 @@
             jax.ShapeDtypeStruct((N_COL, 128, 128), BF16),
         )
         + (piece,) * 8,
-        in_specs=vmem(4) + [ANY] * 2,
-        out_specs=tuple(vmem(2)) + (ANY,) * 8,
+        in_specs=vmem(6),
+        out_specs=tuple(vmem(2)) + (HBM,) * 8,
         scratch_shapes=[
             pltpu.VMEM((TOK, D), F32),
             pltpu.VMEM((LAYERS, TOK, D), F32),
@@ -432,13 +420,9 @@
             pltpu.VMEM((LAYERS, TOK, D), BF16),
             pltpu.VMEM((4, TOK, D), BF16),
             pltpu.VMEM((LAYERS, 16, CHUNK, D), BF16),
-            pltpu.VMEM((LAYERS, D, 4 * D), BF16),
-            pltpu.VMEM((LAYERS, D, D), BF16),
-            pltpu.SemaphoreType.DMA((LAYERS, 6, 4)),
-            pltpu.SemaphoreType.DMA((LAYERS, 4)),
-            pltpu.SemaphoreType.DMA((LAYERS,)),
+            pltpu.SemaphoreType.DMA((3, 4)),
         ],
-        compiler_params=params(),
+        compiler_params=params(36),
         cost_estimate=cost(16),
         name="layers",
     )(index, emb, segment, cotangent, weight_in, weight_out)
@@ -481,49 +465,51 @@
     return terms[0].astype(BF16)
 
 
-def sum_everywhere(keep, send, gather_columns, send_back, exchange, scatter):
-    order = (1, 3, 2, 0)
+def sum_everywhere(keep, send, grad_emb, gather_columns, send_back, exchange, scatter):
+    order = (2, 1, 3, 0)
     got = {k: to_core(send[k]) for k in order}
     chip = {k: add_all(keep[k], got[k]) for k in order}
-    came = {k: along(chip[k], 0, k) for k in (1, 3, 2)}
+    came = {k: along(chip[k], 0, k) for k in (2, 1, 3)}
     line = add_all(chip[0], came[2], came[1], came[3])
-    line, columns = lax.optimization_barrier((line, gather_columns()))
-    outgoing = send_back(columns)
-    came = {k: along(line[k], 1, k) for k in (1, 3, 2)}
+    line, grad_emb = lax.optimization_barrier((line, grad_emb))
+    came = {k: along(line[k], 1, k) for k in (2, 1, 3)}
     plane = add_all(line[0], came[2], came[1], came[3])
-    came = {k: along(plane, 2, k) for k in (1, 3, 2)}
+    outgoing = send_back(gather_columns(grad_emb))
+    came = {k: along(plane, 2, k) for k in (2, 1, 3)}
     total = add_all(plane, came[2], came[1], came[3])
     row = jnp.stack([total] + [along(total, 1, -k) for k in (1, 2, 3)])
-    row, incoming = lax.optimization_barrier((row, exchange(outgoing)))
-    mine = [row] + [along(row, 0, -k) for k in (1, 2, 3)]
+    incoming = exchange(outgoing)
+    mine = {k: along(row, 0, -k) for k in (2, 1, 3)}
+    mine[0] = row
+    other = {0: to_core(row)}
     table_grad = scatter(incoming)
-    last, table_grad = lax.optimization_barrier((mine[2], table_grad))
-    other = [to_core(value) for value in (mine[0], mine[1], last, mine[3])]
-    return mine, other, table_grad
-
-
-def finish_kernel(own, *refs):
-    sources = refs[:4]
-    if own:
-        win_ref, wout_ref, hot_ref, stage_in, stage_out, hot_rows, sems = refs[4:]
-    else:
-        win_ref, wout_ref, stage_in, stage_out, sems = refs[6:]
+    grads = finish([row, other[0]], [(0, True), (0, False)])
+    pieces = lax.optimization_barrier((mine[1], mine[2], mine[3], table_grad, grads))
+    mine[1], mine[2], mine[3], table_grad, grads = pieces
+    other.update({k: to_core(mine[k]) for k in (1, 2, 3)})
+    grads = finish([mine[k] for k in (1, 2, 3)], [(k, True) for k in (1, 2, 3)], grads)
+    hot_grad = hot_sums([mine[k] for k in range(4)])
+    grads = finish([other[k] for k in (1, 2, 3)], [(k, False) for k in (1, 2, 3)], grads)
+    return grads[0], grads[1], hot_grad, table_grad
+
+
+def finish_kernel(pieces, start, *refs):
+    sources, refs = refs[: len(pieces)], refs[len(pieces) :]
+    win_ref, wout_ref, stage_in, stage_out, sems = refs if start else refs[2:]
     (x, y, z), core = places()
-    layer = core if own else 1 - core
-    first = jnp.where(layer == 0, x, y)
-    second = jnp.where(layer == 0, y, z)
     copies = []
-    for a in range(4):
+    for i, (a, own) in enumerate(pieces):
+        layer = core if own else 1 - core
+        first = jnp.where(layer == 0, x, y)
+        second = jnp.where(layer == 0, y, z)
         for b in range(4):
             chunk = 4 * ((a + first) & 3) + ((b + second) & 3)
-            step = 4 * a + b
+            step = 4 * i + b
             for part in range(4):
-                stage_in[step, :, part * D : (part + 1) * D] = sources[a][
+                stage_in[step, :, part * D : (part + 1) * D] = sources[i][
                     b, part * 32 : (part + 1) * 32, :
                 ].astype(F32)
-            stage_out[step] = sources[a][b, 128:160, :].astype(F32)
-            if own:
-                hot_rows[pl.ds(pl.multiple_of(chunk * 16, 16), 16), :] = sources[a][b, 160:CHUNK, :]
+            stage_out[step] = sources[i][b, 128:160, :].astype(F32)
             rows = pl.ds(pl.multiple_of(chunk * 32, 32), 32)
             here = [
                 pltpu.make_async_copy(stage_in.at[step], win_ref.at[layer, rows], sems.at[step, 0]),
@@ -532,38 +518,61 @@
             for copy in here:
                 copy.start()
             copies += here
-    if own:
-        col = lax.axis_index("col")
-        pick = jnp.where(
-            lax.broadcasted_iota(I32, (COLS, D), 1) == lax.broadcasted_iota(I32, (COLS, D), 0) + col * COLS,
-            1.0,
-            0.0,
-        ).astype(BF16)
-        hot_ref[...] = mm(pick, hot_rows[...], NT)
     for copy in copies:
         copy.wait()
 
 
-def finish(own, sources, *partial):
-    shapes = (
-        jax.ShapeDtypeStruct((LAYERS, D, 4 * D), F32),
-        jax.ShapeDtypeStruct((LAYERS, D, D), F32),
-    )
-    scratch = [pltpu.VMEM((16, 32, 4 * D), F32), pltpu.VMEM((16, 32, D), F32)]
-    if own:
-        shapes += (jax.ShapeDtypeStruct((COLS, HOT), F32),)
-        scratch += [pltpu.VMEM((HOT, D), BF16)]
-    return pl.pallas_call(
-        functools.partial(finish_kernel, own),
-        out_shape=shapes,
-        in_specs=vmem(4) + [ANY] * len(partial),
-        out_specs=(ANY, ANY) + tuple(vmem(1) if own else ()),
-        scratch_shapes=scratch + [pltpu.SemaphoreType.DMA((16, 2))],
-        input_output_aliases={} if own else {4: 0, 5: 1},
-        compiler_params=params(),
-        cost_estimate=cost(4),
-        name="finish_own" if own else "finish_other",
+def finish(sources, pieces, partial=()):
+    steps = 4 * len(pieces)
+    return pl.pallas_call(
+        functools.partial(finish_kernel, pieces, not partial),
+        out_shape=(
+            jax.ShapeDtypeStruct((LAYERS, D, 4 * D), F32),
+            jax.ShapeDtypeStruct((LAYERS, D, D), F32),
+        ),
+        in_specs=vmem(len(pieces)) + [ANY] * len(partial),
+        out_specs=(ANY, ANY),
+        scratch_shapes=[
+            pltpu.VMEM((steps, 32, 4 * D), F32),
+            pltpu.VMEM((steps, 32, D), F32),
+            pltpu.SemaphoreType.DMA((steps, 2)),
+        ],
+        input_output_aliases={len(pieces): 0, len(pieces) + 1: 1} if partial else {},
+        compiler_params=params(6 + 3 * len(pieces)),
+        cost_estimate=cost(0.5 + 0.6 * len(pieces)),
+        name="widen_sums",
     )(*sources, *partial)
+
+
+def hot_kernel(*refs):
+    sources, hot_ref, rows = refs[:4], refs[4], refs[5]
+    (x, y, z), core = places()
+    col = lax.axis_index("col")
+    first = jnp.where(core == 0, x, y)
+    second = jnp.where(core == 0, y, z)
+    for a in range(4):
+        for b in range(4):
+            chunk = 4 * ((a + first) & 3) + ((b + second) & 3)
+            rows[pl.ds(pl.multiple_of(chunk * 16, 16), 16), :] = sources[a][b]
+    pick = jnp.where(
+        lax.broadcasted_iota(I32, (COLS, D), 1) == lax.broadcasted_iota(I32, (COLS, D), 0) + col * COLS,
+        1.0,
+        0.0,
+    ).astype(BF16)
+    hot_ref[...] = mm(pick, rows[...], NT)
+
+
+def hot_sums(mine):
+    return pl.pallas_call(
+        hot_kernel,
+        out_shape=jax.ShapeDtypeStruct((COLS, HOT), F32),
+        in_specs=vmem(4),
+        out_specs=vmem(1)[0],
+        scratch_shapes=[pltpu.VMEM((HOT, D), BF16)],
+        compiler_params=params(8),
+        cost_estimate=cost(1),
+        name="hot_sums",
+    )(*[value[:, 160:CHUNK] for value in mine]).T
 
 
 def on_device(
@@ -581,7 +590,7 @@
     outs = run_stack(index, emb, weight_in, weight_out, segment, cotangent)
     encoded, grad_emb, keep, send = outs[0], outs[1], outs[2:6], outs[6:10]
 
-    def gather_columns():
+    def gather_columns(grad_emb):
         return lax.all_to_all(grad_emb, "col", split_axis=0, concat_axis=0, tiled=True)
 
     def send_back(columns):
@@ -593,12 +602,10 @@
     def scatter(incoming):
         return scatter_rows(received, incoming)
 
-    mine, other, table_grad = sum_everywhere(
-        keep, send, gather_columns, send_back, exchange, scatter
+    grad_in, grad_out, hot_grad, table_grad = sum_everywhere(
+        keep, send, grad_emb, gather_columns, send_back, exchange, scatter
     )
-    grad_in, grad_out, hot_grad = finish(True, mine)
-    grad_in, grad_out = finish(False, other, grad_in, grad_out)
-    return (encoded, table_grad, hot_grad.T, grad_in, grad_out)
+    return (encoded, table_grad, hot_grad, grad_in, grad_out)
 
 
 def solution(mesh):

time: 171 us -> 157 us (0.918)
  Pallas kernels: 54.2 us -> 47.6 us
  local copies, waits for them, and re-layouts: 4.18 us -> 0.43 us
  starting transfers between devices: 37.9 us -> 41.5 us
  other arithmetic: 4.2 us -> 1.33 us
  waiting for transfers between devices: 41 us -> 38.4 us
    ppermute x15, waiting for transfers between devices: 33.5 us -> 27.9 us  [along(): return lax.ppermute(value, BOTH, device_pairs(move))]
    ppermute x15, starting transfers between devices: 15.1 us -> 18.5 us  [along(): return lax.ppermute(value, BOTH, device_pairs(move))]
    convert_element_type x6, other arithmetic: 4.11 us -> 1.24 us  [add_all(): return terms[0].astype(BF16)]
    unnamed x30 -> x14, local copies, waits for them, and re-layouts: 2.48 us -> 0.03 us
    ppermute x8, starting transfers between devices: 6.4 us -> 3.98 us  [to_core(): lax.ppermute(value, BOTH, device_pairs(lambda z, y, x, c: (z, y, x, 1 - c)))]
    pallas_call x1, Pallas kernels: 16 us -> 13.9 us  [run_stack(): pl.pallas_call(stack_kernel, out_shape=(jax.ShapeDtypeStruct((TOK, D), BF...]
    pallas_call x1, Pallas kernels: 8.79 us -> 7 us  [pick_rows(): pl.pallas_call(pick_kernel, out_shape=jax.ShapeDtypeStruct((N_SEQ, 128, 1...]
    pallas_call x2 -> x4, Pallas kernels: 9.39 us -> 7.85 us  [the longest x3 6.98 us: finish(): pl.pallas_call(functools.partial(finish_kernel, pieces, not partial), out...]
  transfers between devices with their start and end apart: 26 -> 26, of which waited for: 14 -> 13; matrix products, arithmetic and copies ran while one was open for 3% -> 1% of each run, Pallas kernels for 11% -> 12%
where the time goes in v3:
time: 157 us; the launch traced here: 156 us
  Pallas kernels  47.6 us (30%)
  starting transfers between devices  41.5 us (26%)
  waiting for transfers between devices  38.4 us (24%)
  blocking collectives  26.2 us (17%)
    ppermute x15, waiting for transfers between devices, along(): return lax.ppermute(value, BOTH, device_pairs(move))  27.9 us
    ppermute x15, starting transfers between devices, along(): return lax.ppermute(value, BOTH, device_pairs(move))  18.5 us
    pallas_call x1, Pallas kernels, run_stack(): pl.pallas_call(stack_kernel, out_shape=(jax.ShapeDtypeStruct((TOK, D), BF...  13.9 us
    all_to_all x1, blocking collectives, on_device(): emb = lax.all_to_all(placed, 'col', split_axis=0, concat_axis=0, tiled=True)  13.6 us
    all_to_all x1, blocking collectives, on_device(): lax.all_to_all(picked, 'seq', split_axis=0, concat_axis=0, tiled=True)  12.6 us
    pallas_call x1, Pallas kernels, scatter_rows(): pl.pallas_call(scatter_kernel, out_shape=jax.ShapeDtypeStruct((COLS, ITEM...  9.65 us
    all_to_all x1, starting transfers between devices, on_device(): lax.all_to_all(requests, 'seq', split_axis=0, concat_axis=0, tiled=True)  8.6 us
    pallas_call x1, Pallas kernels, pick_rows(): pl.pallas_call(pick_kernel, out_shape=jax.ShapeDtypeStruct((N_SEQ, 128, 1...  7 us
  transfers between devices with their start and end apart: 26, of which 13 were waited for; matrix products, arithmetic and copies ran while one was open for 1% of the time, Pallas kernels for 12%

profile of v3, /device:TPU:1, one launch (start us, length us, event | category | flops | bytes accessed | tf_op | source)
XLA Modules:
  0.0 156.5 jit_solution(13532630279078046849)
XLA Ops:
  0.6 2.5 %slots.1 = (s32[16,2,128]{2,1,0:T(2,128)}, s32[8,2,128]{2,1,0:T(2,128)}) custom-call(s32[1,2048]{1,0:T(1,128)} %bitcast.31, s32[1,2048]{1,0:T(1,128)} %bitcast.32, s32[1,2048]{1,0:T(1,128)} %bitcast.33, s32[1,2048]{1,0:T(1,128)} %bitcast.34), custom_call_target="tpu_custom_call" | custom-call | flops 2750000128 | bytes 9000000 | tf_op jit(solution)/shard_map/slots/pallas_call | solution.py:96
  3.1 8.6 %all-to-all-start = ((s32[16,2,128]{2,1,0:T(2,128)}), s32[16,2,128]{2,1,0:T(2,128)S(1)}, u32[]{:S(2)}, u32[]{:S(2)}) async-start(s32[16,2,128]{2,1,0:T(2,128)} %get-tuple-element.32), calls=%async_computation | async-start | bytes 32768 | tf_op jit(solution)/shard_map/all_to_all | solution.py:585
  11.7 0.3 copy.20.table_ref
  12.1 6.1 %all-to-all-done = s32[16,2,128]{2,1,0:T(2,128)S(1)} async-done(((s32[16,2,128]{2,1,0:T(2,128)}), s32[16,2,128]{2,1,0:T(2,128)S(1)}, u32[]{:S(2)}, u32[]{:S(2)}) %all-to-all-start) | async-done | bytes 16416 | tf_op jit(solution)/shard_map/all_to_all | solution.py:585
  18.2 7.0 %pick_rows.1 = bf16[16,128,128]{2,1,0:T(8,128)(2,1)S(1)} custom-call(s32[4096]{0:T(1024)S(1)} %bitcast.22, f32[4096,64]{1,0:T(8,128)S(1)} %copy.20.table_ref), custom_call_target="tpu_custom_call" | custom-call | flops 7699999744 | bytes 25200000 | tf_op jit(solution)/shard_map/pick_rows/pallas_call | solution.py:139
  25.2 12.6 %all_to_all.25.returned_ref = bf16[16,128,128]{2,1,0:T(8,128)(2,1)S(1)} all-to-all(bf16[16,128,128]{2,1,0:T(8,128)(2,1)S(1)} %pick_rows.1), channel_id=1, replica_groups=mesh['seq'=16,'col'=8] {'seq'}, dimensions={0} | all-to-all | bytes 1048576 | tf_op jit(solution)/shard_map/all_to_all | solution.py:587
  37.8 2.9 %place_rows.1 = bf16[8,128,128]{2,1,0:T(8,128)(2,1)S(1)} custom-call(s32[2048]{0:T(1024)S(1)} %bitcast.25, bf16[16,128,128]{2,1,0:T(8,128)(2,1)S(1)} %all_to_all.25.returned_ref, bf16[64,256]{1,0:T(8,128)(2,1)S(1)} %bitcast.24), custom_call_target="tpu_custom_call" | custom-call | flops 4400000000 | bytes 14400000 | tf_op jit(solution)/shard_map/place_rows/pallas_call | solution.py:167
  40.8 13.6 %all_to_all.26.emb_ref = bf16[8,128,128]{2,1,0:T(8,128)(2,1)S(1)} all-to-all(bf16[8,128,128]{2,1,0:T(8,128)(2,1)S(1)} %place_rows.1), channel_id=1, replica_groups=mesh['seq'=16,'col'=8] {'col'}, dimensions={0} | all-to-all | bytes 524288 | tf_op jit(solution)/shard_map/all_to_all | solution.py:589
  54.4 13.9 %layers.1 = (bf16[256,512]{1,0:T(8,128)(2,1)}, bf16[8,128,128]{2,1,0:T(8,128)(2,1)}, bf16[4,176,512]{2,1,0:T(8,128)(2,1)S(1)}, bf16[4,176,512]{2,1,0:T(8,128)(2,...) custom-call(s32[8,2,128]{2,1,0:T(2,128)S(1)} %copy-done.5, ...), custom_call_target="tpu_custom_call" | custom-call | flops 17600000000 | bytes 57600000 | tf_op jit(solution)/shard_map/layers/pallas_call | solution.py:401
  68.3 1.1 collective-permute-start.1
  69.5 0.4 collective-permute-start.5
  70.0 1.2 collective-permute-done.1
  71.3 0.2 add_convert_fusion.3
  71.4 0.6 collective-permute-start.2
  72.0 0.3 collective-permute-done.3
  72.5 0.3 collective-permute-start.4
  72.8 0.5 collective-permute-done.5
  73.5 2.0 %collective-permute-start.6 = (bf16[4,176,512]{2,1,0:T(8,128)(2,1)S(1)}, bf16[4,176,512]{2,1,0:T(8,128)(2,1)S(1)}, u32[]{:S(2)}, u32[]{:S(2)}) collective-permute-start(bf16[4,176,512]{2,1,0:T(8,128)(2,1)S(1)} %add_convert_fusion.1), channel_id=1, source_target_pairs={{0,6},{1,25},{2,0},{3,27},{4,2},{5,29},{6,4},{7,31},{8,14},{9,1},{... | collective-permute-start | bytes 2162696 | tf_op jit(solution)/shard_map/ppermute | solution.py:458
  75.5 8.0 %collective-permute-done.2 = bf16[4,176,512]{2,1,0:T(8,128)(2,1)S(1)} collective-permute-done((bf16[4,176,512]{2,1,0:T(8,128)(2,1)S(1)}, bf16[4,176,512]{2,1,0:T(8,128)(2,1)S(1)}, u32[]{:S(2)}, u32[]{:S(2)}) %collective-permute-start.2) | collective-permute-done | bytes 720928 | tf_op jit(solution)/shard_map/ppermute | solution.py:458
  83.5 7.7 %collective-permute-done.4 = bf16[4,176,512]{2,1,0:T(8,128)(2,1)S(1)} collective-permute-done((bf16[4,176,512]{2,1,0:T(8,128)(2,1)S(1)}, bf16[4,176,512]{2,1,0:T(8,128)(2,1)S(1)}, u32[]{:S(2)}, u32[]{:S(2)}) %collective-permute-start.4) | collective-permute-done | bytes 720928 | tf_op jit(solution)/shard_map/ppermute | solution.py:458
  91.2 0.5 add_convert_fusion
  91.7 0.7 collective-permute-start.7
  92.4 1.3 collective-permute-start.9
  93.9 5.7 %all-to-all-start.3 = ((bf16[8,128,128]{2,1,0:T(8,128)(2,1)}), bf16[8,128,128]{2,1,0:T(8,128)(2,1)S(1)}, u32[]{:S(2)}, u32[]{:S(2)}) async-start(bf16[8,128,128]{2,1,0:T(8,128)(2,1)} %get-tuple-element.44), calls=%async_computation.3 | async-start | bytes 524288 | tf_op jit(solution)/shard_map/all_to_all | solution.py:594
  99.7 2.7 %collective-permute-start.12 = (bf16[176,512]{1,0:T(8,128)(2,1)S(1)}, bf16[176,512]{1,0:T(8,128)(2,1)S(1)}, u32[]{:S(2)}, u32[]{:S(2)}) collective-permute-start(bf16[176,512]{1,0:T(8,128)(2,1)S(1)} %fusion.1), channel_id=1, source_target_pairs={{0,96},{1,7},{2,98},{3,1},{4,100},{5,3},{6,102},{7,5},{8,104},{9,1... | collective-permute-start | bytes 540680 | tf_op jit(solution)/shard_map/ppermute | solution.py:458
  102.4 1.7 %collective-permute-start.10 = (bf16[176,512]{1,0:T(8,128)(2,1)S(1)}, bf16[176,512]{1,0:T(8,128)(2,1)S(1)}, u32[]{:S(2)}, u32[]{:S(2)}) collective-permute-start(bf16[176,512]{1,0:T(8,128)(2,1)S(1)} %fusion.1), channel_id=1, source_target_pairs={{0,64},{1,5},{2,66},{3,7},{4,68},{5,1},{6,70},{7,3},{8,72},{9,13},... | collective-permute-start | bytes 540680 | tf_op jit(solution)/shard_map/ppermute | solution.py:458
  104.1 2.1 %all-to-all-done.3.grad_ref = bf16[8,128,128]{2,1,0:T(8,128)(2,1)S(1)} async-done(((bf16[8,128,128]{2,1,0:T(8,128)(2,1)}), bf16[8,128,128]{2,1,0:T(8,128)(2,1)S(1)}, u32[]{:S(2)}, u32[]{:S(2)}) %all-to-all-start.3) | async-done | bytes 262176 | tf_op jit(solution)/shard_map/all_to_all | solution.py:594
  106.2 3.8 %return_rows.1 = bf16[16,128,128]{2,1,0:T(8,128)(2,1)} custom-call(s32[2048]{0:T(1024)S(1)} %bitcast.26, bf16[8,128,128]{2,1,0:T(8,128)(2,1)S(1)} %all-to-all-done.3.grad_ref), custom_call_target="tpu_custom_call" | custom-call | flops 4400000000 | bytes 14400000 | tf_op jit(solution)/shard_map/return_rows/pallas_call | solution.py:195
  110.0 4.6 %all-to-all-start.4 = ((bf16[16,128,128]{2,1,0:T(8,128)(2,1)}), bf16[16,128,128]{2,1,0:T(8,128)(2,1)S(1)}, u32[]{:S(2)}, u32[]{:S(2)}) async-start(bf16[16,128,128]{2,1,0:T(8,128)(2,1)} %return_rows.1), calls=%async_computation.4 | async-start | bytes 1048576 | tf_op jit(solution)/shard_map/all_to_all | solution.py:600
  114.8 1.4 collective-permute-start.15
  116.2 2.4 %collective-permute-start.14 = (bf16[176,512]{1,0:T(8,128)(2,1)S(1)}, bf16[176,512]{1,0:T(8,128)(2,1)S(1)}, u32[]{:S(2)}, u32[]{:S(2)}) collective-permute-start(bf16[176,512]{1,0:T(8,128)(2,1)S(1)} %add_convert_fusion.5), channel_id=1, source_target_pairs={{0,16},{1,65},{2,18},{3,67},{4,20},{5,69},{6,22},{7,71},{8,24},{9,... | collective-permute-start | bytes 540680 | tf_op jit(solution)/shard_map/ppermute | solution.py:458
  118.6 1.2 collective-permute-start.13
  119.8 5.4 %collective-permute-done.15 = bf16[176,512]{1,0:T(8,128)(2,1)S(1)} collective-permute-done((bf16[176,512]{1,0:T(8,128)(2,1)S(1)}, bf16[176,512]{1,0:T(8,128)(2,1)S(1)}, u32[]{:S(2)}, u32[]{:S(2)}) %collective-permute-start.15) | collective-permute-done | bytes 180256 | tf_op jit(solution)/shard_map/ppermute | solution.py:458
  125.2 3.3 %collective-permute-done.14 = bf16[176,512]{1,0:T(8,128)(2,1)S(1)} collective-permute-done((bf16[176,512]{1,0:T(8,128)(2,1)S(1)}, bf16[176,512]{1,0:T(8,128)(2,1)S(1)}, u32[]{:S(2)}, u32[]{:S(2)}) %collective-permute-start.14) | collective-permute-done | bytes 180256 | tf_op jit(solution)/shard_map/ppermute | solution.py:458
  128.6 0.5 collective-permute-start.19
  129.1 0.7 collective-permute-start.18
  129.8 2.2 %collective-permute-start.17 = (bf16[4,176,512]{2,1,0:T(8,128)(2,1)S(1)}, bf16[4,176,512]{2,1,0:T(8,128)(2,1)S(1)}, u32[]{:S(2)}, u32[]{:S(2)}) collective-permute-start(bf16[4,176,512]{2,1,0:T(8,128)(2,1)S(1)} %pad_maximum_fusion.refs_0_), channel_id=1, source_target_pairs={{0,4},{1,17},{2,6},{3,19},{4,0},{5,21},{6,2},{7,23},{8,12},{9,25},... | collective-permute-start | bytes 2162696 | tf_op jit(solution)/shard_map/ppermute | solution.py:458
  132.0 1.2 collective-permute-start.16
  133.2 9.6 %scatter_rows.1 = f32[64,4096]{1,0:T(8,128)} custom-call(s32[4096]{0:T(1024)S(1)} %bitcast.23, bf16[16,128,128]{2,1,0:T(8,128)(2,1)S(1)} %all-to-all-done.4.incoming_ref), custom_call_target="tpu_custom_call" | custom-call | flops 12099999744 | bytes 39600000 | tf_op jit(solution)/shard_map/scatter_rows/pallas_call | solution.py:236
  142.8 2.7 %widen_sums.3 = (f32[2,512,2048]{2,1,0:T(8,128)}, f32[2,512,512]{2,1,0:T(8,128)}) custom-call(bf16[4,176,512]{2,1,0:T(8,128)(2,1)S(1)} %pad_maximum_fusion.refs_0_, bf16[4,176,512]{2,1,0:T(8,128)(2,1)} %collective-permute-done.19.refs_1_), custom_call_target="tpu_custom_call" | custom-call | flops 1870000000 | bytes 6120000 | tf_op jit(solution)/shard_map/widen_sums/pallas_call | solution.py:527
  145.6 2.9 %collective-permute-done.17.refs_1_ = bf16[4,176,512]{2,1,0:T(8,128)(2,1)S(1)} collective-permute-done((bf16[4,176,512]{2,1,0:T(8,128)(2,1)S(1)}, bf16[4,176,512]{2,1,0:T(8,128)(2,1)S(1)}, u32[]{:S(2)}, u32[]{:S(2)}) %collective-permute-start.17) | collective-permute-done | bytes 720928 | tf_op jit(solution)/shard_map/ppermute | solution.py:458
  148.5 0.6 collective-permute-done.16.refs_0_
  149.1 1.2 collective-permute-start.20
  150.3 0.5 collective-permute-start.22
  150.9 0.9 hot_sums.1
  151.7 2.1 %widen_sums.4 = (f32[2,512,2048]{2,1,0:T(8,128)}, f32[2,512,512]{2,1,0:T(8,128)}) custom-call(bf16[4,176,512]{2,1,0:T(8,128)(2,1)S(1)} %collective-permute-done.16.refs_0_, bf16[4,176,512]{2,1,0:T(8,128)(2,1)S(1)} %collective-permute-done.17.refs_1_, ...), custom_call_target="tpu_custom_call", output_to_operand_aliasing={{0}: (3, {}), {1}: (4, {})} | custom-call | flops 2529999872 | bytes 8279999 | tf_op jit(solution)/shard_map/widen_sums/pallas_call | solution.py:527
  153.9 0.3 collective-permute-done.22.refs_2_
  154.2 2.1 %widen_sums.5 = (f32[2,512,2048]{2,1,0:T(8,128)}, f32[2,512,512]{2,1,0:T(8,128)}) custom-call(bf16[4,176,512]{2,1,0:T(8,128)(2,1)S(1)} %collective-permute-done.20.refs_0_, bf16[4,176,512]{2,1,0:T(8,128)(2,1)S(1)} %collective-permute-done.21.refs_1_, ...), custom_call_target="tpu_custom_call", output_to_operand_aliasing={{0}: (3, {}), {1}: (4, {})} | custom-call | flops 2529999872 | bytes 8279999 | tf_op jit(solution)/shard_map/widen_sums/pallas_call | solution.py:527
  (43 shorter events, 1.2 us)
Async XLA Ops:
  0.6 11.1 %copy-start.6 = (bf16[4096,64]{0,1:T(8,128)(2,1)S(1)}, bf16[4096,64]{0,1:T(8,128)(2,1)}, u32[]{:S(2)}) copy-start(bf16[4096,64]{0,1:T(8,128)(2,1)} %param.10) | copy-start | bytes 1572868
  3.1 15.0 %all-to-all-start = ((s32[16,2,128]{2,1,0:T(2,128)}), s32[16,2,128]{2,1,0:T(2,128)S(1)}, u32[]{:S(2)}, u32[]{:S(2)}) async-start(s32[16,2,128]{2,1,0:T(2,128)} %get-tuple-element.32), calls=%async_computation | async-start | bytes 32768 | tf_op jit(solution)/shard_map/all_to_all | solution.py:585
  18.2 19.6 %copy-start.3 = (bf16[256,64]{0,1:T(8,128)(2,1)S(1)}, bf16[256,64]{0,1:T(8,128)(2,1)}, u32[]{:S(2)}) copy-start(bf16[256,64]{0,1:T(8,128)(2,1)} %param.11) | copy-start | bytes 98308
  18.2 19.6 %copy-start.5 = (s32[8,2,128]{2,1,0:T(2,128)S(1)}, s32[8,2,128]{2,1,0:T(2,128)}, u32[]{:S(2)}) copy-start(s32[8,2,128]{2,1,0:T(2,128)} %get-tuple-element.31.index_ref) | copy-start | bytes 24580
  37.8 16.6 %copy-start = (bf16[2,512,2048]{2,1,0:T(8,128)(2,1)S(1)}, bf16[2,512,2048]{2,1,0:T(8,128)(2,1)}, u32[]{:S(2)}) copy-start(bf16[2,512,2048]{2,1,0:T(8,128)(2,1)} %win_ref.1) | copy-start | bytes 12582916
  37.8 16.6 %copy-start.1 = (bf16[2,512,512]{2,1,0:T(8,128)(2,1)S(1)}, bf16[2,512,512]{2,1,0:T(8,128)(2,1)}, u32[]{:S(2)}) copy-start(bf16[2,512,512]{2,1,0:T(8,128)(2,1)} %wout_ref.1) | copy-start | bytes 3145732
  37.8 16.6 %copy-start.2 = (bf16[256,512]{1,0:T(8,128)(2,1)S(1)}, bf16[256,512]{1,0:T(8,128)(2,1)}, u32[]{:S(2)}) copy-start(bf16[256,512]{1,0:T(8,128)(2,1)} %cot_ref.1) | copy-start | bytes 786436
  37.8 16.6 %copy-start.4 = (s32[1,256]{1,0:T(1,128)S(1)}, s32[1,256]{1,0:T(1,128)}, u32[]{:S(2)}) copy-start(s32[1,256]{1,0:T(1,128)} %segment_ref.1) | copy-start | bytes 3076
  68.3 3.0 %collective-permute-start.1 = (bf16[4,176,512]{2,1,0:T(8,128)(2,1)S(1)}, bf16[4,176,512]{2,1,0:T(8,128)(2,1)S(1)}, u32[]{:S(2)}, u32[]{:S(2)}) collective-permute-start(bf16[4,176,512]{2,1,0:T(8,128)(2,1)S(1)} %get-tuple-element.37), channel_id=1, source_target_pairs={{0,1},{1,0},{2,3},{3,2},{4,5},{5,4},{6,7},{7,6},{8,9},{9,8},{10,11... | collective-permute-start | bytes 2162696 | tf_op jit(solution)/shard_map/ppermute | solution.py:448
  69.4 2.8 %collective-permute-start.3 = (bf16[4,176,512]{2,1,0:T(8,128)(2,1)S(1)}, bf16[4,176,512]{2,1,0:T(8,128)(2,1)S(1)}, u32[]{:S(2)}, u32[]{:S(2)}) collective-permute-start(bf16[4,176,512]{2,1,0:T(8,128)(2,1)S(1)} %get-tuple-element.39), channel_id=1, source_target_pairs={{0,1},{1,0},{2,3},{3,2},{4,5},{5,4},{6,7},{7,6},{8,9},{9,8},{10,11... | collective-permute-start | bytes 2162696 | tf_op jit(solution)/shard_map/ppermute | solution.py:448
  69.5 3.8 %collective-permute-start.5 = (bf16[4,176,512]{2,1,0:T(8,128)(2,1)S(1)}, bf16[4,176,512]{2,1,0:T(8,128)(2,1)S(1)}, u32[]{:S(2)}, u32[]{:S(2)}) collective-permute-start(bf16[4,176,512]{2,1,0:T(8,128)(2,1)S(1)} %get-tuple-element.41), channel_id=1, source_target_pairs={{0,1},{1,0},{2,3},{3,2},{4,5},{5,4},{6,7},{7,6},{8,9},{9,8},{10,11... | collective-permute-start | bytes 2162696 | tf_op jit(solution)/shard_map/ppermute | solution.py:448
  69.9 5.5 %collective-permute-start = (bf16[4,176,512]{2,1,0:T(8,128)(2,1)S(1)}, bf16[4,176,512]{2,1,0:T(8,128)(2,1)S(1)}, u32[]{:S(2)}, u32[]{:S(2)}) collective-permute-start(bf16[4,176,512]{2,1,0:T(8,128)(2,1)S(1)} %get-tuple-element.35), channel_id=1, source_target_pairs={{0,1},{1,0},{2,3},{3,2},{4,5},{5,4},{6,7},{7,6},{8,9},{9,8},{10,11... | collective-permute-start | bytes 2162696 | tf_op jit(solution)/shard_map/ppermute | solution.py:448
  71.4 12.1 %collective-permute-start.2 = (bf16[4,176,512]{2,1,0:T(8,128)(2,1)S(1)}, bf16[4,176,512]{2,1,0:T(8,128)(2,1)S(1)}, u32[]{:S(2)}, u32[]{:S(2)}) collective-permute-start(bf16[4,176,512]{2,1,0:T(8,128)(2,1)S(1)} %add_convert_fusion.3), channel_id=1, source_target_pairs={{0,4},{1,17},{2,6},{3,19},{4,0},{5,21},{6,2},{7,23},{8,12},{9,25},... | collective-permute-start | bytes 2162696 | tf_op jit(solution)/shard_map/ppermute | solution.py:458
  72.5 18.7 %collective-permute-start.4 = (bf16[4,176,512]{2,1,0:T(8,128)(2,1)S(1)}, bf16[4,176,512]{2,1,0:T(8,128)(2,1)S(1)}, u32[]{:S(2)}, u32[]{:S(2)}) collective-permute-start(bf16[4,176,512]{2,1,0:T(8,128)(2,1)S(1)} %add_convert_fusion.2), channel_id=1, source_target_pairs={{0,2},{1,9},{2,4},{3,11},{4,6},{5,13},{6,0},{7,15},{8,10},{9,17},{... | collective-permute-start | bytes 2162696 | tf_op jit(solution)/shard_map/ppermute | solution.py:458
  73.5 17.7 %collective-permute-start.6 = (bf16[4,176,512]{2,1,0:T(8,128)(2,1)S(1)}, bf16[4,176,512]{2,1,0:T(8,128)(2,1)S(1)}, u32[]{:S(2)}, u32[]{:S(2)}) collective-permute-start(bf16[4,176,512]{2,1,0:T(8,128)(2,1)S(1)} %add_convert_fusion.1), channel_id=1, source_target_pairs={{0,6},{1,25},{2,0},{3,27},{4,2},{5,29},{6,4},{7,31},{8,14},{9,1},{... | collective-permute-start | bytes 2162696 | tf_op jit(solution)/shard_map/ppermute | solution.py:458
  91.7 7.9 %collective-permute-start.7 = (bf16[176,512]{1,0:T(8,128)(2,1)S(1)}, bf16[176,512]{1,0:T(8,128)(2,1)S(1)}, u32[]{:S(2)}, u32[]{:S(2)}) collective-permute-start(bf16[176,512]{1,0:T(8,128)(2,1)S(1)} %get-tuple-element.57), channel_id=1, source_target_pairs={{0,16},{1,65},{2,18},{3,67},{4,20},{5,69},{6,22},{7,71},{8,24},{9,... | collective-permute-start | bytes 540680 | tf_op jit(solution)/shard_map/ppermute | solution.py:458
  92.4 7.2 %collective-permute-start.9 = (bf16[176,512]{1,0:T(8,128)(2,1)S(1)}, bf16[176,512]{1,0:T(8,128)(2,1)S(1)}, u32[]{:S(2)}, u32[]{:S(2)}) collective-permute-start(bf16[176,512]{1,0:T(8,128)(2,1)S(1)} %get-tuple-element.58), channel_id=1, source_target_pairs={{0,24},{1,97},{2,26},{3,99},{4,28},{5,101},{6,30},{7,103},{8,0},{9... | collective-permute-start | bytes 540680 | tf_op jit(solution)/shard_map/ppermute | solution.py:458
  93.7 5.9 %collective-permute-start.8 = (bf16[176,512]{1,0:T(8,128)(2,1)S(1)}, bf16[176,512]{1,0:T(8,128)(2,1)S(1)}, u32[]{:S(2)}, u32[]{:S(2)}) collective-permute-start(bf16[176,512]{1,0:T(8,128)(2,1)S(1)} %get-tuple-element.59), channel_id=1, source_target_pairs={{0,8},{1,33},{2,10},{3,35},{4,12},{5,37},{6,14},{7,39},{8,16},{9,4... | collective-permute-start | bytes 540680 | tf_op jit(solution)/shard_map/ppermute | solution.py:458
  93.9 12.4 %all-to-all-start.3 = ((bf16[8,128,128]{2,1,0:T(8,128)(2,1)}), bf16[8,128,128]{2,1,0:T(8,128)(2,1)S(1)}, u32[]{:S(2)}, u32[]{:S(2)}) async-start(bf16[8,128,128]{2,1,0:T(8,128)(2,1)} %get-tuple-element.44), calls=%async_computation.3 | async-start | bytes 524288 | tf_op jit(solution)/shard_map/all_to_all | solution.py:594
  99.7 14.9 %collective-permute-start.12 = (bf16[176,512]{1,0:T(8,128)(2,1)S(1)}, bf16[176,512]{1,0:T(8,128)(2,1)S(1)}, u32[]{:S(2)}, u32[]{:S(2)}) collective-permute-start(bf16[176,512]{1,0:T(8,128)(2,1)S(1)} %fusion.1), channel_id=1, source_target_pairs={{0,96},{1,7},{2,98},{3,1},{4,100},{5,3},{6,102},{7,5},{8,104},{9,1... | collective-permute-start | bytes 540680 | tf_op jit(solution)/shard_map/ppermute | solution.py:458
  102.4 12.3 %collective-permute-start.11 = (bf16[176,512]{1,0:T(8,128)(2,1)S(1)}, bf16[176,512]{1,0:T(8,128)(2,1)S(1)}, u32[]{:S(2)}, u32[]{:S(2)}) collective-permute-start(bf16[176,512]{1,0:T(8,128)(2,1)S(1)} %fusion.1), channel_id=1, source_target_pairs={{0,32},{1,3},{2,34},{3,5},{4,36},{5,7},{6,38},{7,1},{8,40},{9,11},... | collective-permute-start | bytes 540680 | tf_op jit(solution)/shard_map/ppermute | solution.py:458
  102.4 12.3 %collective-permute-start.10 = (bf16[176,512]{1,0:T(8,128)(2,1)S(1)}, bf16[176,512]{1,0:T(8,128)(2,1)S(1)}, u32[]{:S(2)}, u32[]{:S(2)}) collective-permute-start(bf16[176,512]{1,0:T(8,128)(2,1)S(1)} %fusion.1), channel_id=1, source_target_pairs={{0,64},{1,5},{2,66},{3,7},{4,68},{5,1},{6,70},{7,3},{8,72},{9,13},... | collective-permute-start | bytes 540680 | tf_op jit(solution)/shard_map/ppermute | solution.py:458
  110.0 23.2 %all-to-all-start.4 = ((bf16[16,128,128]{2,1,0:T(8,128)(2,1)}), bf16[16,128,128]{2,1,0:T(8,128)(2,1)S(1)}, u32[]{:S(2)}, u32[]{:S(2)}) async-start(bf16[16,128,128]{2,1,0:T(8,128)(2,1)} %return_rows.1), calls=%async_computation.4 | async-start | bytes 1048576 | tf_op jit(solution)/shard_map/all_to_all | solution.py:600
  114.8 10.4 %collective-permute-start.15 = (bf16[176,512]{1,0:T(8,128)(2,1)S(1)}, bf16[176,512]{1,0:T(8,128)(2,1)S(1)}, u32[]{:S(2)}, u32[]{:S(2)}) collective-permute-start(bf16[176,512]{1,0:T(8,128)(2,1)S(1)} %add_convert_fusion.5), channel_id=1, source_target_pairs={{0,8},{1,33},{2,10},{3,35},{4,12},{5,37},{6,14},{7,39},{8,16},{9,4... | collective-permute-start | bytes 540680 | tf_op jit(solution)/shard_map/ppermute | solution.py:458
  116.2 12.3 %collective-permute-start.14 = (bf16[176,512]{1,0:T(8,128)(2,1)S(1)}, bf16[176,512]{1,0:T(8,128)(2,1)S(1)}, u32[]{:S(2)}, u32[]{:S(2)}) collective-permute-start(bf16[176,512]{1,0:T(8,128)(2,1)S(1)} %add_convert_fusion.5), channel_id=1, source_target_pairs={{0,16},{1,65},{2,18},{3,67},{4,20},{5,69},{6,22},{7,71},{8,24},{9,... | collective-permute-start | bytes 540680 | tf_op jit(solution)/shard_map/ppermute | solution.py:458
  118.6 9.9 %collective-permute-start.13 = (bf16[176,512]{1,0:T(8,128)(2,1)S(1)}, bf16[176,512]{1,0:T(8,128)(2,1)S(1)}, u32[]{:S(2)}, u32[]{:S(2)}) collective-permute-start(bf16[176,512]{1,0:T(8,128)(2,1)S(1)} %add_convert_fusion.5), channel_id=1, source_target_pairs={{0,24},{1,97},{2,26},{3,99},{4,28},{5,101},{6,30},{7,103},{8,0},{9... | collective-permute-start | bytes 540680 | tf_op jit(solution)/shard_map/ppermute | solution.py:458
  128.6 14.2 %collective-permute-start.19 = (bf16[4,176,512]{2,1,0:T(8,128)(2,1)S(1)}, bf16[4,176,512]{2,1,0:T(8,128)(2,1)}, u32[]{:S(2)}, u32[]{:S(2)}) collective-permute-start(bf16[4,176,512]{2,1,0:T(8,128)(2,1)S(1)} %pad_maximum_fusion.refs_0_), channel_id=1, source_target_pairs={{0,1},{1,0},{2,3},{3,2},{4,5},{5,4},{6,7},{7,6},{8,9},{9,8},{10,11... | collective-permute-start | bytes 2162696 | tf_op jit(solution)/shard_map/ppermute | solution.py:448
  129.1 16.5 %collective-permute-start.18 = (bf16[4,176,512]{2,1,0:T(8,128)(2,1)S(1)}, bf16[4,176,512]{2,1,0:T(8,128)(2,1)S(1)}, u32[]{:S(2)}, u32[]{:S(2)}) collective-permute-start(bf16[4,176,512]{2,1,0:T(8,128)(2,1)S(1)} %pad_maximum_fusion.refs_0_), channel_id=1, source_target_pairs={{0,2},{1,9},{2,4},{3,11},{4,6},{5,13},{6,0},{7,15},{8,10},{9,17},{... | collective-permute-start | bytes 2162696 | tf_op jit(solution)/shard_map/ppermute | solution.py:458
  129.8 18.7 %collective-permute-start.17 = (bf16[4,176,512]{2,1,0:T(8,128)(2,1)S(1)}, bf16[4,176,512]{2,1,0:T(8,128)(2,1)S(1)}, u32[]{:S(2)}, u32[]{:S(2)}) collective-permute-start(bf16[4,176,512]{2,1,0:T(8,128)(2,1)S(1)} %pad_maximum_fusion.refs_0_), channel_id=1, source_target_pairs={{0,4},{1,17},{2,6},{3,19},{4,0},{5,21},{6,2},{7,23},{8,12},{9,25},... | collective-permute-start | bytes 2162696 | tf_op jit(solution)/shard_map/ppermute | solution.py:458
  132.0 17.1 %collective-permute-start.16 = (bf16[4,176,512]{2,1,0:T(8,128)(2,1)S(1)}, bf16[4,176,512]{2,1,0:T(8,128)(2,1)S(1)}, u32[]{:S(2)}, u32[]{:S(2)}) collective-permute-start(bf16[4,176,512]{2,1,0:T(8,128)(2,1)S(1)} %pad_maximum_fusion.refs_0_), channel_id=1, source_target_pairs={{0,6},{1,25},{2,0},{3,27},{4,2},{5,29},{6,4},{7,31},{8,14},{9,1},{... | collective-permute-start | bytes 2162696 | tf_op jit(solution)/shard_map/ppermute | solution.py:458
  149.1 4.8 %collective-permute-start.20 = (bf16[4,176,512]{2,1,0:T(8,128)(2,1)S(1)}, bf16[4,176,512]{2,1,0:T(8,128)(2,1)S(1)}, u32[]{:S(2)}, u32[]{:S(2)}) collective-permute-start(bf16[4,176,512]{2,1,0:T(8,128)(2,1)S(1)} %collective-permute-done.16.refs_0_), channel_id=1, source_target_pairs={{0,1},{1,0},{2,3},{3,2},{4,5},{5,4},{6,7},{7,6},{8,9},{9,8},{10,11... | collective-permute-start | bytes 2162696 | tf_op jit(solution)/shard_map/ppermute | solution.py:448
  150.3 3.6 %collective-permute-start.21 = (bf16[4,176,512]{2,1,0:T(8,128)(2,1)S(1)}, bf16[4,176,512]{2,1,0:T(8,128)(2,1)S(1)}, u32[]{:S(2)}, u32[]{:S(2)}) collective-permute-start(bf16[4,176,512]{2,1,0:T(8,128)(2,1)S(1)} %collective-permute-done.17.refs_1_), channel_id=1, source_target_pairs={{0,1},{1,0},{2,3},{3,2},{4,5},{5,4},{6,7},{7,6},{8,9},{9,8},{10,11... | collective-permute-start | bytes 2162696 | tf_op jit(solution)/shard_map/ppermute | solution.py:448
  150.3 3.9 %collective-permute-start.22 = (bf16[4,176,512]{2,1,0:T(8,128)(2,1)S(1)}, bf16[4,176,512]{2,1,0:T(8,128)(2,1)S(1)}, u32[]{:S(2)}, u32[]{:S(2)}) collective-permute-start(bf16[4,176,512]{2,1,0:T(8,128)(2,1)S(1)} %collective-permute-done.18.refs_2_), channel_id=1, source_target_pairs={{0,1},{1,0},{2,3},{3,2},{4,5},{5,4},{6,7},{7,6},{8,9},{9,8},{10,11... | collective-permute-start | bytes 2162696 | tf_op jit(solution)/shard_map/ppermute | solution.py:448

commit v4 on v3

--- a/solution.py
+++ b/solution.py
@@ -125,12 +125,21 @@
     lax.fori_loop(0, count // unroll, step, 0)
 
 
+GROUP = 32
+
+
 def pick_kernel(request_ref, table_ref, out_ref, rows):
-    def one(slot):
-        row = jnp.minimum(request_ref[slot], ITEMS_DEV - 1)
-        rows[pl.ds(slot, 1), :] = table_ref[pl.ds(row, 1), :]
-
-    each_row(SLOTS, one)
+    def group(i, carry):
+        start = i * GROUP
+
+        @pl.when(request_ref[start] < ITEMS_DEV)
+        def asked():
+            for u in range(GROUP):
+                rows[pl.ds(start + u, 1), :] = table_ref[pl.ds(request_ref[start + u], 1), :]
+
+        return carry
+
+    lax.fori_loop(0, SLOTS // GROUP, group, 0)
     for requester in range(N_SEQ):
         out_ref[requester] = narrow(rows[requester * CAP : (requester + 1) * CAP, :])
 
@@ -216,14 +225,20 @@
         rows[requester * CAP + 128 : (requester + 1) * CAP, :] = second
     part = SLOTS // len(totals)
 
-    def step(i, carry):
-        for u in range(8):
-            for t, total in enumerate(totals):
-                slot = t * part + i * 8 + u
-                total[pl.ds(request_ref[slot], 1), :] += rows[pl.ds(slot, 1), :]
+    def group(i, carry):
+        starts = [t * part + i * 8 for t in range(len(totals))]
+        held = [request_ref[start] < ITEMS_DEV for start in starts]
+
+        @pl.when(functools.reduce(jnp.logical_or, held))
+        def some():
+            for u in range(8):
+                for start, total in zip(starts, totals):
+                    slot = start + u
+                    total[pl.ds(request_ref[slot], 1), :] += rows[pl.ds(slot, 1), :]
+
         return carry
 
-    lax.fori_loop(0, part // 8, step, 0)
+    lax.fori_loop(0, part // 8, group, 0)
     for block in range(ITEMS_DEV // 128):
         span = slice(block * 128, (block + 1) * 128)
         value = totals[0][span, :]
@@ -288,7 +303,9 @@
         pl.when(core == l)(lambda: each(keep))
         pl.when(core != l)(lambda: each(send))
 
-    moves = ((1, slice(0, 160), 0), (1, slice(160, CHUNK), 1), (0, slice(0, CHUNK), 2))
+    moves = tuple((l, span, i) for i, (l, span) in enumerate(
+        ((1, slice(0, 160)), (0, slice(0, 160)), (1, slice(160, CHUNK)), (0, slice(160, CHUNK)))
+    ))
     col = lax.axis_index("col")
 
     segment = jnp.broadcast_to(segment_ref[...].astype(F32), (TOK, TOK))
@@ -312,15 +329,15 @@
         normed[l] = value
         normed_scale[l] = scale
         rounded = value.astype(BF16)
-        for part in range(4):
+        for part in (2, 3, 1, 0):
             pre = mm(rounded, win_ref[l, :, part * D : (part + 1) * D])
             out, tilt = silu_parts(pre)
             proj[l, part] = out.astype(BF16)
             slope[l, part] = tilt
+        scores = [mm(proj[l, 2, :, lanes_of(h)], proj[l, 3, :, lanes_of(h)], NT) for h in range(HEADS)]
         for head in range(HEADS):
             lanes = lanes_of(head)
-            score = mm(proj[l, 2, :, lanes], proj[l, 3, :, lanes], NT) * scaling
-            out, tilt = silu_parts(score)
+            out, tilt = silu_parts(scores[head] * scaling)
             weight = jnp.where(allowed, out, 0.0).astype(BF16)
             attn[l, head] = weight
             attn_slope[l, head] = jnp.where(allowed, tilt * scaling, 0.0)
@@ -351,28 +368,31 @@
         hat = mixed[l]
         dproj[0] = ((dgated * hat).astype(BF16).astype(F32) * slope[l, 0]).astype(BF16)
         dmixed = norm_back(dgated * proj[l, 0].astype(F32), hat, mixed_scale[l]).astype(BF16)
-        for head in range(HEADS):
-            lanes = lanes_of(head)
-            dmix = dmixed[:, lanes]
-            dvalue = mm(attn[l, head], dmix, TN).astype(BF16).astype(F32)
-            dproj[1, :, lanes] = (dvalue * slope[l, 1, :, lanes]).astype(BF16)
-            dattn = mm(dmix, proj[l, 1, :, lanes], NT).astype(BF16).astype(F32)
-            dscore = (dattn * attn_slope[l, head]).astype(BF16)
-            dquery = mm(dscore, proj[l, 3, :, lanes]).astype(BF16).astype(F32)
-            dproj[2, :, lanes] = (dquery * slope[l, 2, :, lanes]).astype(BF16)
-            dkey = mm(dscore, proj[l, 2, :, lanes], TN).astype(BF16).astype(F32)
-            dproj[3, :, lanes] = (dkey * slope[l, 3, :, lanes]).astype(BF16)
+        heads = [lanes_of(h) for h in range(HEADS)]
+        dmixes = [dmixed[:, lanes] for lanes in heads]
+        dattns = [mm(dmix, proj[l, 1, :, lanes], NT) for dmix, lanes in zip(dmixes, heads)]
+        dvalues = [mm(attn[l, h], dmixes[h], TN) for h in range(HEADS)]
+        dscores = [
+            (dattn.astype(BF16).astype(F32) * attn_slope[l, h]).astype(BF16)
+            for h, dattn in enumerate(dattns)
+        ]
+        dqueries = [mm(dscore, proj[l, 3, :, lanes]) for dscore, lanes in zip(dscores, heads)]
+        dkeys = [mm(dscore, proj[l, 2, :, lanes], TN) for dscore, lanes in zip(dscores, heads)]
+        for part, grads in ((1, dvalues), (2, dqueries), (3, dkeys)):
+            for lanes, piece in zip(heads, grads):
+                piece = piece.astype(BF16).astype(F32)
+                dproj[part, :, lanes] = (piece * slope[l, part, :, lanes]).astype(BF16)
         value = normed[l]
         rounded = value.astype(BF16)
         dnormed = jnp.zeros((TOK, D), F32)
         for part in range(4):
             dpre = dproj[part]
-            put(part, mm(rounded, dpre, TN).astype(BF16))
             dnormed += mm(dpre, win_ref[l, :, part * D : (part + 1) * D], NT)
+        for part in range(4):
+            put(part, mm(rounded, dproj[part], TN).astype(BF16))
         dnormed = dnormed.astype(BF16).astype(F32)
+        leave(*moves[1 - l], "start")
         stream[...] = grad + norm_back(dnormed, value, normed_scale[l])
-        if l == 1:
-            leave(*moves[0], "start")
 
     grad = stream[...]
     for pair in range(N_COL // 2):
@@ -390,7 +410,7 @@
                 chunk = 4 * a + b
                 place = 4 * ((a - first) & 3) + ((b - second) & 3)
                 pay[l, place, 160:CHUNK, :] = hot_part[chunk * 16 : (chunk + 1) * 16, :]
-    for move in moves[1:]:
+    for move in moves[2:]:
         leave(*move, "start")
     for move in moves:
         leave(*move, "wait")
@@ -420,7 +440,7 @@
             pltpu.VMEM((LAYERS, TOK, D), BF16),
             pltpu.VMEM((4, TOK, D), BF16),
             pltpu.VMEM((LAYERS, 16, CHUNK, D), BF16),
-            pltpu.SemaphoreType.DMA((3, 4)),
+            pltpu.SemaphoreType.DMA((4, 4)),
         ],
         compiler_params=params(36),
         cost_estimate=cost(16),
@@ -583,7 +603,7 @@
         row_owner.reshape(line), item_row.reshape(line), hot_flag.reshape(line), hot_row.reshape(line)
     )
     received = lax.all_to_all(requests, "seq", split_axis=0, concat_axis=0, tiled=True)
-    picked = pick_rows(received, item_table.astype(F32))
+    picked = pick_rows(received, jnp.pad(item_table.astype(F32), ((0, 8), (0, 0))))
     returned = lax.all_to_all(picked, "seq", split_axis=0, concat_axis=0, tiled=True)
     placed = place_rows(index, returned, hot_table)
     emb = lax.all_to_all(placed, "col", split_axis=0, concat_axis=0, tiled=True)

time: 157 us -> 153 us (0.975)
  Pallas kernels: 47.6 us -> 41.5 us
    pallas_call x1, Pallas kernels: 7 us -> 4.48 us  [pick_rows(): pl.pallas_call(pick_kernel, out_shape=jax.ShapeDtypeStruct((N_SEQ, 128, 1...]
    pallas_call x1, Pallas kernels: 13.9 us -> 11.7 us  [run_stack(): pl.pallas_call(stack_kernel, out_shape=(jax.ShapeDtypeStruct((TOK, D), BF...]
  transfers between devices with their start and end apart: 26 -> 26, of which waited for: 13 -> 12; matrix products, arithmetic and copies ran while one was open for 1% -> 1% of each run, Pallas kernels for 12% -> 12%
where the time goes in v4:
time: 153 us; the launch traced here: 152 us
  starting transfers between devices  41.8 us (27%)
  Pallas kernels  41.5 us (27%)
  waiting for transfers between devices  39.4 us (26%)
  blocking collectives  26.7 us (17%)
    ppermute x15, waiting for transfers between devices, along(): return lax.ppermute(value, BOTH, device_pairs(move))  29.3 us
    ppermute x15, starting transfers between devices, along(): return lax.ppermute(value, BOTH, device_pairs(move))  18.7 us
    all_to_all x1, blocking collectives, on_device(): emb = lax.all_to_all(placed, 'col', split_axis=0, concat_axis=0, tiled=True)  13.8 us
    all_to_all x1, blocking collectives, on_device(): lax.all_to_all(picked, 'seq', split_axis=0, concat_axis=0, tiled=True)  12.9 us
    pallas_call x1, Pallas kernels, run_stack(): pl.pallas_call(stack_kernel, out_shape=(jax.ShapeDtypeStruct((TOK, D), BF...  11.7 us
    all_to_all x1, starting transfers between devices, on_device(): lax.all_to_all(requests, 'seq', split_axis=0, concat_axis=0, tiled=True)  8.6 us
    pallas_call x1, Pallas kernels, scatter_rows(): pl.pallas_call(scatter_kernel, out_shape=jax.ShapeDtypeStruct((COLS, ITEM...  8.2 us
    pallas_call x3, Pallas kernels, finish(): pl.pallas_call(functools.partial(finish_kernel, pieces, not partial), out...  6.98 us
  transfers between devices with their start and end apart: 26, of which 12 were waited for; matrix products, arithmetic and copies ran while one was open for 1% of the time, Pallas kernels for 12%

profile of v4, /device:TPU:1, one launch (start us, length us, event | category | flops | bytes accessed | tf_op | source)
XLA Modules:
  0.0 152.5 jit_solution(1329053171356420327)
XLA Ops:
  0.6 2.5 %slots.1 = (s32[16,2,128]{2,1,0:T(2,128)}, s32[8,2,128]{2,1,0:T(2,128)}) custom-call(s32[1,2048]{1,0:T(1,128)} %bitcast.31, s32[1,2048]{1,0:T(1,128)} %bitcast.32, s32[1,2048]{1,0:T(1,128)} %bitcast.33, s32[1,2048]{1,0:T(1,128)} %bitcast.34), custom_call_target="tpu_custom_call" | custom-call | flops 2750000128 | bytes 9000000 | tf_op jit(solution)/shard_map/slots/pallas_call | solution.py:96
  3.1 8.6 %all-to-all-start = ((s32[16,2,128]{2,1,0:T(2,128)}), s32[16,2,128]{2,1,0:T(2,128)S(1)}, u32[]{:S(2)}, u32[]{:S(2)}) async-start(s32[16,2,128]{2,1,0:T(2,128)} %get-tuple-element.32), calls=%async_computation | async-start | bytes 32768 | tf_op jit(solution)/shard_map/all_to_all | solution.py:605
  11.7 0.5 copy.19
  12.4 5.8 %all-to-all-done = s32[16,2,128]{2,1,0:T(2,128)S(1)} async-done(((s32[16,2,128]{2,1,0:T(2,128)}), s32[16,2,128]{2,1,0:T(2,128)S(1)}, u32[]{:S(2)}, u32[]{:S(2)}) %all-to-all-start) | async-done | bytes 16416 | tf_op jit(solution)/shard_map/all_to_all | solution.py:605
  18.2 4.5 %pick_rows.1 = bf16[16,128,128]{2,1,0:T(8,128)(2,1)S(1)} custom-call(s32[4096]{0:T(1024)S(1)} %bitcast.22, f32[4104,64]{1,0:T(8,128)S(1)} %pad_convert_fusion.table_ref), custom_call_target="tpu_custom_call" | custom-call | flops 7699999744 | bytes 25200000 | tf_op jit(solution)/shard_map/pick_rows/pallas_call | solution.py:148
  22.7 12.9 %all_to_all.25.returned_ref = bf16[16,128,128]{2,1,0:T(8,128)(2,1)S(1)} all-to-all(bf16[16,128,128]{2,1,0:T(8,128)(2,1)S(1)} %pick_rows.1), channel_id=1, replica_groups=mesh['seq'=16,'col'=8] {'seq'}, dimensions={0} | all-to-all | bytes 1048576 | tf_op jit(solution)/shard_map/all_to_all | solution.py:607
  35.6 2.9 %place_rows.1 = bf16[8,128,128]{2,1,0:T(8,128)(2,1)S(1)} custom-call(s32[2048]{0:T(1024)S(1)} %bitcast.25, bf16[16,128,128]{2,1,0:T(8,128)(2,1)S(1)} %all_to_all.25.returned_ref, bf16[64,256]{1,0:T(8,128)(2,1)S(1)} %bitcast.24), custom_call_target="tpu_custom_call" | custom-call | flops 4400000000 | bytes 14400000 | tf_op jit(solution)/shard_map/place_rows/pallas_call | solution.py:176
  38.6 13.8 %all_to_all.26.emb_ref = bf16[8,128,128]{2,1,0:T(8,128)(2,1)S(1)} all-to-all(bf16[8,128,128]{2,1,0:T(8,128)(2,1)S(1)} %place_rows.1), channel_id=1, replica_groups=mesh['seq'=16,'col'=8] {'col'}, dimensions={0} | all-to-all | bytes 524288 | tf_op jit(solution)/shard_map/all_to_all | solution.py:609
  52.4 11.7 %layers.1 = (bf16[256,512]{1,0:T(8,128)(2,1)}, bf16[8,128,128]{2,1,0:T(8,128)(2,1)}, bf16[4,176,512]{2,1,0:T(8,128)(2,1)S(1)}, bf16[4,176,512]{2,1,0:T(8,128)(2,...) custom-call(s32[8,2,128]{2,1,0:T(2,128)S(1)} %copy-done.5, ...), custom_call_target="tpu_custom_call" | custom-call | flops 17600000000 | bytes 57600000 | tf_op jit(solution)/shard_map/layers/pallas_call | solution.py:421
  64.1 1.3 collective-permute-start.1
  65.5 0.4 collective-permute-start.5
  66.0 1.2 collective-permute-done.1
  67.2 0.2 add_convert_fusion.3
  67.4 0.6 collective-permute-start.2
  68.1 0.2 collective-permute-done.3
  68.4 0.4 collective-permute-start.4
  68.8 0.4 collective-permute-done.5
  69.5 2.0 %collective-permute-start.6 = (bf16[4,176,512]{2,1,0:T(8,128)(2,1)S(1)}, bf16[4,176,512]{2,1,0:T(8,128)(2,1)S(1)}, u32[]{:S(2)}, u32[]{:S(2)}) collective-permute-start(bf16[4,176,512]{2,1,0:T(8,128)(2,1)S(1)} %add_convert_fusion.1), channel_id=1, source_target_pairs={{0,6},{1,25},{2,0},{3,27},{4,2},{5,29},{6,4},{7,31},{8,14},{9,1},{... | collective-permute-start | bytes 2162696 | tf_op jit(solution)/shard_map/ppermute | solution.py:478
  71.5 8.0 %collective-permute-done.2 = bf16[4,176,512]{2,1,0:T(8,128)(2,1)S(1)} collective-permute-done((bf16[4,176,512]{2,1,0:T(8,128)(2,1)S(1)}, bf16[4,176,512]{2,1,0:T(8,128)(2,1)S(1)}, u32[]{:S(2)}, u32[]{:S(2)}) %collective-permute-start.2) | collective-permute-done | bytes 720928 | tf_op jit(solution)/shard_map/ppermute | solution.py:478
  79.5 7.7 %collective-permute-done.4 = bf16[4,176,512]{2,1,0:T(8,128)(2,1)S(1)} collective-permute-done((bf16[4,176,512]{2,1,0:T(8,128)(2,1)S(1)}, bf16[4,176,512]{2,1,0:T(8,128)(2,1)S(1)}, u32[]{:S(2)}, u32[]{:S(2)}) %collective-permute-start.4) | collective-permute-done | bytes 720928 | tf_op jit(solution)/shard_map/ppermute | solution.py:478
  87.2 0.5 add_convert_fusion
  87.7 0.7 collective-permute-start.7
  88.3 1.4 collective-permute-start.9
  89.8 5.8 %all-to-all-start.3 = ((bf16[8,128,128]{2,1,0:T(8,128)(2,1)}), bf16[8,128,128]{2,1,0:T(8,128)(2,1)S(1)}, u32[]{:S(2)}, u32[]{:S(2)}) async-start(bf16[8,128,128]{2,1,0:T(8,128)(2,1)} %get-tuple-element.44), calls=%async_computation.3 | async-start | bytes 524288 | tf_op jit(solution)/shard_map/all_to_all | solution.py:614
  95.7 2.7 %collective-permute-start.12 = (bf16[176,512]{1,0:T(8,128)(2,1)S(1)}, bf16[176,512]{1,0:T(8,128)(2,1)S(1)}, u32[]{:S(2)}, u32[]{:S(2)}) collective-permute-start(bf16[176,512]{1,0:T(8,128)(2,1)S(1)} %fusion.1), channel_id=1, source_target_pairs={{0,96},{1,7},{2,98},{3,1},{4,100},{5,3},{6,102},{7,5},{8,104},{9,1... | collective-permute-start | bytes 540680 | tf_op jit(solution)/shard_map/ppermute | solution.py:478
  98.4 1.7 %collective-permute-start.10 = (bf16[176,512]{1,0:T(8,128)(2,1)S(1)}, bf16[176,512]{1,0:T(8,128)(2,1)S(1)}, u32[]{:S(2)}, u32[]{:S(2)}) collective-permute-start(bf16[176,512]{1,0:T(8,128)(2,1)S(1)} %fusion.1), channel_id=1, source_target_pairs={{0,64},{1,5},{2,66},{3,7},{4,68},{5,1},{6,70},{7,3},{8,72},{9,13},... | collective-permute-start | bytes 540680 | tf_op jit(solution)/shard_map/ppermute | solution.py:478
  100.2 2.1 %all-to-all-done.3.grad_ref = bf16[8,128,128]{2,1,0:T(8,128)(2,1)S(1)} async-done(((bf16[8,128,128]{2,1,0:T(8,128)(2,1)}), bf16[8,128,128]{2,1,0:T(8,128)(2,1)S(1)}, u32[]{:S(2)}, u32[]{:S(2)}) %all-to-all-start.3) | async-done | bytes 262176 | tf_op jit(solution)/shard_map/all_to_all | solution.py:614
  102.2 3.8 %return_rows.1 = bf16[16,128,128]{2,1,0:T(8,128)(2,1)} custom-call(s32[2048]{0:T(1024)S(1)} %bitcast.26, bf16[8,128,128]{2,1,0:T(8,128)(2,1)S(1)} %all-to-all-done.3.grad_ref), custom_call_target="tpu_custom_call" | custom-call | flops 4400000000 | bytes 14400000 | tf_op jit(solution)/shard_map/return_rows/pallas_call | solution.py:204
  106.0 4.6 %all-to-all-start.4 = ((bf16[16,128,128]{2,1,0:T(8,128)(2,1)}), bf16[16,128,128]{2,1,0:T(8,128)(2,1)S(1)}, u32[]{:S(2)}, u32[]{:S(2)}) async-start(bf16[16,128,128]{2,1,0:T(8,128)(2,1)} %return_rows.1), calls=%async_computation.4 | async-start | bytes 1048576 | tf_op jit(solution)/shard_map/all_to_all | solution.py:620
  110.8 1.4 collective-permute-start.15
  112.2 2.4 %collective-permute-start.14 = (bf16[176,512]{1,0:T(8,128)(2,1)S(1)}, bf16[176,512]{1,0:T(8,128)(2,1)S(1)}, u32[]{:S(2)}, u32[]{:S(2)}) collective-permute-start(bf16[176,512]{1,0:T(8,128)(2,1)S(1)} %add_convert_fusion.5), channel_id=1, source_target_pairs={{0,16},{1,65},{2,18},{3,67},{4,20},{5,69},{6,22},{7,71},{8,24},{9,... | collective-permute-start | bytes 540680 | tf_op jit(solution)/shard_map/ppermute | solution.py:478
  114.6 1.2 collective-permute-start.13
  115.8 5.4 %collective-permute-done.15 = bf16[176,512]{1,0:T(8,128)(2,1)S(1)} collective-permute-done((bf16[176,512]{1,0:T(8,128)(2,1)S(1)}, bf16[176,512]{1,0:T(8,128)(2,1)S(1)}, u32[]{:S(2)}, u32[]{:S(2)}) %collective-permute-start.15) | collective-permute-done | bytes 180256 | tf_op jit(solution)/shard_map/ppermute | solution.py:478
  121.2 3.3 %collective-permute-done.14 = bf16[176,512]{1,0:T(8,128)(2,1)S(1)} collective-permute-done((bf16[176,512]{1,0:T(8,128)(2,1)S(1)}, bf16[176,512]{1,0:T(8,128)(2,1)S(1)}, u32[]{:S(2)}, u32[]{:S(2)}) %collective-permute-start.14) | collective-permute-done | bytes 180256 | tf_op jit(solution)/shard_map/ppermute | solution.py:478
  124.6 0.5 collective-permute-start.19
  125.1 0.7 collective-permute-start.18
  125.8 2.2 %collective-permute-start.17 = (bf16[4,176,512]{2,1,0:T(8,128)(2,1)S(1)}, bf16[4,176,512]{2,1,0:T(8,128)(2,1)S(1)}, u32[]{:S(2)}, u32[]{:S(2)}) collective-permute-start(bf16[4,176,512]{2,1,0:T(8,128)(2,1)S(1)} %pad_maximum_fusion.refs_0_), channel_id=1, source_target_pairs={{0,4},{1,17},{2,6},{3,19},{4,0},{5,21},{6,2},{7,23},{8,12},{9,25},... | collective-permute-start | bytes 2162696 | tf_op jit(solution)/shard_map/ppermute | solution.py:478
  128.0 1.2 collective-permute-start.16
  129.2 8.2 %scatter_rows.1 = f32[64,4096]{1,0:T(8,128)} custom-call(s32[4096]{0:T(1024)S(1)} %bitcast.23, bf16[16,128,128]{2,1,0:T(8,128)(2,1)S(1)} %all-to-all-done.4.incoming_ref), custom_call_target="tpu_custom_call" | custom-call | flops 12099999744 | bytes 39600000 | tf_op jit(solution)/shard_map/scatter_rows/pallas_call | solution.py:251
  137.4 2.7 %widen_sums.3 = (f32[2,512,2048]{2,1,0:T(8,128)}, f32[2,512,512]{2,1,0:T(8,128)}) custom-call(bf16[4,176,512]{2,1,0:T(8,128)(2,1)S(1)} %pad_maximum_fusion.refs_0_, bf16[4,176,512]{2,1,0:T(8,128)(2,1)} %collective-permute-done.19.refs_1_), custom_call_target="tpu_custom_call" | custom-call | flops 1870000000 | bytes 6120000 | tf_op jit(solution)/shard_map/widen_sums/pallas_call | solution.py:547
  140.2 4.3 %collective-permute-done.17.refs_1_ = bf16[4,176,512]{2,1,0:T(8,128)(2,1)S(1)} collective-permute-done((bf16[4,176,512]{2,1,0:T(8,128)(2,1)S(1)}, bf16[4,176,512]{2,1,0:T(8,128)(2,1)S(1)}, u32[]{:S(2)}, u32[]{:S(2)}) %collective-permute-start.17) | collective-permute-done | bytes 720928 | tf_op jit(solution)/shard_map/ppermute | solution.py:478
  144.5 0.6 collective-permute-done.16.refs_0_
  145.1 1.2 collective-permute-start.20
  146.3 0.5 collective-permute-start.22
  146.9 0.9 hot_sums.1
  147.8 2.1 %widen_sums.4 = (f32[2,512,2048]{2,1,0:T(8,128)}, f32[2,512,512]{2,1,0:T(8,128)}) custom-call(bf16[4,176,512]{2,1,0:T(8,128)(2,1)S(1)} %collective-permute-done.16.refs_0_, bf16[4,176,512]{2,1,0:T(8,128)(2,1)S(1)} %collective-permute-done.17.refs_1_, ...), custom_call_target="tpu_custom_call", output_to_operand_aliasing={{0}: (3, {}), {1}: (4, {})} | custom-call | flops 2529999872 | bytes 8279999 | tf_op jit(solution)/shard_map/widen_sums/pallas_call | solution.py:547
  149.9 0.3 collective-permute-done.22.refs_2_
  150.2 2.1 %widen_sums.5 = (f32[2,512,2048]{2,1,0:T(8,128)}, f32[2,512,512]{2,1,0:T(8,128)}) custom-call(bf16[4,176,512]{2,1,0:T(8,128)(2,1)S(1)} %collective-permute-done.20.refs_0_, bf16[4,176,512]{2,1,0:T(8,128)(2,1)S(1)} %collective-permute-done.21.refs_1_, ...), custom_call_target="tpu_custom_call", output_to_operand_aliasing={{0}: (3, {}), {1}: (4, {})} | custom-call | flops 2529999872 | bytes 8279999 | tf_op jit(solution)/shard_map/widen_sums/pallas_call | solution.py:547
  (44 shorter events, 1.1 us)
Async XLA Ops:
  0.6 11.1 %copy-start.6 = (bf16[4096,64]{0,1:T(8,128)(2,1)S(1)}, bf16[4096,64]{0,1:T(8,128)(2,1)}, u32[]{:S(2)}) copy-start(bf16[4096,64]{0,1:T(8,128)(2,1)} %param.10) | copy-start | bytes 1572868
  3.1 15.0 %all-to-all-start = ((s32[16,2,128]{2,1,0:T(2,128)}), s32[16,2,128]{2,1,0:T(2,128)S(1)}, u32[]{:S(2)}, u32[]{:S(2)}) async-start(s32[16,2,128]{2,1,0:T(2,128)} %get-tuple-element.32), calls=%async_computation | async-start | bytes 32768 | tf_op jit(solution)/shard_map/all_to_all | solution.py:605
  18.2 17.4 %copy-start.3 = (bf16[256,64]{0,1:T(8,128)(2,1)S(1)}, bf16[256,64]{0,1:T(8,128)(2,1)}, u32[]{:S(2)}) copy-start(bf16[256,64]{0,1:T(8,128)(2,1)} %param.11) | copy-start | bytes 98308
  18.2 17.4 %copy-start.5 = (s32[8,2,128]{2,1,0:T(2,128)S(1)}, s32[8,2,128]{2,1,0:T(2,128)}, u32[]{:S(2)}) copy-start(s32[8,2,128]{2,1,0:T(2,128)} %get-tuple-element.31.index_ref) | copy-start | bytes 24580
  35.6 16.8 %copy-start = (bf16[2,512,2048]{2,1,0:T(8,128)(2,1)S(1)}, bf16[2,512,2048]{2,1,0:T(8,128)(2,1)}, u32[]{:S(2)}) copy-start(bf16[2,512,2048]{2,1,0:T(8,128)(2,1)} %win_ref.1) | copy-start | bytes 12582916
  35.6 16.8 %copy-start.1 = (bf16[2,512,512]{2,1,0:T(8,128)(2,1)S(1)}, bf16[2,512,512]{2,1,0:T(8,128)(2,1)}, u32[]{:S(2)}) copy-start(bf16[2,512,512]{2,1,0:T(8,128)(2,1)} %wout_ref.1) | copy-start | bytes 3145732
  35.6 16.7 %copy-start.2 = (bf16[256,512]{1,0:T(8,128)(2,1)S(1)}, bf16[256,512]{1,0:T(8,128)(2,1)}, u32[]{:S(2)}) copy-start(bf16[256,512]{1,0:T(8,128)(2,1)} %cot_ref.1) | copy-start | bytes 786436
  35.6 16.7 %copy-start.4 = (s32[1,256]{1,0:T(1,128)S(1)}, s32[1,256]{1,0:T(1,128)}, u32[]{:S(2)}) copy-start(s32[1,256]{1,0:T(1,128)} %segment_ref.1) | copy-start | bytes 3076
  64.1 3.1 %collective-permute-start.1 = (bf16[4,176,512]{2,1,0:T(8,128)(2,1)S(1)}, bf16[4,176,512]{2,1,0:T(8,128)(2,1)S(1)}, u32[]{:S(2)}, u32[]{:S(2)}) collective-permute-start(bf16[4,176,512]{2,1,0:T(8,128)(2,1)S(1)} %get-tuple-element.37), channel_id=1, source_target_pairs={{0,1},{1,0},{2,3},{3,2},{4,5},{5,4},{6,7},{7,6},{8,9},{9,8},{10,11... | collective-permute-start | bytes 2162696 | tf_op jit(solution)/shard_map/ppermute | solution.py:468
  65.4 2.8 %collective-permute-start.3 = (bf16[4,176,512]{2,1,0:T(8,128)(2,1)S(1)}, bf16[4,176,512]{2,1,0:T(8,128)(2,1)S(1)}, u32[]{:S(2)}, u32[]{:S(2)}) collective-permute-start(bf16[4,176,512]{2,1,0:T(8,128)(2,1)S(1)} %get-tuple-element.39), channel_id=1, source_target_pairs={{0,1},{1,0},{2,3},{3,2},{4,5},{5,4},{6,7},{7,6},{8,9},{9,8},{10,11... | collective-permute-start | bytes 2162696 | tf_op jit(solution)/shard_map/ppermute | solution.py:468
  65.5 3.8 %collective-permute-start.5 = (bf16[4,176,512]{2,1,0:T(8,128)(2,1)S(1)}, bf16[4,176,512]{2,1,0:T(8,128)(2,1)S(1)}, u32[]{:S(2)}, u32[]{:S(2)}) collective-permute-start(bf16[4,176,512]{2,1,0:T(8,128)(2,1)S(1)} %get-tuple-element.41), channel_id=1, source_target_pairs={{0,1},{1,0},{2,3},{3,2},{4,5},{5,4},{6,7},{7,6},{8,9},{9,8},{10,11... | collective-permute-start | bytes 2162696 | tf_op jit(solution)/shard_map/ppermute | solution.py:468
  65.9 5.5 %collective-permute-start = (bf16[4,176,512]{2,1,0:T(8,128)(2,1)S(1)}, bf16[4,176,512]{2,1,0:T(8,128)(2,1)S(1)}, u32[]{:S(2)}, u32[]{:S(2)}) collective-permute-start(bf16[4,176,512]{2,1,0:T(8,128)(2,1)S(1)} %get-tuple-element.35), channel_id=1, source_target_pairs={{0,1},{1,0},{2,3},{3,2},{4,5},{5,4},{6,7},{7,6},{8,9},{9,8},{10,11... | collective-permute-start | bytes 2162696 | tf_op jit(solution)/shard_map/ppermute | solution.py:468
  67.4 12.1 %collective-permute-start.2 = (bf16[4,176,512]{2,1,0:T(8,128)(2,1)S(1)}, bf16[4,176,512]{2,1,0:T(8,128)(2,1)S(1)}, u32[]{:S(2)}, u32[]{:S(2)}) collective-permute-start(bf16[4,176,512]{2,1,0:T(8,128)(2,1)S(1)} %add_convert_fusion.3), channel_id=1, source_target_pairs={{0,4},{1,17},{2,6},{3,19},{4,0},{5,21},{6,2},{7,23},{8,12},{9,25},... | collective-permute-start | bytes 2162696 | tf_op jit(solution)/shard_map/ppermute | solution.py:478
  68.4 18.7 %collective-permute-start.4 = (bf16[4,176,512]{2,1,0:T(8,128)(2,1)S(1)}, bf16[4,176,512]{2,1,0:T(8,128)(2,1)S(1)}, u32[]{:S(2)}, u32[]{:S(2)}) collective-permute-start(bf16[4,176,512]{2,1,0:T(8,128)(2,1)S(1)} %add_convert_fusion.2), channel_id=1, source_target_pairs={{0,2},{1,9},{2,4},{3,11},{4,6},{5,13},{6,0},{7,15},{8,10},{9,17},{... | collective-permute-start | bytes 2162696 | tf_op jit(solution)/shard_map/ppermute | solution.py:478
  69.5 17.7 %collective-permute-start.6 = (bf16[4,176,512]{2,1,0:T(8,128)(2,1)S(1)}, bf16[4,176,512]{2,1,0:T(8,128)(2,1)S(1)}, u32[]{:S(2)}, u32[]{:S(2)}) collective-permute-start(bf16[4,176,512]{2,1,0:T(8,128)(2,1)S(1)} %add_convert_fusion.1), channel_id=1, source_target_pairs={{0,6},{1,25},{2,0},{3,27},{4,2},{5,29},{6,4},{7,31},{8,14},{9,1},{... | collective-permute-start | bytes 2162696 | tf_op jit(solution)/shard_map/ppermute | solution.py:478
  87.7 7.9 %collective-permute-start.7 = (bf16[176,512]{1,0:T(8,128)(2,1)S(1)}, bf16[176,512]{1,0:T(8,128)(2,1)S(1)}, u32[]{:S(2)}, u32[]{:S(2)}) collective-permute-start(bf16[176,512]{1,0:T(8,128)(2,1)S(1)} %get-tuple-element.57), channel_id=1, source_target_pairs={{0,16},{1,65},{2,18},{3,67},{4,20},{5,69},{6,22},{7,71},{8,24},{9,... | collective-permute-start | bytes 540680 | tf_op jit(solution)/shard_map/ppermute | solution.py:478
  88.3 7.2 %collective-permute-start.9 = (bf16[176,512]{1,0:T(8,128)(2,1)S(1)}, bf16[176,512]{1,0:T(8,128)(2,1)S(1)}, u32[]{:S(2)}, u32[]{:S(2)}) collective-permute-start(bf16[176,512]{1,0:T(8,128)(2,1)S(1)} %get-tuple-element.58), channel_id=1, source_target_pairs={{0,24},{1,97},{2,26},{3,99},{4,28},{5,101},{6,30},{7,103},{8,0},{9... | collective-permute-start | bytes 540680 | tf_op jit(solution)/shard_map/ppermute | solution.py:478
  89.8 5.8 %collective-permute-start.8 = (bf16[176,512]{1,0:T(8,128)(2,1)S(1)}, bf16[176,512]{1,0:T(8,128)(2,1)S(1)}, u32[]{:S(2)}, u32[]{:S(2)}) collective-permute-start(bf16[176,512]{1,0:T(8,128)(2,1)S(1)} %get-tuple-element.59), channel_id=1, source_target_pairs={{0,8},{1,33},{2,10},{3,35},{4,12},{5,37},{6,14},{7,39},{8,16},{9,4... | collective-permute-start | bytes 540680 | tf_op jit(solution)/shard_map/ppermute | solution.py:478
  89.8 12.4 %all-to-all-start.3 = ((bf16[8,128,128]{2,1,0:T(8,128)(2,1)}), bf16[8,128,128]{2,1,0:T(8,128)(2,1)S(1)}, u32[]{:S(2)}, u32[]{:S(2)}) async-start(bf16[8,128,128]{2,1,0:T(8,128)(2,1)} %get-tuple-element.44), calls=%async_computation.3 | async-start | bytes 524288 | tf_op jit(solution)/shard_map/all_to_all | solution.py:614
  95.7 15.0 %collective-permute-start.12 = (bf16[176,512]{1,0:T(8,128)(2,1)S(1)}, bf16[176,512]{1,0:T(8,128)(2,1)S(1)}, u32[]{:S(2)}, u32[]{:S(2)}) collective-permute-start(bf16[176,512]{1,0:T(8,128)(2,1)S(1)} %fusion.1), channel_id=1, source_target_pairs={{0,96},{1,7},{2,98},{3,1},{4,100},{5,3},{6,102},{7,5},{8,104},{9,1... | collective-permute-start | bytes 540680 | tf_op jit(solution)/shard_map/ppermute | solution.py:478
  98.4 12.3 %collective-permute-start.11 = (bf16[176,512]{1,0:T(8,128)(2,1)S(1)}, bf16[176,512]{1,0:T(8,128)(2,1)S(1)}, u32[]{:S(2)}, u32[]{:S(2)}) collective-permute-start(bf16[176,512]{1,0:T(8,128)(2,1)S(1)} %fusion.1), channel_id=1, source_target_pairs={{0,32},{1,3},{2,34},{3,5},{4,36},{5,7},{6,38},{7,1},{8,40},{9,11},... | collective-permute-start | bytes 540680 | tf_op jit(solution)/shard_map/ppermute | solution.py:478
  98.4 12.3 %collective-permute-start.10 = (bf16[176,512]{1,0:T(8,128)(2,1)S(1)}, bf16[176,512]{1,0:T(8,128)(2,1)S(1)}, u32[]{:S(2)}, u32[]{:S(2)}) collective-permute-start(bf16[176,512]{1,0:T(8,128)(2,1)S(1)} %fusion.1), channel_id=1, source_target_pairs={{0,64},{1,5},{2,66},{3,7},{4,68},{5,1},{6,70},{7,3},{8,72},{9,13},... | collective-permute-start | bytes 540680 | tf_op jit(solution)/shard_map/ppermute | solution.py:478
  106.0 23.2 %all-to-all-start.4 = ((bf16[16,128,128]{2,1,0:T(8,128)(2,1)}), bf16[16,128,128]{2,1,0:T(8,128)(2,1)S(1)}, u32[]{:S(2)}, u32[]{:S(2)}) async-start(bf16[16,128,128]{2,1,0:T(8,128)(2,1)} %return_rows.1), calls=%async_computation.4 | async-start | bytes 1048576 | tf_op jit(solution)/shard_map/all_to_all | solution.py:620
  110.8 10.4 %collective-permute-start.15 = (bf16[176,512]{1,0:T(8,128)(2,1)S(1)}, bf16[176,512]{1,0:T(8,128)(2,1)S(1)}, u32[]{:S(2)}, u32[]{:S(2)}) collective-permute-start(bf16[176,512]{1,0:T(8,128)(2,1)S(1)} %add_convert_fusion.5), channel_id=1, source_target_pairs={{0,8},{1,33},{2,10},{3,35},{4,12},{5,37},{6,14},{7,39},{8,16},{9,4... | collective-permute-start | bytes 540680 | tf_op jit(solution)/shard_map/ppermute | solution.py:478
  112.2 12.3 %collective-permute-start.14 = (bf16[176,512]{1,0:T(8,128)(2,1)S(1)}, bf16[176,512]{1,0:T(8,128)(2,1)S(1)}, u32[]{:S(2)}, u32[]{:S(2)}) collective-permute-start(bf16[176,512]{1,0:T(8,128)(2,1)S(1)} %add_convert_fusion.5), channel_id=1, source_target_pairs={{0,16},{1,65},{2,18},{3,67},{4,20},{5,69},{6,22},{7,71},{8,24},{9,... | collective-permute-start | bytes 540680 | tf_op jit(solution)/shard_map/ppermute | solution.py:478
  114.6 9.9 %collective-permute-start.13 = (bf16[176,512]{1,0:T(8,128)(2,1)S(1)}, bf16[176,512]{1,0:T(8,128)(2,1)S(1)}, u32[]{:S(2)}, u32[]{:S(2)}) collective-permute-start(bf16[176,512]{1,0:T(8,128)(2,1)S(1)} %add_convert_fusion.5), channel_id=1, source_target_pairs={{0,24},{1,97},{2,26},{3,99},{4,28},{5,101},{6,30},{7,103},{8,0},{9... | collective-permute-start | bytes 540680 | tf_op jit(solution)/shard_map/ppermute | solution.py:478
  124.6 12.8 %collective-permute-start.19 = (bf16[4,176,512]{2,1,0:T(8,128)(2,1)S(1)}, bf16[4,176,512]{2,1,0:T(8,128)(2,1)}, u32[]{:S(2)}, u32[]{:S(2)}) collective-permute-start(bf16[4,176,512]{2,1,0:T(8,128)(2,1)S(1)} %pad_maximum_fusion.refs_0_), channel_id=1, source_target_pairs={{0,1},{1,0},{2,3},{3,2},{4,5},{5,4},{6,7},{7,6},{8,9},{9,8},{10,11... | collective-permute-start | bytes 2162696 | tf_op jit(solution)/shard_map/ppermute | solution.py:468
  125.1 15.1 %collective-permute-start.18 = (bf16[4,176,512]{2,1,0:T(8,128)(2,1)S(1)}, bf16[4,176,512]{2,1,0:T(8,128)(2,1)S(1)}, u32[]{:S(2)}, u32[]{:S(2)}) collective-permute-start(bf16[4,176,512]{2,1,0:T(8,128)(2,1)S(1)} %pad_maximum_fusion.refs_0_), channel_id=1, source_target_pairs={{0,2},{1,9},{2,4},{3,11},{4,6},{5,13},{6,0},{7,15},{8,10},{9,17},{... | collective-permute-start | bytes 2162696 | tf_op jit(solution)/shard_map/ppermute | solution.py:478
  125.8 18.7 %collective-permute-start.17 = (bf16[4,176,512]{2,1,0:T(8,128)(2,1)S(1)}, bf16[4,176,512]{2,1,0:T(8,128)(2,1)S(1)}, u32[]{:S(2)}, u32[]{:S(2)}) collective-permute-start(bf16[4,176,512]{2,1,0:T(8,128)(2,1)S(1)} %pad_maximum_fusion.refs_0_), channel_id=1, source_target_pairs={{0,4},{1,17},{2,6},{3,19},{4,0},{5,21},{6,2},{7,23},{8,12},{9,25},... | collective-permute-start | bytes 2162696 | tf_op jit(solution)/shard_map/ppermute | solution.py:478
  128.0 17.1 %collective-permute-start.16 = (bf16[4,176,512]{2,1,0:T(8,128)(2,1)S(1)}, bf16[4,176,512]{2,1,0:T(8,128)(2,1)S(1)}, u32[]{:S(2)}, u32[]{:S(2)}) collective-permute-start(bf16[4,176,512]{2,1,0:T(8,128)(2,1)S(1)} %pad_maximum_fusion.refs_0_), channel_id=1, source_target_pairs={{0,6},{1,25},{2,0},{3,27},{4,2},{5,29},{6,4},{7,31},{8,14},{9,1},{... | collective-permute-start | bytes 2162696 | tf_op jit(solution)/shard_map/ppermute | solution.py:478
  145.1 4.8 %collective-permute-start.20 = (bf16[4,176,512]{2,1,0:T(8,128)(2,1)S(1)}, bf16[4,176,512]{2,1,0:T(8,128)(2,1)S(1)}, u32[]{:S(2)}, u32[]{:S(2)}) collective-permute-start(bf16[4,176,512]{2,1,0:T(8,128)(2,1)S(1)} %collective-permute-done.16.refs_0_), channel_id=1, source_target_pairs={{0,1},{1,0},{2,3},{3,2},{4,5},{5,4},{6,7},{7,6},{8,9},{9,8},{10,11... | collective-permute-start | bytes 2162696 | tf_op jit(solution)/shard_map/ppermute | solution.py:468
  146.3 3.6 %collective-permute-start.21 = (bf16[4,176,512]{2,1,0:T(8,128)(2,1)S(1)}, bf16[4,176,512]{2,1,0:T(8,128)(2,1)S(1)}, u32[]{:S(2)}, u32[]{:S(2)}) collective-permute-start(bf16[4,176,512]{2,1,0:T(8,128)(2,1)S(1)} %collective-permute-done.17.refs_1_), channel_id=1, source_target_pairs={{0,1},{1,0},{2,3},{3,2},{4,5},{5,4},{6,7},{7,6},{8,9},{9,8},{10,11... | collective-permute-start | bytes 2162696 | tf_op jit(solution)/shard_map/ppermute | solution.py:468
  146.3 3.9 %collective-permute-start.22 = (bf16[4,176,512]{2,1,0:T(8,128)(2,1)S(1)}, bf16[4,176,512]{2,1,0:T(8,128)(2,1)S(1)}, u32[]{:S(2)}, u32[]{:S(2)}) collective-permute-start(bf16[4,176,512]{2,1,0:T(8,128)(2,1)S(1)} %collective-permute-done.18.refs_2_), channel_id=1, source_target_pairs={{0,1},{1,0},{2,3},{3,2},{4,5},{5,4},{6,7},{7,6},{8,9},{9,8},{10,11... | collective-permute-start | bytes 2162696 | tf_op jit(solution)/shard_map/ppermute | solution.py:468

commit v5 on v4

--- a/solution.py
+++ b/solution.py
@@ -116,7 +116,7 @@
     return jnp.concatenate([rows[:128], rows[128:]], axis=1).astype(BF16)
 
 
-def each_row(count, body, unroll=32):
+def each_row(count, body, unroll=64):
     def step(i, carry):
         for u in range(unroll):
             body(i * unroll + u)
@@ -426,7 +426,7 @@
         )
         + (piece,) * 8,
         in_specs=vmem(6),
-        out_specs=tuple(vmem(2)) + (HBM,) * 8,
+        out_specs=tuple(vmem(2)) + (ANY,) * 8,
         scratch_shapes=[
             pltpu.VMEM((TOK, D), F32),
             pltpu.VMEM((LAYERS, TOK, D), F32),
@@ -489,17 +489,17 @@
     order = (2, 1, 3, 0)
     got = {k: to_core(send[k]) for k in order}
     chip = {k: add_all(keep[k], got[k]) for k in order}
-    came = {k: along(chip[k], 0, k) for k in (2, 1, 3)}
+    came = {k: along(chip[k], 0, k) for k in (1, 3, 2)}
     line = add_all(chip[0], came[2], came[1], came[3])
     line, grad_emb = lax.optimization_barrier((line, grad_emb))
-    came = {k: along(line[k], 1, k) for k in (2, 1, 3)}
+    came = {k: along(line[k], 1, k) for k in (1, 3, 2)}
     plane = add_all(line[0], came[2], came[1], came[3])
     outgoing = send_back(gather_columns(grad_emb))
-    came = {k: along(plane, 2, k) for k in (2, 1, 3)}
+    came = {k: along(plane, 2, k) for k in (1, 3, 2)}
     total = add_all(plane, came[2], came[1], came[3])
     row = jnp.stack([total] + [along(total, 1, -k) for k in (1, 2, 3)])
     incoming = exchange(outgoing)
-    mine = {k: along(row, 0, -k) for k in (2, 1, 3)}
+    mine = {k: along(row, 0, -k) for k in (1, 3, 2)}
     mine[0] = row
     other = {0: to_core(row)}
     table_grad = scatter(incoming)

time: 153 us -> 153 us (level)
  Pallas kernels: 41.5 us -> 43.4 us
where the time goes in v5:
time: 153 us; the launch traced here: 152 us
  Pallas kernels  43.4 us (28%)
  starting transfers between devices  41.7 us (27%)
  waiting for transfers between devices  38.1 us (25%)
  blocking collectives  25.9 us (17%)
    ppermute x15, waiting for transfers between devices, along(): return lax.ppermute(value, BOTH, device_pairs(move))  28.1 us
    ppermute x15, starting transfers between devices, along(): return lax.ppermute(value, BOTH, device_pairs(move))  18.7 us
    all_to_all x1, blocking collectives, on_device(): emb = lax.all_to_all(placed, 'col', split_axis=0, concat_axis=0, tiled=True)  13.8 us
    all_to_all x1, blocking collectives, on_device(): lax.all_to_all(picked, 'seq', split_axis=0, concat_axis=0, tiled=True)  12.1 us
    pallas_call x1, Pallas kernels, run_stack(): pl.pallas_call(stack_kernel, out_shape=(jax.ShapeDtypeStruct((TOK, D), BF...  11.9 us
    pallas_call x1, Pallas kernels, scatter_rows(): pl.pallas_call(scatter_kernel, out_shape=jax.ShapeDtypeStruct((COLS, ITEM...  9.46 us
    all_to_all x1, starting transfers between devices, on_device(): lax.all_to_all(requests, 'seq', split_axis=0, concat_axis=0, tiled=True)  8.6 us
    pallas_call x3, Pallas kernels, finish(): pl.pallas_call(functools.partial(finish_kernel, pieces, not partial), out...  6.98 us
  transfers between devices with their start and end apart: 26, of which 12 were waited for; matrix products, arithmetic and copies ran while one was open for 1% of the time, Pallas kernels for 12%

profile of v5, /device:TPU:1, one launch (start us, length us, event | category | flops | bytes accessed | tf_op | source)
XLA Modules:
  0.0 152.2 jit_solution(12553810953069922383)
XLA Ops:
  0.6 2.5 %slots.1 = (s32[16,2,128]{2,1,0:T(2,128)}, s32[8,2,128]{2,1,0:T(2,128)}) custom-call(s32[1,2048]{1,0:T(1,128)} %bitcast.31, s32[1,2048]{1,0:T(1,128)} %bitcast.32, s32[1,2048]{1,0:T(1,128)} %bitcast.33, s32[1,2048]{1,0:T(1,128)} %bitcast.34), custom_call_target="tpu_custom_call" | custom-call | flops 2750000128 | bytes 9000000 | tf_op jit(solution)/shard_map/slots/pallas_call | solution.py:96
  3.1 8.6 %all-to-all-start = ((s32[16,2,128]{2,1,0:T(2,128)}), s32[16,2,128]{2,1,0:T(2,128)S(1)}, u32[]{:S(2)}, u32[]{:S(2)}) async-start(s32[16,2,128]{2,1,0:T(2,128)} %get-tuple-element.32), calls=%async_computation | async-start | bytes 32768 | tf_op jit(solution)/shard_map/all_to_all | solution.py:605
  11.7 0.5 copy.19
  12.4 5.8 %all-to-all-done = s32[16,2,128]{2,1,0:T(2,128)S(1)} async-done(((s32[16,2,128]{2,1,0:T(2,128)}), s32[16,2,128]{2,1,0:T(2,128)S(1)}, u32[]{:S(2)}, u32[]{:S(2)}) %all-to-all-start) | async-done | bytes 16416 | tf_op jit(solution)/shard_map/all_to_all | solution.py:605
  18.2 5.2 %pick_rows.1 = bf16[16,128,128]{2,1,0:T(8,128)(2,1)S(1)} custom-call(s32[4096]{0:T(1024)S(1)} %bitcast.22, f32[4104,64]{1,0:T(8,128)S(1)} %pad_convert_fusion.table_ref), custom_call_target="tpu_custom_call" | custom-call | flops 7699999744 | bytes 25200000 | tf_op jit(solution)/shard_map/pick_rows/pallas_call | solution.py:148
  23.4 12.1 %all_to_all.25.returned_ref = bf16[16,128,128]{2,1,0:T(8,128)(2,1)S(1)} all-to-all(bf16[16,128,128]{2,1,0:T(8,128)(2,1)S(1)} %pick_rows.1), channel_id=1, replica_groups=mesh['seq'=16,'col'=8] {'seq'}, dimensions={0} | all-to-all | bytes 1048576 | tf_op jit(solution)/shard_map/all_to_all | solution.py:607
  35.6 2.8 %place_rows.1 = bf16[8,128,128]{2,1,0:T(8,128)(2,1)S(1)} custom-call(s32[2048]{0:T(1024)S(1)} %bitcast.25, bf16[16,128,128]{2,1,0:T(8,128)(2,1)S(1)} %all_to_all.25.returned_ref, bf16[64,256]{1,0:T(8,128)(2,1)S(1)} %bitcast.24), custom_call_target="tpu_custom_call" | custom-call | flops 4400000000 | bytes 14400000 | tf_op jit(solution)/shard_map/place_rows/pallas_call | solution.py:176
  38.4 13.8 %all_to_all.26.emb_ref = bf16[8,128,128]{2,1,0:T(8,128)(2,1)S(1)} all-to-all(bf16[8,128,128]{2,1,0:T(8,128)(2,1)S(1)} %place_rows.1), channel_id=1, replica_groups=mesh['seq'=16,'col'=8] {'col'}, dimensions={0} | all-to-all | bytes 524288 | tf_op jit(solution)/shard_map/all_to_all | solution.py:609
  52.2 11.9 %layers.1 = (bf16[256,512]{1,0:T(8,128)(2,1)}, bf16[8,128,128]{2,1,0:T(8,128)(2,1)}, bf16[4,176,512]{2,1,0:T(8,128)(2,1)S(1)}, bf16[4,176,512]{2,1,0:T(8,128)(2,...) custom-call(s32[8,2,128]{2,1,0:T(2,128)S(1)} %copy-done.5, ...), custom_call_target="tpu_custom_call" | custom-call | flops 17600000000 | bytes 57600000 | tf_op jit(solution)/shard_map/layers/pallas_call | solution.py:421
  64.1 1.1 collective-permute-start.1
  65.3 0.4 collective-permute-start.5
  65.8 1.2 collective-permute-done.1
  67.1 0.2 add_convert_fusion.3
  67.2 0.6 collective-permute-start.2
  67.9 0.2 collective-permute-done.3
  68.3 0.4 collective-permute-start.4
  68.7 0.4 collective-permute-done.5
  69.3 2.0 %collective-permute-start.6 = (bf16[4,176,512]{2,1,0:T(8,128)(2,1)S(1)}, bf16[4,176,512]{2,1,0:T(8,128)(2,1)S(1)}, u32[]{:S(2)}, u32[]{:S(2)}) collective-permute-start(bf16[4,176,512]{2,1,0:T(8,128)(2,1)S(1)} %add_convert_fusion.1), channel_id=1, source_target_pairs={{0,6},{1,25},{2,0},{3,27},{4,2},{5,29},{6,4},{7,31},{8,14},{9,1},{... | collective-permute-start | bytes 2162696 | tf_op jit(solution)/shard_map/ppermute | solution.py:478
  71.3 8.0 %collective-permute-done.2 = bf16[4,176,512]{2,1,0:T(8,128)(2,1)S(1)} collective-permute-done((bf16[4,176,512]{2,1,0:T(8,128)(2,1)S(1)}, bf16[4,176,512]{2,1,0:T(8,128)(2,1)S(1)}, u32[]{:S(2)}, u32[]{:S(2)}) %collective-permute-start.2) | collective-permute-done | bytes 720928 | tf_op jit(solution)/shard_map/ppermute | solution.py:478
  79.3 7.7 %collective-permute-done.4 = bf16[4,176,512]{2,1,0:T(8,128)(2,1)S(1)} collective-permute-done((bf16[4,176,512]{2,1,0:T(8,128)(2,1)S(1)}, bf16[4,176,512]{2,1,0:T(8,128)(2,1)S(1)}, u32[]{:S(2)}, u32[]{:S(2)}) %collective-permute-start.4) | collective-permute-done | bytes 720928 | tf_op jit(solution)/shard_map/ppermute | solution.py:478
  87.0 0.5 add_convert_fusion
  87.5 0.7 collective-permute-start.7
  88.2 1.4 collective-permute-start.9
  89.6 5.8 %all-to-all-start.3 = ((bf16[8,128,128]{2,1,0:T(8,128)(2,1)}), bf16[8,128,128]{2,1,0:T(8,128)(2,1)S(1)}, u32[]{:S(2)}, u32[]{:S(2)}) async-start(bf16[8,128,128]{2,1,0:T(8,128)(2,1)} %get-tuple-element.44), calls=%async_computation.3 | async-start | bytes 524288 | tf_op jit(solution)/shard_map/all_to_all | solution.py:614
  95.6 2.7 %collective-permute-start.12 = (bf16[176,512]{1,0:T(8,128)(2,1)S(1)}, bf16[176,512]{1,0:T(8,128)(2,1)S(1)}, u32[]{:S(2)}, u32[]{:S(2)}) collective-permute-start(bf16[176,512]{1,0:T(8,128)(2,1)S(1)} %fusion.1), channel_id=1, source_target_pairs={{0,96},{1,7},{2,98},{3,1},{4,100},{5,3},{6,102},{7,5},{8,104},{9,1... | collective-permute-start | bytes 540680 | tf_op jit(solution)/shard_map/ppermute | solution.py:478
  98.3 1.7 %collective-permute-start.10 = (bf16[176,512]{1,0:T(8,128)(2,1)S(1)}, bf16[176,512]{1,0:T(8,128)(2,1)S(1)}, u32[]{:S(2)}, u32[]{:S(2)}) collective-permute-start(bf16[176,512]{1,0:T(8,128)(2,1)S(1)} %fusion.1), channel_id=1, source_target_pairs={{0,64},{1,5},{2,66},{3,7},{4,68},{5,1},{6,70},{7,3},{8,72},{9,13},... | collective-permute-start | bytes 540680 | tf_op jit(solution)/shard_map/ppermute | solution.py:478
  100.0 2.1 %all-to-all-done.3.grad_ref = bf16[8,128,128]{2,1,0:T(8,128)(2,1)S(1)} async-done(((bf16[8,128,128]{2,1,0:T(8,128)(2,1)}), bf16[8,128,128]{2,1,0:T(8,128)(2,1)S(1)}, u32[]{:S(2)}, u32[]{:S(2)}) %all-to-all-start.3) | async-done | bytes 262176 | tf_op jit(solution)/shard_map/all_to_all | solution.py:614
  102.1 3.6 %return_rows.1 = bf16[16,128,128]{2,1,0:T(8,128)(2,1)} custom-call(s32[2048]{0:T(1024)S(1)} %bitcast.26, bf16[8,128,128]{2,1,0:T(8,128)(2,1)S(1)} %all-to-all-done.3.grad_ref), custom_call_target="tpu_custom_call" | custom-call | flops 4400000000 | bytes 14400000 | tf_op jit(solution)/shard_map/return_rows/pallas_call | solution.py:204
  105.7 4.6 %all-to-all-start.4 = ((bf16[16,128,128]{2,1,0:T(8,128)(2,1)}), bf16[16,128,128]{2,1,0:T(8,128)(2,1)S(1)}, u32[]{:S(2)}, u32[]{:S(2)}) async-start(bf16[16,128,128]{2,1,0:T(8,128)(2,1)} %return_rows.1), calls=%async_computation.4 | async-start | bytes 1048576 | tf_op jit(solution)/shard_map/all_to_all | solution.py:620
  110.5 1.4 collective-permute-start.15
  111.9 2.4 %collective-permute-start.14 = (bf16[176,512]{1,0:T(8,128)(2,1)S(1)}, bf16[176,512]{1,0:T(8,128)(2,1)S(1)}, u32[]{:S(2)}, u32[]{:S(2)}) collective-permute-start(bf16[176,512]{1,0:T(8,128)(2,1)S(1)} %add_convert_fusion.5), channel_id=1, source_target_pairs={{0,16},{1,65},{2,18},{3,67},{4,20},{5,69},{6,22},{7,71},{8,24},{9,... | collective-permute-start | bytes 540680 | tf_op jit(solution)/shard_map/ppermute | solution.py:478
  114.3 1.2 collective-permute-start.13
  115.5 5.4 %collective-permute-done.15 = bf16[176,512]{1,0:T(8,128)(2,1)S(1)} collective-permute-done((bf16[176,512]{1,0:T(8,128)(2,1)S(1)}, bf16[176,512]{1,0:T(8,128)(2,1)S(1)}, u32[]{:S(2)}, u32[]{:S(2)}) %collective-permute-start.15) | collective-permute-done | bytes 180256 | tf_op jit(solution)/shard_map/ppermute | solution.py:478
  120.9 3.3 %collective-permute-done.14 = bf16[176,512]{1,0:T(8,128)(2,1)S(1)} collective-permute-done((bf16[176,512]{1,0:T(8,128)(2,1)S(1)}, bf16[176,512]{1,0:T(8,128)(2,1)S(1)}, u32[]{:S(2)}, u32[]{:S(2)}) %collective-permute-start.14) | collective-permute-done | bytes 180256 | tf_op jit(solution)/shard_map/ppermute | solution.py:478
  124.3 0.5 collective-permute-start.19
  124.8 0.7 collective-permute-start.18
  125.5 2.2 %collective-permute-start.17 = (bf16[4,176,512]{2,1,0:T(8,128)(2,1)S(1)}, bf16[4,176,512]{2,1,0:T(8,128)(2,1)S(1)}, u32[]{:S(2)}, u32[]{:S(2)}) collective-permute-start(bf16[4,176,512]{2,1,0:T(8,128)(2,1)S(1)} %pad_maximum_fusion.refs_0_), channel_id=1, source_target_pairs={{0,4},{1,17},{2,6},{3,19},{4,0},{5,21},{6,2},{7,23},{8,12},{9,25},... | collective-permute-start | bytes 2162696 | tf_op jit(solution)/shard_map/ppermute | solution.py:478
  127.7 1.2 collective-permute-start.16
  128.9 9.5 %scatter_rows.1 = f32[64,4096]{1,0:T(8,128)} custom-call(s32[4096]{0:T(1024)S(1)} %bitcast.23, bf16[16,128,128]{2,1,0:T(8,128)(2,1)S(1)} %all-to-all-done.4.incoming_ref), custom_call_target="tpu_custom_call" | custom-call | flops 12099999744 | bytes 39600000 | tf_op jit(solution)/shard_map/scatter_rows/pallas_call | solution.py:251
  138.4 2.7 %widen_sums.3 = (f32[2,512,2048]{2,1,0:T(8,128)}, f32[2,512,512]{2,1,0:T(8,128)}) custom-call(bf16[4,176,512]{2,1,0:T(8,128)(2,1)S(1)} %pad_maximum_fusion.refs_0_, bf16[4,176,512]{2,1,0:T(8,128)(2,1)} %collective-permute-done.19.refs_1_), custom_call_target="tpu_custom_call" | custom-call | flops 1870000000 | bytes 6120000 | tf_op jit(solution)/shard_map/widen_sums/pallas_call | solution.py:547
  141.1 3.0 %collective-permute-done.17.refs_1_ = bf16[4,176,512]{2,1,0:T(8,128)(2,1)S(1)} collective-permute-done((bf16[4,176,512]{2,1,0:T(8,128)(2,1)S(1)}, bf16[4,176,512]{2,1,0:T(8,128)(2,1)S(1)}, u32[]{:S(2)}, u32[]{:S(2)}) %collective-permute-start.17) | collective-permute-done | bytes 720928 | tf_op jit(solution)/shard_map/ppermute | solution.py:478
  144.2 0.6 collective-permute-done.16.refs_0_
  144.8 1.2 collective-permute-start.20
  146.0 0.5 collective-permute-start.22
  146.6 0.9 hot_sums.1
  147.4 2.1 %widen_sums.4 = (f32[2,512,2048]{2,1,0:T(8,128)}, f32[2,512,512]{2,1,0:T(8,128)}) custom-call(bf16[4,176,512]{2,1,0:T(8,128)(2,1)S(1)} %collective-permute-done.16.refs_0_, bf16[4,176,512]{2,1,0:T(8,128)(2,1)S(1)} %collective-permute-done.17.refs_1_, ...), custom_call_target="tpu_custom_call", output_to_operand_aliasing={{0}: (3, {}), {1}: (4, {})} | custom-call | flops 2529999872 | bytes 8279999 | tf_op jit(solution)/shard_map/widen_sums/pallas_call | solution.py:547
  149.6 0.3 collective-permute-done.22.refs_2_
  149.9 2.1 %widen_sums.5 = (f32[2,512,2048]{2,1,0:T(8,128)}, f32[2,512,512]{2,1,0:T(8,128)}) custom-call(bf16[4,176,512]{2,1,0:T(8,128)(2,1)S(1)} %collective-permute-done.20.refs_0_, bf16[4,176,512]{2,1,0:T(8,128)(2,1)S(1)} %collective-permute-done.21.refs_1_, ...), custom_call_target="tpu_custom_call", output_to_operand_aliasing={{0}: (3, {}), {1}: (4, {})} | custom-call | flops 2529999872 | bytes 8279999 | tf_op jit(solution)/shard_map/widen_sums/pallas_call | solution.py:547
  (44 shorter events, 1.1 us)
Async XLA Ops:
  0.6 11.1 %copy-start.6 = (bf16[4096,64]{0,1:T(8,128)(2,1)S(1)}, bf16[4096,64]{0,1:T(8,128)(2,1)}, u32[]{:S(2)}) copy-start(bf16[4096,64]{0,1:T(8,128)(2,1)} %param.10) | copy-start | bytes 1572868
  3.1 15.0 %all-to-all-start = ((s32[16,2,128]{2,1,0:T(2,128)}), s32[16,2,128]{2,1,0:T(2,128)S(1)}, u32[]{:S(2)}, u32[]{:S(2)}) async-start(s32[16,2,128]{2,1,0:T(2,128)} %get-tuple-element.32), calls=%async_computation | async-start | bytes 32768 | tf_op jit(solution)/shard_map/all_to_all | solution.py:605
  18.2 17.4 %copy-start.3 = (bf16[256,64]{0,1:T(8,128)(2,1)S(1)}, bf16[256,64]{0,1:T(8,128)(2,1)}, u32[]{:S(2)}) copy-start(bf16[256,64]{0,1:T(8,128)(2,1)} %param.11) | copy-start | bytes 98308
  18.2 17.4 %copy-start.5 = (s32[8,2,128]{2,1,0:T(2,128)S(1)}, s32[8,2,128]{2,1,0:T(2,128)}, u32[]{:S(2)}) copy-start(s32[8,2,128]{2,1,0:T(2,128)} %get-tuple-element.31.index_ref) | copy-start | bytes 24580
  35.6 16.6 %copy-start = (bf16[2,512,2048]{2,1,0:T(8,128)(2,1)S(1)}, bf16[2,512,2048]{2,1,0:T(8,128)(2,1)}, u32[]{:S(2)}) copy-start(bf16[2,512,2048]{2,1,0:T(8,128)(2,1)} %win_ref.1) | copy-start | bytes 12582916
  35.6 16.6 %copy-start.1 = (bf16[2,512,512]{2,1,0:T(8,128)(2,1)S(1)}, bf16[2,512,512]{2,1,0:T(8,128)(2,1)}, u32[]{:S(2)}) copy-start(bf16[2,512,512]{2,1,0:T(8,128)(2,1)} %wout_ref.1) | copy-start | bytes 3145732
  35.6 16.6 %copy-start.2 = (bf16[256,512]{1,0:T(8,128)(2,1)S(1)}, bf16[256,512]{1,0:T(8,128)(2,1)}, u32[]{:S(2)}) copy-start(bf16[256,512]{1,0:T(8,128)(2,1)} %cot_ref.1) | copy-start | bytes 786436
  35.6 16.6 %copy-start.4 = (s32[1,256]{1,0:T(1,128)S(1)}, s32[1,256]{1,0:T(1,128)}, u32[]{:S(2)}) copy-start(s32[1,256]{1,0:T(1,128)} %segment_ref.1) | copy-start | bytes 3076
  64.1 2.9 %collective-permute-start.1 = (bf16[4,176,512]{2,1,0:T(8,128)(2,1)S(1)}, bf16[4,176,512]{2,1,0:T(8,128)(2,1)S(1)}, u32[]{:S(2)}, u32[]{:S(2)}) collective-permute-start(bf16[4,176,512]{2,1,0:T(8,128)(2,1)S(1)} %get-tuple-element.37), channel_id=1, source_target_pairs={{0,1},{1,0},{2,3},{3,2},{4,5},{5,4},{6,7},{7,6},{8,9},{9,8},{10,11... | collective-permute-start | bytes 2162696 | tf_op jit(solution)/shard_map/ppermute | solution.py:468
  65.2 2.8 %collective-permute-start.3 = (bf16[4,176,512]{2,1,0:T(8,128)(2,1)S(1)}, bf16[4,176,512]{2,1,0:T(8,128)(2,1)S(1)}, u32[]{:S(2)}, u32[]{:S(2)}) collective-permute-start(bf16[4,176,512]{2,1,0:T(8,128)(2,1)S(1)} %get-tuple-element.39), channel_id=1, source_target_pairs={{0,1},{1,0},{2,3},{3,2},{4,5},{5,4},{6,7},{7,6},{8,9},{9,8},{10,11... | collective-permute-start | bytes 2162696 | tf_op jit(solution)/shard_map/ppermute | solution.py:468
  65.3 3.8 %collective-permute-start.5 = (bf16[4,176,512]{2,1,0:T(8,128)(2,1)S(1)}, bf16[4,176,512]{2,1,0:T(8,128)(2,1)S(1)}, u32[]{:S(2)}, u32[]{:S(2)}) collective-permute-start(bf16[4,176,512]{2,1,0:T(8,128)(2,1)S(1)} %get-tuple-element.41), channel_id=1, source_target_pairs={{0,1},{1,0},{2,3},{3,2},{4,5},{5,4},{6,7},{7,6},{8,9},{9,8},{10,11... | collective-permute-start | bytes 2162696 | tf_op jit(solution)/shard_map/ppermute | solution.py:468
  65.7 5.5 %collective-permute-start = (bf16[4,176,512]{2,1,0:T(8,128)(2,1)S(1)}, bf16[4,176,512]{2,1,0:T(8,128)(2,1)S(1)}, u32[]{:S(2)}, u32[]{:S(2)}) collective-permute-start(bf16[4,176,512]{2,1,0:T(8,128)(2,1)S(1)} %get-tuple-element.35), channel_id=1, source_target_pairs={{0,1},{1,0},{2,3},{3,2},{4,5},{5,4},{6,7},{7,6},{8,9},{9,8},{10,11... | collective-permute-start | bytes 2162696 | tf_op jit(solution)/shard_map/ppermute | solution.py:468
  67.2 12.1 %collective-permute-start.2 = (bf16[4,176,512]{2,1,0:T(8,128)(2,1)S(1)}, bf16[4,176,512]{2,1,0:T(8,128)(2,1)S(1)}, u32[]{:S(2)}, u32[]{:S(2)}) collective-permute-start(bf16[4,176,512]{2,1,0:T(8,128)(2,1)S(1)} %add_convert_fusion.3), channel_id=1, source_target_pairs={{0,4},{1,17},{2,6},{3,19},{4,0},{5,21},{6,2},{7,23},{8,12},{9,25},... | collective-permute-start | bytes 2162696 | tf_op jit(solution)/shard_map/ppermute | solution.py:478
  68.3 18.7 %collective-permute-start.4 = (bf16[4,176,512]{2,1,0:T(8,128)(2,1)S(1)}, bf16[4,176,512]{2,1,0:T(8,128)(2,1)S(1)}, u32[]{:S(2)}, u32[]{:S(2)}) collective-permute-start(bf16[4,176,512]{2,1,0:T(8,128)(2,1)S(1)} %add_convert_fusion.2), channel_id=1, source_target_pairs={{0,2},{1,9},{2,4},{3,11},{4,6},{5,13},{6,0},{7,15},{8,10},{9,17},{... | collective-permute-start | bytes 2162696 | tf_op jit(solution)/shard_map/ppermute | solution.py:478
  69.3 17.7 %collective-permute-start.6 = (bf16[4,176,512]{2,1,0:T(8,128)(2,1)S(1)}, bf16[4,176,512]{2,1,0:T(8,128)(2,1)S(1)}, u32[]{:S(2)}, u32[]{:S(2)}) collective-permute-start(bf16[4,176,512]{2,1,0:T(8,128)(2,1)S(1)} %add_convert_fusion.1), channel_id=1, source_target_pairs={{0,6},{1,25},{2,0},{3,27},{4,2},{5,29},{6,4},{7,31},{8,14},{9,1},{... | collective-permute-start | bytes 2162696 | tf_op jit(solution)/shard_map/ppermute | solution.py:478
  87.5 7.9 %collective-permute-start.7 = (bf16[176,512]{1,0:T(8,128)(2,1)S(1)}, bf16[176,512]{1,0:T(8,128)(2,1)S(1)}, u32[]{:S(2)}, u32[]{:S(2)}) collective-permute-start(bf16[176,512]{1,0:T(8,128)(2,1)S(1)} %get-tuple-element.57), channel_id=1, source_target_pairs={{0,16},{1,65},{2,18},{3,67},{4,20},{5,69},{6,22},{7,71},{8,24},{9,... | collective-permute-start | bytes 540680 | tf_op jit(solution)/shard_map/ppermute | solution.py:478
  88.2 7.3 %collective-permute-start.9 = (bf16[176,512]{1,0:T(8,128)(2,1)S(1)}, bf16[176,512]{1,0:T(8,128)(2,1)S(1)}, u32[]{:S(2)}, u32[]{:S(2)}) collective-permute-start(bf16[176,512]{1,0:T(8,128)(2,1)S(1)} %get-tuple-element.58), channel_id=1, source_target_pairs={{0,24},{1,97},{2,26},{3,99},{4,28},{5,101},{6,30},{7,103},{8,0},{9... | collective-permute-start | bytes 540680 | tf_op jit(solution)/shard_map/ppermute | solution.py:478
  89.6 5.8 %collective-permute-start.8 = (bf16[176,512]{1,0:T(8,128)(2,1)S(1)}, bf16[176,512]{1,0:T(8,128)(2,1)S(1)}, u32[]{:S(2)}, u32[]{:S(2)}) collective-permute-start(bf16[176,512]{1,0:T(8,128)(2,1)S(1)} %get-tuple-element.59), channel_id=1, source_target_pairs={{0,8},{1,33},{2,10},{3,35},{4,12},{5,37},{6,14},{7,39},{8,16},{9,4... | collective-permute-start | bytes 540680 | tf_op jit(solution)/shard_map/ppermute | solution.py:478
  89.6 12.4 %all-to-all-start.3 = ((bf16[8,128,128]{2,1,0:T(8,128)(2,1)}), bf16[8,128,128]{2,1,0:T(8,128)(2,1)S(1)}, u32[]{:S(2)}, u32[]{:S(2)}) async-start(bf16[8,128,128]{2,1,0:T(8,128)(2,1)} %get-tuple-element.44), calls=%async_computation.3 | async-start | bytes 524288 | tf_op jit(solution)/shard_map/all_to_all | solution.py:614
  95.6 14.8 %collective-permute-start.12 = (bf16[176,512]{1,0:T(8,128)(2,1)S(1)}, bf16[176,512]{1,0:T(8,128)(2,1)S(1)}, u32[]{:S(2)}, u32[]{:S(2)}) collective-permute-start(bf16[176,512]{1,0:T(8,128)(2,1)S(1)} %fusion.1), channel_id=1, source_target_pairs={{0,96},{1,7},{2,98},{3,1},{4,100},{5,3},{6,102},{7,5},{8,104},{9,1... | collective-permute-start | bytes 540680 | tf_op jit(solution)/shard_map/ppermute | solution.py:478
  98.3 12.1 %collective-permute-start.11 = (bf16[176,512]{1,0:T(8,128)(2,1)S(1)}, bf16[176,512]{1,0:T(8,128)(2,1)S(1)}, u32[]{:S(2)}, u32[]{:S(2)}) collective-permute-start(bf16[176,512]{1,0:T(8,128)(2,1)S(1)} %fusion.1), channel_id=1, source_target_pairs={{0,32},{1,3},{2,34},{3,5},{4,36},{5,7},{6,38},{7,1},{8,40},{9,11},... | collective-permute-start | bytes 540680 | tf_op jit(solution)/shard_map/ppermute | solution.py:478
  98.3 12.1 %collective-permute-start.10 = (bf16[176,512]{1,0:T(8,128)(2,1)S(1)}, bf16[176,512]{1,0:T(8,128)(2,1)S(1)}, u32[]{:S(2)}, u32[]{:S(2)}) collective-permute-start(bf16[176,512]{1,0:T(8,128)(2,1)S(1)} %fusion.1), channel_id=1, source_target_pairs={{0,64},{1,5},{2,66},{3,7},{4,68},{5,1},{6,70},{7,3},{8,72},{9,13},... | collective-permute-start | bytes 540680 | tf_op jit(solution)/shard_map/ppermute | solution.py:478
  105.7 23.2 %all-to-all-start.4 = ((bf16[16,128,128]{2,1,0:T(8,128)(2,1)}), bf16[16,128,128]{2,1,0:T(8,128)(2,1)S(1)}, u32[]{:S(2)}, u32[]{:S(2)}) async-start(bf16[16,128,128]{2,1,0:T(8,128)(2,1)} %return_rows.1), calls=%async_computation.4 | async-start | bytes 1048576 | tf_op jit(solution)/shard_map/all_to_all | solution.py:620
  110.5 10.4 %collective-permute-start.15 = (bf16[176,512]{1,0:T(8,128)(2,1)S(1)}, bf16[176,512]{1,0:T(8,128)(2,1)S(1)}, u32[]{:S(2)}, u32[]{:S(2)}) collective-permute-start(bf16[176,512]{1,0:T(8,128)(2,1)S(1)} %add_convert_fusion.5), channel_id=1, source_target_pairs={{0,8},{1,33},{2,10},{3,35},{4,12},{5,37},{6,14},{7,39},{8,16},{9,4... | collective-permute-start | bytes 540680 | tf_op jit(solution)/shard_map/ppermute | solution.py:478
  111.9 12.3 %collective-permute-start.14 = (bf16[176,512]{1,0:T(8,128)(2,1)S(1)}, bf16[176,512]{1,0:T(8,128)(2,1)S(1)}, u32[]{:S(2)}, u32[]{:S(2)}) collective-permute-start(bf16[176,512]{1,0:T(8,128)(2,1)S(1)} %add_convert_fusion.5), channel_id=1, source_target_pairs={{0,16},{1,65},{2,18},{3,67},{4,20},{5,69},{6,22},{7,71},{8,24},{9,... | collective-permute-start | bytes 540680 | tf_op jit(solution)/shard_map/ppermute | solution.py:478
  114.3 9.9 %collective-permute-start.13 = (bf16[176,512]{1,0:T(8,128)(2,1)S(1)}, bf16[176,512]{1,0:T(8,128)(2,1)S(1)}, u32[]{:S(2)}, u32[]{:S(2)}) collective-permute-start(bf16[176,512]{1,0:T(8,128)(2,1)S(1)} %add_convert_fusion.5), channel_id=1, source_target_pairs={{0,24},{1,97},{2,26},{3,99},{4,28},{5,101},{6,30},{7,103},{8,0},{9... | collective-permute-start | bytes 540680 | tf_op jit(solution)/shard_map/ppermute | solution.py:478
  124.3 14.1 %collective-permute-start.19 = (bf16[4,176,512]{2,1,0:T(8,128)(2,1)S(1)}, bf16[4,176,512]{2,1,0:T(8,128)(2,1)}, u32[]{:S(2)}, u32[]{:S(2)}) collective-permute-start(bf16[4,176,512]{2,1,0:T(8,128)(2,1)S(1)} %pad_maximum_fusion.refs_0_), channel_id=1, source_target_pairs={{0,1},{1,0},{2,3},{3,2},{4,5},{5,4},{6,7},{7,6},{8,9},{9,8},{10,11... | collective-permute-start | bytes 2162696 | tf_op jit(solution)/shard_map/ppermute | solution.py:468
  124.8 16.3 %collective-permute-start.18 = (bf16[4,176,512]{2,1,0:T(8,128)(2,1)S(1)}, bf16[4,176,512]{2,1,0:T(8,128)(2,1)S(1)}, u32[]{:S(2)}, u32[]{:S(2)}) collective-permute-start(bf16[4,176,512]{2,1,0:T(8,128)(2,1)S(1)} %pad_maximum_fusion.refs_0_), channel_id=1, source_target_pairs={{0,2},{1,9},{2,4},{3,11},{4,6},{5,13},{6,0},{7,15},{8,10},{9,17},{... | collective-permute-start | bytes 2162696 | tf_op jit(solution)/shard_map/ppermute | solution.py:478
  125.5 18.7 %collective-permute-start.17 = (bf16[4,176,512]{2,1,0:T(8,128)(2,1)S(1)}, bf16[4,176,512]{2,1,0:T(8,128)(2,1)S(1)}, u32[]{:S(2)}, u32[]{:S(2)}) collective-permute-start(bf16[4,176,512]{2,1,0:T(8,128)(2,1)S(1)} %pad_maximum_fusion.refs_0_), channel_id=1, source_target_pairs={{0,4},{1,17},{2,6},{3,19},{4,0},{5,21},{6,2},{7,23},{8,12},{9,25},... | collective-permute-start | bytes 2162696 | tf_op jit(solution)/shard_map/ppermute | solution.py:478
  127.7 17.1 %collective-permute-start.16 = (bf16[4,176,512]{2,1,0:T(8,128)(2,1)S(1)}, bf16[4,176,512]{2,1,0:T(8,128)(2,1)S(1)}, u32[]{:S(2)}, u32[]{:S(2)}) collective-permute-start(bf16[4,176,512]{2,1,0:T(8,128)(2,1)S(1)} %pad_maximum_fusion.refs_0_), channel_id=1, source_target_pairs={{0,6},{1,25},{2,0},{3,27},{4,2},{5,29},{6,4},{7,31},{8,14},{9,1},{... | collective-permute-start | bytes 2162696 | tf_op jit(solution)/shard_map/ppermute | solution.py:478
  144.8 4.8 %collective-permute-start.20 = (bf16[4,176,512]{2,1,0:T(8,128)(2,1)S(1)}, bf16[4,176,512]{2,1,0:T(8,128)(2,1)S(1)}, u32[]{:S(2)}, u32[]{:S(2)}) collective-permute-start(bf16[4,176,512]{2,1,0:T(8,128)(2,1)S(1)} %collective-permute-done.16.refs_0_), channel_id=1, source_target_pairs={{0,1},{1,0},{2,3},{3,2},{4,5},{5,4},{6,7},{7,6},{8,9},{9,8},{10,11... | collective-permute-start | bytes 2162696 | tf_op jit(solution)/shard_map/ppermute | solution.py:468
  146.0 3.6 %collective-permute-start.21 = (bf16[4,176,512]{2,1,0:T(8,128)(2,1)S(1)}, bf16[4,176,512]{2,1,0:T(8,128)(2,1)S(1)}, u32[]{:S(2)}, u32[]{:S(2)}) collective-permute-start(bf16[4,176,512]{2,1,0:T(8,128)(2,1)S(1)} %collective-permute-done.17.refs_1_), channel_id=1, source_target_pairs={{0,1},{1,0},{2,3},{3,2},{4,5},{5,4},{6,7},{7,6},{8,9},{9,8},{10,11... | collective-permute-start | bytes 2162696 | tf_op jit(solution)/shard_map/ppermute | solution.py:468
  146.0 3.9 %collective-permute-start.22 = (bf16[4,176,512]{2,1,0:T(8,128)(2,1)S(1)}, bf16[4,176,512]{2,1,0:T(8,128)(2,1)S(1)}, u32[]{:S(2)}, u32[]{:S(2)}) collective-permute-start(bf16[4,176,512]{2,1,0:T(8,128)(2,1)S(1)} %collective-permute-done.18.refs_2_), channel_id=1, source_target_pairs={{0,1},{1,0},{2,3},{3,2},{4,5},{5,4},{6,7},{7,6},{8,9},{9,8},{10,11... | collective-permute-start | bytes 2162696 | tf_op jit(solution)/shard_map/ppermute | solution.py:468

commit v6 on v5

--- a/solution.py
+++ b/solution.py
@@ -65,26 +65,26 @@
     upper = jnp.where(
         lax.broadcasted_iota(I32, (TOK, TOK), 0) <= lax.broadcasted_iota(I32, (TOK, TOK), 1), 1.0, 0.0
     ).astype(BF16)
+    item = item_ref[...]
+    parts = jnp.concatenate(
+        [member * (item >> 6).astype(F32), member * (item & 63).astype(F32), member], axis=0
+    ).astype(BF16)
+    spans = [slice(block * TOK, (block + 1) * TOK) for block in range(N_COL)]
+    counts = [mm(member_b[:, span], upper) for span in spans]
     carry = jnp.zeros((N_SEQ, 1), F32)
-    requests = jnp.zeros((3 * N_SEQ, CAP), F32)
-    item = item_ref[...]
-    high = (item >> 6).astype(F32)
-    low = (item & 63).astype(F32)
-    for block in range(N_COL):
-        span = slice(block * TOK, (block + 1) * TOK)
-        here = member[:, span]
-        count = mm(member_b[:, span], upper) + carry
-        carry = count[:, TOK - 1 : TOK]
-        slot = jnp.sum((count - 1.0) * here, axis=0, keepdims=True).astype(I32)
+    slots = lax.broadcasted_iota(I32, (CAP, TOK), 0)
+    picks = []
+    for block, span in enumerate(spans):
+        count = counts[block] + carry
+        carry = carry + counts[block][:, TOK - 1 : TOK]
+        slot = jnp.sum((count - 1.0) * member[:, span], axis=0, keepdims=True).astype(I32)
         place = jnp.where(
             regular[:, span], owner[:, span] * CAP + slot, SLOTS + hot_ref[:, span]
         )
         index_ref[block, 0:1, :] = place[:, :128]
         index_ref[block, 1:2, :] = place[:, 128:]
-        slots = lax.broadcasted_iota(I32, (CAP, TOK), 0)
-        pick = jnp.where(slots == slot, 1.0, 0.0).astype(BF16)
-        parts = jnp.concatenate([here * high[:, span], here * low[:, span], here], axis=0)
-        requests += mm(parts.astype(BF16), pick, NT)
+        picks.append(jnp.where(slots == slot, 1.0, 0.0).astype(BF16))
+    requests = mm(parts, jnp.concatenate(picks, axis=1), NT)
     rows = requests[:N_SEQ] * 64.0 + requests[N_SEQ : 2 * N_SEQ]
     rows = jnp.where(requests[2 * N_SEQ :] > 0.5, rows, float(ITEMS_DEV))
     rows = rows.astype(I32)
@@ -363,7 +363,6 @@
 
         grad = stream[...]
         grad_b = grad.astype(BF16)
-        put(4, mm(gated[l], grad_b, TN).astype(BF16))
         dgated = mm(grad_b, wout_ref[l], NT).astype(BF16).astype(F32)
         hat = mixed[l]
         dproj[0] = ((dgated * hat).astype(BF16).astype(F32) * slope[l, 0]).astype(BF16)
@@ -388,6 +387,7 @@
         for part in range(4):
             dpre = dproj[part]
             dnormed += mm(dpre, win_ref[l, :, part * D : (part + 1) * D], NT)
+        put(4, mm(gated[l], grad_b, TN).astype(BF16))
         for part in range(4):
             put(part, mm(rounded, dproj[part], TN).astype(BF16))
         dnormed = dnormed.astype(BF16).astype(F32)

time: 153 us -> 152 us (level)
  Pallas kernels: 43.4 us -> 38 us
  waiting for transfers between devices: 38.1 us -> 41 us
  blocking collectives: 25.9 us -> 27.6 us
    ppermute x15, waiting for transfers between devices: 28.1 us -> 31 us  [along(): return lax.ppermute(value, BOTH, device_pairs(move))]
    pallas_call x1, Pallas kernels: 9.46 us -> 6.54 us  [scatter_rows(): pl.pallas_call(scatter_kernel, out_shape=jax.ShapeDtypeStruct((COLS, ITEM...]
    all_to_all x1, blocking collectives: 12.1 us -> 13.8 us  [on_device(): lax.all_to_all(picked, 'seq', split_axis=0, concat_axis=0, tiled=True)]
    pallas_call x1, Pallas kernels: 5.24 us -> 3.64 us  [pick_rows(): pl.pallas_call(pick_kernel, out_shape=jax.ShapeDtypeStruct((N_SEQ, 128, 1...]
  transfers between devices with their start and end apart: 26 -> 26, of which waited for: 12 -> 12; matrix products, arithmetic and copies ran while one was open for 1% -> 1% of each run, Pallas kernels for 12% -> 10%
where the time goes in v6:
time: 152 us
  starting transfers between devices  41.8 us (28%)
  waiting for transfers between devices  41 us (27%)
  Pallas kernels  38 us (25%)
  blocking collectives  27.6 us (18%)
    ppermute x15, waiting for transfers between devices, along(): return lax.ppermute(value, BOTH, device_pairs(move))  31 us
    ppermute x15, starting transfers between devices, along(): return lax.ppermute(value, BOTH, device_pairs(move))  18.7 us
    all_to_all x1, blocking collectives, on_device(): lax.all_to_all(picked, 'seq', split_axis=0, concat_axis=0, tiled=True)  13.8 us
    all_to_all x1, blocking collectives, on_device(): emb = lax.all_to_all(placed, 'col', split_axis=0, concat_axis=0, tiled=True)  13.8 us
    pallas_call x1, Pallas kernels, run_stack(): pl.pallas_call(stack_kernel, out_shape=(jax.ShapeDtypeStruct((TOK, D), BF...  11.5 us
    all_to_all x1, starting transfers between devices, on_device(): lax.all_to_all(requests, 'seq', split_axis=0, concat_axis=0, tiled=True)  8.6 us
    pallas_call x3, Pallas kernels, finish(): pl.pallas_call(functools.partial(finish_kernel, pieces, not partial), out...  6.98 us
    pallas_call x1, Pallas kernels, scatter_rows(): pl.pallas_call(scatter_kernel, out_shape=jax.ShapeDtypeStruct((COLS, ITEM...  6.54 us
  transfers between devices with their start and end apart: 26, of which 12 were waited for; matrix products, arithmetic and copies ran while one was open for 1% of the time, Pallas kernels for 10%

profile of v6, /device:TPU:1, one launch (start us, length us, event | category | flops | bytes accessed | tf_op | source)
XLA Modules:
  0.0 151.6 jit_solution(6493617941683962259)
XLA Ops:
  0.6 2.1 %slots.1 = (s32[16,2,128]{2,1,0:T(2,128)}, s32[8,2,128]{2,1,0:T(2,128)}) custom-call(s32[1,2048]{1,0:T(1,128)} %bitcast.31, s32[1,2048]{1,0:T(1,128)} %bitcast.32, s32[1,2048]{1,0:T(1,128)} %bitcast.33, s32[1,2048]{1,0:T(1,128)} %bitcast.34), custom_call_target="tpu_custom_call" | custom-call | flops 2750000128 | bytes 9000000 | tf_op jit(solution)/shard_map/slots/pallas_call | solution.py:96
  2.7 8.6 %all-to-all-start = ((s32[16,2,128]{2,1,0:T(2,128)}), s32[16,2,128]{2,1,0:T(2,128)S(1)}, u32[]{:S(2)}, u32[]{:S(2)}) async-start(s32[16,2,128]{2,1,0:T(2,128)} %get-tuple-element.32), calls=%async_computation | async-start | bytes 32768 | tf_op jit(solution)/shard_map/all_to_all | solution.py:605
  11.3 0.5 copy.19
  12.0 5.8 %all-to-all-done = s32[16,2,128]{2,1,0:T(2,128)S(1)} async-done(((s32[16,2,128]{2,1,0:T(2,128)}), s32[16,2,128]{2,1,0:T(2,128)S(1)}, u32[]{:S(2)}, u32[]{:S(2)}) %all-to-all-start) | async-done | bytes 16416 | tf_op jit(solution)/shard_map/all_to_all | solution.py:605
  17.8 3.6 %pick_rows.1 = bf16[16,128,128]{2,1,0:T(8,128)(2,1)S(1)} custom-call(s32[4096]{0:T(1024)S(1)} %bitcast.22, f32[4104,64]{1,0:T(8,128)S(1)} %pad_convert_fusion.table_ref), custom_call_target="tpu_custom_call" | custom-call | flops 7699999744 | bytes 25200000 | tf_op jit(solution)/shard_map/pick_rows/pallas_call | solution.py:148
  21.4 13.8 %all_to_all.25.returned_ref = bf16[16,128,128]{2,1,0:T(8,128)(2,1)S(1)} all-to-all(bf16[16,128,128]{2,1,0:T(8,128)(2,1)S(1)} %pick_rows.1), channel_id=1, replica_groups=mesh['seq'=16,'col'=8] {'seq'}, dimensions={0} | all-to-all | bytes 1048576 | tf_op jit(solution)/shard_map/all_to_all | solution.py:607
  35.3 2.8 %place_rows.1 = bf16[8,128,128]{2,1,0:T(8,128)(2,1)S(1)} custom-call(s32[2048]{0:T(1024)S(1)} %bitcast.25, bf16[16,128,128]{2,1,0:T(8,128)(2,1)S(1)} %all_to_all.25.returned_ref, bf16[64,256]{1,0:T(8,128)(2,1)S(1)} %bitcast.24), custom_call_target="tpu_custom_call" | custom-call | flops 4400000000 | bytes 14400000 | tf_op jit(solution)/shard_map/place_rows/pallas_call | solution.py:176
  38.1 13.8 %all_to_all.26.emb_ref = bf16[8,128,128]{2,1,0:T(8,128)(2,1)S(1)} all-to-all(bf16[8,128,128]{2,1,0:T(8,128)(2,1)S(1)} %place_rows.1), channel_id=1, replica_groups=mesh['seq'=16,'col'=8] {'col'}, dimensions={0} | all-to-all | bytes 524288 | tf_op jit(solution)/shard_map/all_to_all | solution.py:609
  51.9 11.5 %layers.1 = (bf16[256,512]{1,0:T(8,128)(2,1)}, bf16[8,128,128]{2,1,0:T(8,128)(2,1)}, bf16[4,176,512]{2,1,0:T(8,128)(2,1)S(1)}, bf16[4,176,512]{2,1,0:T(8,128)(2,...) custom-call(s32[8,2,128]{2,1,0:T(2,128)S(1)} %copy-done.5, ...), custom_call_target="tpu_custom_call" | custom-call | flops 17600000000 | bytes 57600000 | tf_op jit(solution)/shard_map/layers/pallas_call | solution.py:421
  63.4 1.3 collective-permute-start.1
  64.8 0.4 collective-permute-start.5
  65.3 1.2 collective-permute-done.1
  66.5 0.2 add_convert_fusion.3
  66.7 0.6 collective-permute-start.2
  67.3 0.2 collective-permute-done.3
  67.7 0.4 collective-permute-start.4
  68.1 0.4 collective-permute-done.5
  68.7 2.0 %collective-permute-start.6 = (bf16[4,176,512]{2,1,0:T(8,128)(2,1)S(1)}, bf16[4,176,512]{2,1,0:T(8,128)(2,1)S(1)}, u32[]{:S(2)}, u32[]{:S(2)}) collective-permute-start(bf16[4,176,512]{2,1,0:T(8,128)(2,1)S(1)} %add_convert_fusion.1), channel_id=1, source_target_pairs={{0,6},{1,25},{2,0},{3,27},{4,2},{5,29},{6,4},{7,31},{8,14},{9,1},{... | collective-permute-start | bytes 2162696 | tf_op jit(solution)/shard_map/ppermute | solution.py:478
  70.7 8.0 %collective-permute-done.2 = bf16[4,176,512]{2,1,0:T(8,128)(2,1)S(1)} collective-permute-done((bf16[4,176,512]{2,1,0:T(8,128)(2,1)S(1)}, bf16[4,176,512]{2,1,0:T(8,128)(2,1)S(1)}, u32[]{:S(2)}, u32[]{:S(2)}) %collective-permute-start.2) | collective-permute-done | bytes 720928 | tf_op jit(solution)/shard_map/ppermute | solution.py:478
  78.7 7.7 %collective-permute-done.4 = bf16[4,176,512]{2,1,0:T(8,128)(2,1)S(1)} collective-permute-done((bf16[4,176,512]{2,1,0:T(8,128)(2,1)S(1)}, bf16[4,176,512]{2,1,0:T(8,128)(2,1)S(1)}, u32[]{:S(2)}, u32[]{:S(2)}) %collective-permute-start.4) | collective-permute-done | bytes 720928 | tf_op jit(solution)/shard_map/ppermute | solution.py:478
  86.4 0.5 add_convert_fusion
  87.0 0.6 collective-permute-start.7
  87.6 1.4 collective-permute-start.9
  89.1 5.8 %all-to-all-start.3 = ((bf16[8,128,128]{2,1,0:T(8,128)(2,1)}), bf16[8,128,128]{2,1,0:T(8,128)(2,1)S(1)}, u32[]{:S(2)}, u32[]{:S(2)}) async-start(bf16[8,128,128]{2,1,0:T(8,128)(2,1)} %get-tuple-element.44), calls=%async_computation.3 | async-start | bytes 524288 | tf_op jit(solution)/shard_map/all_to_all | solution.py:614
  95.0 2.7 %collective-permute-start.12 = (bf16[176,512]{1,0:T(8,128)(2,1)S(1)}, bf16[176,512]{1,0:T(8,128)(2,1)S(1)}, u32[]{:S(2)}, u32[]{:S(2)}) collective-permute-start(bf16[176,512]{1,0:T(8,128)(2,1)S(1)} %fusion.1), channel_id=1, source_target_pairs={{0,96},{1,7},{2,98},{3,1},{4,100},{5,3},{6,102},{7,5},{8,104},{9,1... | collective-permute-start | bytes 540680 | tf_op jit(solution)/shard_map/ppermute | solution.py:478
  97.7 1.7 %collective-permute-start.10 = (bf16[176,512]{1,0:T(8,128)(2,1)S(1)}, bf16[176,512]{1,0:T(8,128)(2,1)S(1)}, u32[]{:S(2)}, u32[]{:S(2)}) collective-permute-start(bf16[176,512]{1,0:T(8,128)(2,1)S(1)} %fusion.1), channel_id=1, source_target_pairs={{0,64},{1,5},{2,66},{3,7},{4,68},{5,1},{6,70},{7,3},{8,72},{9,13},... | collective-permute-start | bytes 540680 | tf_op jit(solution)/shard_map/ppermute | solution.py:478
  99.4 2.1 %all-to-all-done.3.grad_ref = bf16[8,128,128]{2,1,0:T(8,128)(2,1)S(1)} async-done(((bf16[8,128,128]{2,1,0:T(8,128)(2,1)}), bf16[8,128,128]{2,1,0:T(8,128)(2,1)S(1)}, u32[]{:S(2)}, u32[]{:S(2)}) %all-to-all-start.3) | async-done | bytes 262176 | tf_op jit(solution)/shard_map/all_to_all | solution.py:614
  101.5 3.6 %return_rows.1 = bf16[16,128,128]{2,1,0:T(8,128)(2,1)} custom-call(s32[2048]{0:T(1024)S(1)} %bitcast.26, bf16[8,128,128]{2,1,0:T(8,128)(2,1)S(1)} %all-to-all-done.3.grad_ref), custom_call_target="tpu_custom_call" | custom-call | flops 4400000000 | bytes 14400000 | tf_op jit(solution)/shard_map/return_rows/pallas_call | solution.py:204
  105.2 4.6 %all-to-all-start.4 = ((bf16[16,128,128]{2,1,0:T(8,128)(2,1)}), bf16[16,128,128]{2,1,0:T(8,128)(2,1)S(1)}, u32[]{:S(2)}, u32[]{:S(2)}) async-start(bf16[16,128,128]{2,1,0:T(8,128)(2,1)} %return_rows.1), calls=%async_computation.4 | async-start | bytes 1048576 | tf_op jit(solution)/shard_map/all_to_all | solution.py:620
  109.9 1.4 collective-permute-start.15
  111.3 2.4 %collective-permute-start.14 = (bf16[176,512]{1,0:T(8,128)(2,1)S(1)}, bf16[176,512]{1,0:T(8,128)(2,1)S(1)}, u32[]{:S(2)}, u32[]{:S(2)}) collective-permute-start(bf16[176,512]{1,0:T(8,128)(2,1)S(1)} %add_convert_fusion.5), channel_id=1, source_target_pairs={{0,16},{1,65},{2,18},{3,67},{4,20},{5,69},{6,22},{7,71},{8,24},{9,... | collective-permute-start | bytes 540680 | tf_op jit(solution)/shard_map/ppermute | solution.py:478
  113.7 1.2 collective-permute-start.13
  114.9 5.4 %collective-permute-done.15 = bf16[176,512]{1,0:T(8,128)(2,1)S(1)} collective-permute-done((bf16[176,512]{1,0:T(8,128)(2,1)S(1)}, bf16[176,512]{1,0:T(8,128)(2,1)S(1)}, u32[]{:S(2)}, u32[]{:S(2)}) %collective-permute-start.15) | collective-permute-done | bytes 180256 | tf_op jit(solution)/shard_map/ppermute | solution.py:478
  120.3 3.3 %collective-permute-done.14 = bf16[176,512]{1,0:T(8,128)(2,1)S(1)} collective-permute-done((bf16[176,512]{1,0:T(8,128)(2,1)S(1)}, bf16[176,512]{1,0:T(8,128)(2,1)S(1)}, u32[]{:S(2)}, u32[]{:S(2)}) %collective-permute-start.14) | collective-permute-done | bytes 180256 | tf_op jit(solution)/shard_map/ppermute | solution.py:478
  123.7 0.5 collective-permute-start.19
  124.2 0.7 collective-permute-start.18
  124.9 2.2 %collective-permute-start.17 = (bf16[4,176,512]{2,1,0:T(8,128)(2,1)S(1)}, bf16[4,176,512]{2,1,0:T(8,128)(2,1)S(1)}, u32[]{:S(2)}, u32[]{:S(2)}) collective-permute-start(bf16[4,176,512]{2,1,0:T(8,128)(2,1)S(1)} %pad_maximum_fusion.refs_0_), channel_id=1, source_target_pairs={{0,4},{1,17},{2,6},{3,19},{4,0},{5,21},{6,2},{7,23},{8,12},{9,25},... | collective-permute-start | bytes 2162696 | tf_op jit(solution)/shard_map/ppermute | solution.py:478
  127.1 1.2 collective-permute-start.16
  128.3 6.5 %scatter_rows.1 = f32[64,4096]{1,0:T(8,128)} custom-call(s32[4096]{0:T(1024)S(1)} %bitcast.23, bf16[16,128,128]{2,1,0:T(8,128)(2,1)S(1)} %all-to-all-done.4.incoming_ref), custom_call_target="tpu_custom_call" | custom-call | flops 12099999744 | bytes 39600000 | tf_op jit(solution)/shard_map/scatter_rows/pallas_call | solution.py:251
  134.9 2.7 %widen_sums.3 = (f32[2,512,2048]{2,1,0:T(8,128)}, f32[2,512,512]{2,1,0:T(8,128)}) custom-call(bf16[4,176,512]{2,1,0:T(8,128)(2,1)S(1)} %pad_maximum_fusion.refs_0_, bf16[4,176,512]{2,1,0:T(8,128)(2,1)} %collective-permute-done.19.refs_1_), custom_call_target="tpu_custom_call" | custom-call | flops 1870000000 | bytes 6120000 | tf_op jit(solution)/shard_map/widen_sums/pallas_call | solution.py:547
  137.6 6.0 %collective-permute-done.17.refs_1_ = bf16[4,176,512]{2,1,0:T(8,128)(2,1)S(1)} collective-permute-done((bf16[4,176,512]{2,1,0:T(8,128)(2,1)S(1)}, bf16[4,176,512]{2,1,0:T(8,128)(2,1)S(1)}, u32[]{:S(2)}, u32[]{:S(2)}) %collective-permute-start.17) | collective-permute-done | bytes 720928 | tf_op jit(solution)/shard_map/ppermute | solution.py:478
  143.6 0.6 collective-permute-done.16.refs_0_
  144.2 1.2 collective-permute-start.20
  145.4 0.5 collective-permute-start.22
  146.0 0.9 hot_sums.1
  146.9 2.1 %widen_sums.4 = (f32[2,512,2048]{2,1,0:T(8,128)}, f32[2,512,512]{2,1,0:T(8,128)}) custom-call(bf16[4,176,512]{2,1,0:T(8,128)(2,1)S(1)} %collective-permute-done.16.refs_0_, bf16[4,176,512]{2,1,0:T(8,128)(2,1)S(1)} %collective-permute-done.17.refs_1_, ...), custom_call_target="tpu_custom_call", output_to_operand_aliasing={{0}: (3, {}), {1}: (4, {})} | custom-call | flops 2529999872 | bytes 8279999 | tf_op jit(solution)/shard_map/widen_sums/pallas_call | solution.py:547
  149.0 0.3 collective-permute-done.22.refs_2_
  149.3 2.1 %widen_sums.5 = (f32[2,512,2048]{2,1,0:T(8,128)}, f32[2,512,512]{2,1,0:T(8,128)}) custom-call(bf16[4,176,512]{2,1,0:T(8,128)(2,1)S(1)} %collective-permute-done.20.refs_0_, bf16[4,176,512]{2,1,0:T(8,128)(2,1)S(1)} %collective-permute-done.21.refs_1_, ...), custom_call_target="tpu_custom_call", output_to_operand_aliasing={{0}: (3, {}), {1}: (4, {})} | custom-call | flops 2529999872 | bytes 8279999 | tf_op jit(solution)/shard_map/widen_sums/pallas_call | solution.py:547
  (44 shorter events, 1.1 us)
Async XLA Ops:
  0.6 10.7 %copy-start.6 = (bf16[4096,64]{0,1:T(8,128)(2,1)S(1)}, bf16[4096,64]{0,1:T(8,128)(2,1)}, u32[]{:S(2)}) copy-start(bf16[4096,64]{0,1:T(8,128)(2,1)} %param.10) | copy-start | bytes 1572868
  2.7 15.0 %all-to-all-start = ((s32[16,2,128]{2,1,0:T(2,128)}), s32[16,2,128]{2,1,0:T(2,128)S(1)}, u32[]{:S(2)}, u32[]{:S(2)}) async-start(s32[16,2,128]{2,1,0:T(2,128)} %get-tuple-element.32), calls=%async_computation | async-start | bytes 32768 | tf_op jit(solution)/shard_map/all_to_all | solution.py:605
  17.8 17.5 %copy-start.3 = (bf16[256,64]{0,1:T(8,128)(2,1)S(1)}, bf16[256,64]{0,1:T(8,128)(2,1)}, u32[]{:S(2)}) copy-start(bf16[256,64]{0,1:T(8,128)(2,1)} %param.11) | copy-start | bytes 98308
  17.8 17.5 %copy-start.5 = (s32[8,2,128]{2,1,0:T(2,128)S(1)}, s32[8,2,128]{2,1,0:T(2,128)}, u32[]{:S(2)}) copy-start(s32[8,2,128]{2,1,0:T(2,128)} %get-tuple-element.31.index_ref) | copy-start | bytes 24580
  35.2 16.6 %copy-start = (bf16[2,512,2048]{2,1,0:T(8,128)(2,1)S(1)}, bf16[2,512,2048]{2,1,0:T(8,128)(2,1)}, u32[]{:S(2)}) copy-start(bf16[2,512,2048]{2,1,0:T(8,128)(2,1)} %win_ref.1) | copy-start | bytes 12582916
  35.2 16.6 %copy-start.1 = (bf16[2,512,512]{2,1,0:T(8,128)(2,1)S(1)}, bf16[2,512,512]{2,1,0:T(8,128)(2,1)}, u32[]{:S(2)}) copy-start(bf16[2,512,512]{2,1,0:T(8,128)(2,1)} %wout_ref.1) | copy-start | bytes 3145732
  35.2 16.6 %copy-start.2 = (bf16[256,512]{1,0:T(8,128)(2,1)S(1)}, bf16[256,512]{1,0:T(8,128)(2,1)}, u32[]{:S(2)}) copy-start(bf16[256,512]{1,0:T(8,128)(2,1)} %cot_ref.1) | copy-start | bytes 786436
  35.3 16.6 %copy-start.4 = (s32[1,256]{1,0:T(1,128)S(1)}, s32[1,256]{1,0:T(1,128)}, u32[]{:S(2)}) copy-start(s32[1,256]{1,0:T(1,128)} %segment_ref.1) | copy-start | bytes 3076
  63.4 3.1 %collective-permute-start.1 = (bf16[4,176,512]{2,1,0:T(8,128)(2,1)S(1)}, bf16[4,176,512]{2,1,0:T(8,128)(2,1)S(1)}, u32[]{:S(2)}, u32[]{:S(2)}) collective-permute-start(bf16[4,176,512]{2,1,0:T(8,128)(2,1)S(1)} %get-tuple-element.37), channel_id=1, source_target_pairs={{0,1},{1,0},{2,3},{3,2},{4,5},{5,4},{6,7},{7,6},{8,9},{9,8},{10,11... | collective-permute-start | bytes 2162696 | tf_op jit(solution)/shard_map/ppermute | solution.py:468
  64.7 2.8 %collective-permute-start.3 = (bf16[4,176,512]{2,1,0:T(8,128)(2,1)S(1)}, bf16[4,176,512]{2,1,0:T(8,128)(2,1)S(1)}, u32[]{:S(2)}, u32[]{:S(2)}) collective-permute-start(bf16[4,176,512]{2,1,0:T(8,128)(2,1)S(1)} %get-tuple-element.39), channel_id=1, source_target_pairs={{0,1},{1,0},{2,3},{3,2},{4,5},{5,4},{6,7},{7,6},{8,9},{9,8},{10,11... | collective-permute-start | bytes 2162696 | tf_op jit(solution)/shard_map/ppermute | solution.py:468
  64.8 3.8 %collective-permute-start.5 = (bf16[4,176,512]{2,1,0:T(8,128)(2,1)S(1)}, bf16[4,176,512]{2,1,0:T(8,128)(2,1)S(1)}, u32[]{:S(2)}, u32[]{:S(2)}) collective-permute-start(bf16[4,176,512]{2,1,0:T(8,128)(2,1)S(1)} %get-tuple-element.41), channel_id=1, source_target_pairs={{0,1},{1,0},{2,3},{3,2},{4,5},{5,4},{6,7},{7,6},{8,9},{9,8},{10,11... | collective-permute-start | bytes 2162696 | tf_op jit(solution)/shard_map/ppermute | solution.py:468
  65.2 5.5 %collective-permute-start = (bf16[4,176,512]{2,1,0:T(8,128)(2,1)S(1)}, bf16[4,176,512]{2,1,0:T(8,128)(2,1)S(1)}, u32[]{:S(2)}, u32[]{:S(2)}) collective-permute-start(bf16[4,176,512]{2,1,0:T(8,128)(2,1)S(1)} %get-tuple-element.35), channel_id=1, source_target_pairs={{0,1},{1,0},{2,3},{3,2},{4,5},{5,4},{6,7},{7,6},{8,9},{9,8},{10,11... | collective-permute-start | bytes 2162696 | tf_op jit(solution)/shard_map/ppermute | solution.py:468
  66.7 12.1 %collective-permute-start.2 = (bf16[4,176,512]{2,1,0:T(8,128)(2,1)S(1)}, bf16[4,176,512]{2,1,0:T(8,128)(2,1)S(1)}, u32[]{:S(2)}, u32[]{:S(2)}) collective-permute-start(bf16[4,176,512]{2,1,0:T(8,128)(2,1)S(1)} %add_convert_fusion.3), channel_id=1, source_target_pairs={{0,4},{1,17},{2,6},{3,19},{4,0},{5,21},{6,2},{7,23},{8,12},{9,25},... | collective-permute-start | bytes 2162696 | tf_op jit(solution)/shard_map/ppermute | solution.py:478
  67.7 18.7 %collective-permute-start.4 = (bf16[4,176,512]{2,1,0:T(8,128)(2,1)S(1)}, bf16[4,176,512]{2,1,0:T(8,128)(2,1)S(1)}, u32[]{:S(2)}, u32[]{:S(2)}) collective-permute-start(bf16[4,176,512]{2,1,0:T(8,128)(2,1)S(1)} %add_convert_fusion.2), channel_id=1, source_target_pairs={{0,2},{1,9},{2,4},{3,11},{4,6},{5,13},{6,0},{7,15},{8,10},{9,17},{... | collective-permute-start | bytes 2162696 | tf_op jit(solution)/shard_map/ppermute | solution.py:478
  68.7 17.7 %collective-permute-start.6 = (bf16[4,176,512]{2,1,0:T(8,128)(2,1)S(1)}, bf16[4,176,512]{2,1,0:T(8,128)(2,1)S(1)}, u32[]{:S(2)}, u32[]{:S(2)}) collective-permute-start(bf16[4,176,512]{2,1,0:T(8,128)(2,1)S(1)} %add_convert_fusion.1), channel_id=1, source_target_pairs={{0,6},{1,25},{2,0},{3,27},{4,2},{5,29},{6,4},{7,31},{8,14},{9,1},{... | collective-permute-start | bytes 2162696 | tf_op jit(solution)/shard_map/ppermute | solution.py:478
  87.0 7.9 %collective-permute-start.7 = (bf16[176,512]{1,0:T(8,128)(2,1)S(1)}, bf16[176,512]{1,0:T(8,128)(2,1)S(1)}, u32[]{:S(2)}, u32[]{:S(2)}) collective-permute-start(bf16[176,512]{1,0:T(8,128)(2,1)S(1)} %get-tuple-element.57), channel_id=1, source_target_pairs={{0,16},{1,65},{2,18},{3,67},{4,20},{5,69},{6,22},{7,71},{8,24},{9,... | collective-permute-start | bytes 540680 | tf_op jit(solution)/shard_map/ppermute | solution.py:478
  87.6 7.3 %collective-permute-start.9 = (bf16[176,512]{1,0:T(8,128)(2,1)S(1)}, bf16[176,512]{1,0:T(8,128)(2,1)S(1)}, u32[]{:S(2)}, u32[]{:S(2)}) collective-permute-start(bf16[176,512]{1,0:T(8,128)(2,1)S(1)} %get-tuple-element.58), channel_id=1, source_target_pairs={{0,24},{1,97},{2,26},{3,99},{4,28},{5,101},{6,30},{7,103},{8,0},{9... | collective-permute-start | bytes 540680 | tf_op jit(solution)/shard_map/ppermute | solution.py:478
  89.0 5.8 %collective-permute-start.8 = (bf16[176,512]{1,0:T(8,128)(2,1)S(1)}, bf16[176,512]{1,0:T(8,128)(2,1)S(1)}, u32[]{:S(2)}, u32[]{:S(2)}) collective-permute-start(bf16[176,512]{1,0:T(8,128)(2,1)S(1)} %get-tuple-element.59), channel_id=1, source_target_pairs={{0,8},{1,33},{2,10},{3,35},{4,12},{5,37},{6,14},{7,39},{8,16},{9,4... | collective-permute-start | bytes 540680 | tf_op jit(solution)/shard_map/ppermute | solution.py:478
  89.1 12.4 %all-to-all-start.3 = ((bf16[8,128,128]{2,1,0:T(8,128)(2,1)}), bf16[8,128,128]{2,1,0:T(8,128)(2,1)S(1)}, u32[]{:S(2)}, u32[]{:S(2)}) async-start(bf16[8,128,128]{2,1,0:T(8,128)(2,1)} %get-tuple-element.44), calls=%async_computation.3 | async-start | bytes 524288 | tf_op jit(solution)/shard_map/all_to_all | solution.py:614
  95.0 14.8 %collective-permute-start.12 = (bf16[176,512]{1,0:T(8,128)(2,1)S(1)}, bf16[176,512]{1,0:T(8,128)(2,1)S(1)}, u32[]{:S(2)}, u32[]{:S(2)}) collective-permute-start(bf16[176,512]{1,0:T(8,128)(2,1)S(1)} %fusion.1), channel_id=1, source_target_pairs={{0,96},{1,7},{2,98},{3,1},{4,100},{5,3},{6,102},{7,5},{8,104},{9,1... | collective-permute-start | bytes 540680 | tf_op jit(solution)/shard_map/ppermute | solution.py:478
  97.7 12.1 %collective-permute-start.11 = (bf16[176,512]{1,0:T(8,128)(2,1)S(1)}, bf16[176,512]{1,0:T(8,128)(2,1)S(1)}, u32[]{:S(2)}, u32[]{:S(2)}) collective-permute-start(bf16[176,512]{1,0:T(8,128)(2,1)S(1)} %fusion.1), channel_id=1, source_target_pairs={{0,32},{1,3},{2,34},{3,5},{4,36},{5,7},{6,38},{7,1},{8,40},{9,11},... | collective-permute-start | bytes 540680 | tf_op jit(solution)/shard_map/ppermute | solution.py:478
  97.7 12.1 %collective-permute-start.10 = (bf16[176,512]{1,0:T(8,128)(2,1)S(1)}, bf16[176,512]{1,0:T(8,128)(2,1)S(1)}, u32[]{:S(2)}, u32[]{:S(2)}) collective-permute-start(bf16[176,512]{1,0:T(8,128)(2,1)S(1)} %fusion.1), channel_id=1, source_target_pairs={{0,64},{1,5},{2,66},{3,7},{4,68},{5,1},{6,70},{7,3},{8,72},{9,13},... | collective-permute-start | bytes 540680 | tf_op jit(solution)/shard_map/ppermute | solution.py:478
  105.2 23.2 %all-to-all-start.4 = ((bf16[16,128,128]{2,1,0:T(8,128)(2,1)}), bf16[16,128,128]{2,1,0:T(8,128)(2,1)S(1)}, u32[]{:S(2)}, u32[]{:S(2)}) async-start(bf16[16,128,128]{2,1,0:T(8,128)(2,1)} %return_rows.1), calls=%async_computation.4 | async-start | bytes 1048576 | tf_op jit(solution)/shard_map/all_to_all | solution.py:620
  109.9 10.4 %collective-permute-start.15 = (bf16[176,512]{1,0:T(8,128)(2,1)S(1)}, bf16[176,512]{1,0:T(8,128)(2,1)S(1)}, u32[]{:S(2)}, u32[]{:S(2)}) collective-permute-start(bf16[176,512]{1,0:T(8,128)(2,1)S(1)} %add_convert_fusion.5), channel_id=1, source_target_pairs={{0,8},{1,33},{2,10},{3,35},{4,12},{5,37},{6,14},{7,39},{8,16},{9,4... | collective-permute-start | bytes 540680 | tf_op jit(solution)/shard_map/ppermute | solution.py:478
  111.3 12.3 %collective-permute-start.14 = (bf16[176,512]{1,0:T(8,128)(2,1)S(1)}, bf16[176,512]{1,0:T(8,128)(2,1)S(1)}, u32[]{:S(2)}, u32[]{:S(2)}) collective-permute-start(bf16[176,512]{1,0:T(8,128)(2,1)S(1)} %add_convert_fusion.5), channel_id=1, source_target_pairs={{0,16},{1,65},{2,18},{3,67},{4,20},{5,69},{6,22},{7,71},{8,24},{9,... | collective-permute-start | bytes 540680 | tf_op jit(solution)/shard_map/ppermute | solution.py:478
  113.7 9.9 %collective-permute-start.13 = (bf16[176,512]{1,0:T(8,128)(2,1)S(1)}, bf16[176,512]{1,0:T(8,128)(2,1)S(1)}, u32[]{:S(2)}, u32[]{:S(2)}) collective-permute-start(bf16[176,512]{1,0:T(8,128)(2,1)S(1)} %add_convert_fusion.5), channel_id=1, source_target_pairs={{0,24},{1,97},{2,26},{3,99},{4,28},{5,101},{6,30},{7,103},{8,0},{9... | collective-permute-start | bytes 540680 | tf_op jit(solution)/shard_map/ppermute | solution.py:478
  123.7 11.1 %collective-permute-start.19 = (bf16[4,176,512]{2,1,0:T(8,128)(2,1)S(1)}, bf16[4,176,512]{2,1,0:T(8,128)(2,1)}, u32[]{:S(2)}, u32[]{:S(2)}) collective-permute-start(bf16[4,176,512]{2,1,0:T(8,128)(2,1)S(1)} %pad_maximum_fusion.refs_0_), channel_id=1, source_target_pairs={{0,1},{1,0},{2,3},{3,2},{4,5},{5,4},{6,7},{7,6},{8,9},{9,8},{10,11... | collective-permute-start | bytes 2162696 | tf_op jit(solution)/shard_map/ppermute | solution.py:468
  124.2 13.4 %collective-permute-start.18 = (bf16[4,176,512]{2,1,0:T(8,128)(2,1)S(1)}, bf16[4,176,512]{2,1,0:T(8,128)(2,1)S(1)}, u32[]{:S(2)}, u32[]{:S(2)}) collective-permute-start(bf16[4,176,512]{2,1,0:T(8,128)(2,1)S(1)} %pad_maximum_fusion.refs_0_), channel_id=1, source_target_pairs={{0,2},{1,9},{2,4},{3,11},{4,6},{5,13},{6,0},{7,15},{8,10},{9,17},{... | collective-permute-start | bytes 2162696 | tf_op jit(solution)/shard_map/ppermute | solution.py:478
  124.9 18.7 %collective-permute-start.17 = (bf16[4,176,512]{2,1,0:T(8,128)(2,1)S(1)}, bf16[4,176,512]{2,1,0:T(8,128)(2,1)S(1)}, u32[]{:S(2)}, u32[]{:S(2)}) collective-permute-start(bf16[4,176,512]{2,1,0:T(8,128)(2,1)S(1)} %pad_maximum_fusion.refs_0_), channel_id=1, source_target_pairs={{0,4},{1,17},{2,6},{3,19},{4,0},{5,21},{6,2},{7,23},{8,12},{9,25},... | collective-permute-start | bytes 2162696 | tf_op jit(solution)/shard_map/ppermute | solution.py:478
  127.1 17.1 %collective-permute-start.16 = (bf16[4,176,512]{2,1,0:T(8,128)(2,1)S(1)}, bf16[4,176,512]{2,1,0:T(8,128)(2,1)S(1)}, u32[]{:S(2)}, u32[]{:S(2)}) collective-permute-start(bf16[4,176,512]{2,1,0:T(8,128)(2,1)S(1)} %pad_maximum_fusion.refs_0_), channel_id=1, source_target_pairs={{0,6},{1,25},{2,0},{3,27},{4,2},{5,29},{6,4},{7,31},{8,14},{9,1},{... | collective-permute-start | bytes 2162696 | tf_op jit(solution)/shard_map/ppermute | solution.py:478
  144.2 4.8 %collective-permute-start.20 = (bf16[4,176,512]{2,1,0:T(8,128)(2,1)S(1)}, bf16[4,176,512]{2,1,0:T(8,128)(2,1)S(1)}, u32[]{:S(2)}, u32[]{:S(2)}) collective-permute-start(bf16[4,176,512]{2,1,0:T(8,128)(2,1)S(1)} %collective-permute-done.16.refs_0_), channel_id=1, source_target_pairs={{0,1},{1,0},{2,3},{3,2},{4,5},{5,4},{6,7},{7,6},{8,9},{9,8},{10,11... | collective-permute-start | bytes 2162696 | tf_op jit(solution)/shard_map/ppermute | solution.py:468
  145.4 3.6 %collective-permute-start.21 = (bf16[4,176,512]{2,1,0:T(8,128)(2,1)S(1)}, bf16[4,176,512]{2,1,0:T(8,128)(2,1)S(1)}, u32[]{:S(2)}, u32[]{:S(2)}) collective-permute-start(bf16[4,176,512]{2,1,0:T(8,128)(2,1)S(1)} %collective-permute-done.17.refs_1_), channel_id=1, source_target_pairs={{0,1},{1,0},{2,3},{3,2},{4,5},{5,4},{6,7},{7,6},{8,9},{9,8},{10,11... | collective-permute-start | bytes 2162696 | tf_op jit(solution)/shard_map/ppermute | solution.py:468
  145.4 3.9 %collective-permute-start.22 = (bf16[4,176,512]{2,1,0:T(8,128)(2,1)S(1)}, bf16[4,176,512]{2,1,0:T(8,128)(2,1)S(1)}, u32[]{:S(2)}, u32[]{:S(2)}) collective-permute-start(bf16[4,176,512]{2,1,0:T(8,128)(2,1)S(1)} %collective-permute-done.18.refs_2_), channel_id=1, source_target_pairs={{0,1},{1,0},{2,3},{3,2},{4,5},{5,4},{6,7},{7,6},{8,9},{9,8},{10,11... | collective-permute-start | bytes 2162696 | tf_op jit(solution)/shard_map/ppermute | solution.py:468
